TPU v7x, 32 devices: a whole 2x2x4 slice. The times are simulated.
32 devices in a mesh: groups: 2 (over y), leaf: 4 (over x, core), inner: 4 (over z).
Axes of the slice: x: 2, y: 2, z: 4, core: 2. Of those that a mesh axis runs over, the one named last changes fastest.
Arguments:
- embed: bfloat16 [12288, 256], P(('groups', 'leaf', 'inner')), parts along dimension 0, may hold values from -1.5 to 1.5
- factors: bfloat16 [3, 12288, 128], P(None, ('groups', 'leaf', 'inner')), parts along dimension 1
- targets: float32 [12288, 32], P(('groups', 'leaf', 'inner')), parts along dimension 0
Outputs:
- solution: float32 [12288, 32], P(('groups', 'leaf', 'inner')), parts along dimension 0
- residual: float32 [12288, 32], P(('groups', 'leaf', 'inner')), parts along dimension 0
There are 2 independent parts, one for each index of `groups`. A program takes and returns all parts, laid end to end along the dimension named above; each array names one. Nothing has to cross between parts.
All inputs are finite; a program needn't handle non-finite values.
Results may differ from a plain program's by a relative error of at most 0.0029.
Values may be sent and summed in bfloat16 or wider, within the bound.
No kernel may reach another device: no remote copies, remote signals or barrier semaphores. Data moves between devices by JAX's collectives and lax.ppermute only.
A program may use at most 64 MiB of HBM per device.

v0:
```python
import jax
import jax.numpy as jnp
from jax import lax
from jax.sharding import PartitionSpec as P

ITERS = 2


def swapped(value, axis, apart):
    mask = 2**apart
    pairs = [(source, source ^ mask) for source in range(lax.axis_size(axis))]
    return lax.ppermute(value, axis, pairs)


def matern(left, right):
    left_f = left.astype(jnp.float32)
    right_f = right.astype(jnp.float32)
    left_sq = jnp.sum(left_f * left_f, axis=1)
    right_sq = jnp.sum(right_f * right_f, axis=1)
    inner_prod = lax.dot_general(
        left, right, (((1,), (1,)), ((), ())), preferred_element_type=jnp.float32
    )
    dist2 = left_sq[:, None] + right_sq[None, :] - 2.0 * inner_prod
    scaled = jnp.sqrt(3.0) * jnp.sqrt(jnp.maximum(dist2, 0.0)) / 2.3
    return (1.0 + scaled) * jnp.exp(-scaled)


def squares(residual):
    return lax.psum(jnp.sum(residual * residual, axis=0), ("leaf", "inner"))


def column_gather(embed, column_fn):
    return column_fn(lax.all_gather(embed, "inner", axis=0, tiled=True), jnp.int32(0))


def operate(embed, factors, field):

    def column_terms(piece, start):
        return jnp.dot(matern(piece, embed), field, precision=lax.Precision.HIGHEST)

    terms = column_gather(embed, column_terms)
    dense = lax.psum_scatter(terms, "inner", scatter_dimension=0, tiled=True)
    total = dense + 0.5 * field
    levels = factors.shape[0]
    rounded = field.astype(jnp.bfloat16)
    proj = jnp.einsum("lrk,rc->lkc", factors, rounded, preferred_element_type=jnp.float32)
    proj = lax.psum(proj, "inner")
    for bit in range(levels - 1):
        upper = proj[bit + 1 :]
        partner = swapped(upper, "leaf", bit)
        proj = jnp.concatenate([proj[: bit + 1], upper + partner], axis=0)
    back = jnp.einsum(
        "lrk,lkc->rc", factors, proj.astype(jnp.bfloat16), preferred_element_type=jnp.float32
    )
    return total + back


def on_device(embed, factors, targets):
    solution = jnp.zeros_like(targets)
    residual = targets
    direction = targets
    norm_now = squares(residual)
    for step in range(ITERS):
        image = operate(embed, factors, direction)
        curv = lax.psum(jnp.sum(direction * image, axis=0), ("leaf", "inner"))
        alpha = norm_now / curv
        solution = solution + alpha * direction
        residual = residual - alpha * image
        if step + 1 < ITERS:
            norm_next = squares(residual)
            direction = residual + norm_next / norm_now * direction
            norm_now = norm_next
    return (solution, residual)


def solution(mesh):
    return jax.shard_map(
        on_device,
        mesh=mesh,
        in_specs=(
            P(("groups", "leaf", "inner"), None),
            P(None, ("groups", "leaf", "inner"), None),
            P(("groups", "leaf", "inner"), None),
        ),
        out_specs=(P(("groups", "leaf", "inner"), None), P(("groups", "leaf", "inner"), None)),
        check_vma=False,
    )
```

profile of v0, /device:TPU:0, one launch (start us, length us, event | category | flops | bytes accessed | tf_op | source)
XLA Modules:
  0.0 213.3 jit_solution(7747998831037063356)
XLA Ops:
  7.2 0.0 copy-start
  7.2 0.0 reduce-scatter.3.cloned.1.call-start
  7.2 0.9 copy-done
  8.1 1.0 fusion.23
  9.1 21.2 %psum.43 = f32[3,128,32]{1,2,0:T(8,128)S(1)} all-reduce(f32[3,128,32]{1,2,0:T(8,128)S(1)} %fusion.23), channel_id=1, replica_groups=mesh['groups'=2,'leaf'=4,'inner'=4] {'inner'}, use_global_device_ids=true, to_apply=%region_5.0 | all-reduce | flops 12288 | bytes 98304 | tf_op jit(solution)/shard_map/psum | solution.py:47
  30.3 0.1 collective-permute-start
  30.4 1.1 multiply_reduce_fusion.1
  31.5 18.1 %all_gather.4 = bf16[1536,256]{1,0:T(8,128)(2,1)S(1)} all-gather(bf16[384,256]{1,0:T(8,128)(2,1)} %param.3), channel_id=1, replica_groups=mesh['groups'=2,'leaf'=4,'inner'=4] {'inner'}, dimensions={0}, use_global_device_ids=true | all-gather | bytes 983040 | tf_op jit(solution)/shard_map/all_gather | solution.py:33
  49.6 0.3 multiply_reduce_fusion
  49.9 1.5 exponential_multiply_fusion
  51.4 3.0 %fusion.35 = f32[1536,32]{0,1:T(8,128)} fusion(f32[1536,384]{1,0:T(8,128)S(1)} %exponential_multiply_fusion, f32[384,32]{0,1:T(8,128)S(1)} %copy-done.1), kind=kOutput, calls=%fused_computation.55 | convolution fusion | flops 226492416 | bytes 2605056 | tf_op jit(solution)/shard_map/dot_general | solution.py:39
  54.4 0.0 reduce-scatter.3.cloned.1.call-update
  54.4 0.0 reduce-scatter.5.cloned.1.call-start
  54.5 1.6 collective-permute-start.1
  56.1 2.2 %collective-permute-done.1 = f32[1,128,32]{1,2,0:T(8,128)S(1)} collective-permute-done((f32[1,128,32]{1,2,0:T(8,128)S(1)}, f32[1,128,32]{1,2,0:T(8,128)S(1)}, u32[]{:S(2)}, u32[]{:S(2)}) %collective-permute-start.1) | collective-permute-done | bytes 16416 | tf_op jit(solution)/shard_map/ppermute | solution.py:12
  58.3 15.1 %reduce-scatter.3.cloned.1.call-done = f32[384,32]{0,1:T(8,128)} async-done(((f32[1536,32]{0,1:T(8,128)}), f32[384,32]{0,1:T(8,128)}) %reduce-scatter.3.cloned.1.call-update) | async-done | bytes 49168 | tf_op jit(solution)/shard_map/reduce_scatter | solution.py:42
  73.4 1.1 multiply_reduce_fusion.4
  74.5 29.7 %all-reduce = (f32[32]{0:T(128)S(1)}, f32[32]{0:T(128)S(1)}) all-reduce(f32[32]{0:T(128)S(1)} %get-tuple-element.3, f32[32]{0:T(128)S(1)} %get-tuple-element.2), channel_id=1, replica_groups=mesh['groups'=2,'leaf'=4,'inner'=4] {'leaf','inner'}, use_global_device_ids=true, to_apply=%region_1.0 | all-reduce | flops 64 | bytes 512 | tf_op jit(solution)/shard_map/psum | solution.py:29
  104.2 0.2 multiply_reduce_fusion.3
  104.4 31.9 %psum.45 = f32[32]{0:T(128)S(1)} all-reduce(f32[32]{0:T(128)S(1)} %multiply_reduce_fusion.3), channel_id=1, replica_groups=mesh['groups'=2,'leaf'=4,'inner'=4] {'leaf','inner'}, use_global_device_ids=true, to_apply=%region_9.0 | all-reduce | flops 32 | bytes 256 | tf_op jit(solution)/shard_map/psum | solution.py:29
  136.3 0.1 multiply_add_fusion.1
  136.4 0.2 convolution_bitcast_fusion.1
  136.6 16.1 %psum.46 = f32[3,128,32]{1,2,0:T(8,128)S(1)} all-reduce(f32[3,128,32]{1,2,0:T(8,128)S(1)} %convolution_bitcast_fusion.1), channel_id=1, replica_groups=mesh['groups'=2,'leaf'=4,'inner'=4] {'inner'}, use_global_device_ids=true, to_apply=%region_11.0 | all-reduce | flops 12288 | bytes 98304 | tf_op jit(solution)/shard_map/psum | solution.py:47
  152.7 0.1 collective-permute-start.2
  152.8 3.0 %fusion.36 = f32[1536,32]{0,1:T(8,128)} fusion(f32[1536,384]{1,0:T(8,128)S(1)} %exponential_multiply_fusion, f32[384,32]{0,1:T(8,128)S(1)} %multiply_add_fusion.1), kind=kOutput, calls=%fused_computation.56 | convolution fusion | flops 226492416 | bytes 2605056 | tf_op jit(solution)/shard_map/dot_general | solution.py:39
  155.8 0.0 reduce-scatter.5.cloned.1.call-update
  155.9 1.6 collective-permute-start.3
  157.5 2.2 %collective-permute-done.3 = f32[1,128,32]{1,2,0:T(8,128)S(1)} collective-permute-done((f32[1,128,32]{1,2,0:T(8,128)S(1)}, f32[1,128,32]{1,2,0:T(8,128)S(1)}, u32[]{:S(2)}, u32[]{:S(2)}) %collective-permute-start.3) | collective-permute-done | bytes 16416 | tf_op jit(solution)/shard_map/ppermute | solution.py:12
  159.7 15.3 %reduce-scatter.5.cloned.1.call-done = f32[384,32]{0,1:T(8,128)} async-done(((f32[1536,32]{0,1:T(8,128)}), f32[384,32]{0,1:T(8,128)}) %reduce-scatter.5.cloned.1.call-update) | async-done | bytes 49168 | tf_op jit(solution)/shard_map/reduce_scatter | solution.py:42
  175.0 1.1 multiply_reduce_fusion.2
  176.1 29.7 %psum.47 = f32[32]{0:T(128)S(1)} all-reduce(f32[32]{0:T(128)S(1)} %get-tuple-element.13), channel_id=1, replica_groups=mesh['groups'=2,'leaf'=4,'inner'=4] {'leaf','inner'}, use_global_device_ids=true, to_apply=%region_13.0 | all-reduce | flops 32 | bytes 256 | tf_op jit(solution)/shard_map/psum | solution.py:65
  205.8 0.7 multiply_subtract_fusion
  (19 shorter events, 0.1 us)
Async XLA Ops:
  7.2 1.0 copy-start
  7.2 42.7 %copy-start.2 = (bf16[384,256]{1,0:T(8,128)(2,1)S(1)}, bf16[384,256]{1,0:T(8,128)(2,1)}, u32[]{:S(2)}) copy-start(bf16[384,256]{1,0:T(8,128)(2,1)} %param.3) | copy-start | bytes 589828
  7.2 66.2 %reduce-scatter.3.cloned.1.call-start = ((), (), s32[]{:S(2)}) async-start(), calls=%async_computation.2 | async-start | bytes 245760 | tf_op jit(solution)/shard_map/reduce_scatter | solution.py:42
  30.3 24.1 %collective-permute-start = (f32[2,128,32]{1,2,0:T(8,128)S(1)}, f32[2,128,32]{1,2,0:T(8,128)S(1)}, u32[]{:S(2)}, u32[]{:S(2)}) collective-permute-start(f32[2,128,32]{1,2,0:T(8,128)S(1)} %slice.37), channel_id=1, source_target_pairs={{0,4},{4,0},{8,12},{12,8},{1,5},{5,1},{9,13},{13,9},{2,6},{6,2},{1... | collective-permute-start | bytes 98312 | tf_op jit(solution)/shard_map/ppermute | solution.py:12
  49.9 1.5 copy-start.1
  54.4 120.5 %reduce-scatter.5.cloned.1.call-start = ((), (), s32[]{:S(2)}) async-start(), calls=%async_computation.3 | async-start | bytes 245760 | tf_op jit(solution)/shard_map/reduce_scatter | solution.py:42
  54.5 3.8 %collective-permute-start.1 = (f32[1,128,32]{1,2,0:T(8,128)S(1)}, f32[1,128,32]{1,2,0:T(8,128)S(1)}, u32[]{:S(2)}, u32[]{:S(2)}) collective-permute-start(f32[1,128,32]{1,2,0:T(8,128)S(1)} %slice.38), channel_id=1, source_target_pairs={{0,8},{4,12},{8,0},{12,4},{1,9},{5,13},{9,1},{13,5},{2,10},{6,14},... | collective-permute-start | bytes 49160 | tf_op jit(solution)/shard_map/ppermute | solution.py:12
  152.7 3.1 %collective-permute-start.2 = (f32[2,128,32]{1,2,0:T(8,128)S(1)}, f32[2,128,32]{1,2,0:T(8,128)S(1)}, u32[]{:S(2)}, u32[]{:S(2)}) collective-permute-start(f32[2,128,32]{1,2,0:T(8,128)S(1)} %slice.40), channel_id=1, source_target_pairs={{0,4},{4,0},{8,12},{12,8},{1,5},{5,1},{9,13},{13,9},{2,6},{6,2},{1... | collective-permute-start | bytes 98312 | tf_op jit(solution)/shard_map/ppermute | solution.py:12
  155.9 3.8 %collective-permute-start.3 = (f32[1,128,32]{1,2,0:T(8,128)S(1)}, f32[1,128,32]{1,2,0:T(8,128)S(1)}, u32[]{:S(2)}, u32[]{:S(2)}) collective-permute-start(f32[1,128,32]{1,2,0:T(8,128)S(1)} %slice.41), channel_id=1, source_target_pairs={{0,8},{4,12},{8,0},{12,4},{1,9},{5,13},{9,1},{13,5},{2,10},{6,14},... | collective-permute-start | bytes 49160 | tf_op jit(solution)/shard_map/ppermute | solution.py:12
Sparse Core Ops, SparseCore 0:
  54.5 18.7 reduce-scatter.2
  155.9 18.9 reduce-scatter.4
where the time goes:
time: 214 us; the launch traced here: 213 us
  blocking collectives  147 us (69%)
  waiting for transfers between devices  34.8 us (16%)
  between operations  14.2 us (7%)
  matrix products  10.8 us (5%)
  starting transfers between devices  3.38 us (2%)
  other arithmetic  2.39 us (1%)
    psum x2, blocking collectives, squares(): return lax.psum(jnp.sum(residual * residual, axis=0), ('leaf', 'inner'))  61.6 us
    psum x2, blocking collectives, operate(): proj = lax.psum(proj, 'inner')  37.3 us
    reduce_scatter x2, waiting for transfers between devices, operate(): dense = lax.psum_scatter(terms, 'inner', scatter_dimension=0, tiled=True)  30.4 us
    psum x1, blocking collectives, on_device(): curv = lax.psum(jnp.sum(direction * image, axis=0), ('leaf', 'inner'))  29.7 us
    all_gather x1, blocking collectives, column_gather(): lax.all_gather(embed, 'inner', axis=0, tiled=True)  18.1 us
    dot_general x2, matrix products, column_terms(): return jnp.dot(matern(piece, embed), field, precision=lax.Precision.HIGHEST)  5.99 us
    ppermute x4, waiting for transfers between devices, swapped(): return lax.ppermute(value, axis, pairs)  4.45 us
  transfers between devices with their start and end apart: 6, of which 4 were waited for; matrix products, arithmetic and copies ran while one was open for 4% of the time, Pallas kernels for 0%

commit v1 on v0

v1 whole, which is shorter than its diff:
```python
import functools

import jax
import jax.numpy as jnp
from jax import lax
from jax.experimental import pallas as pl
from jax.experimental.pallas import tpu as pltpu
from jax.sharding import PartitionSpec as P

ITERS = 2
LENGTH_SCALE = 2.3
FAST_LEAF = 2048
F32, BF16 = jnp.float32, jnp.bfloat16
VMEM = pl.BlockSpec(memory_space=pltpu.VMEM)
SMEM = pl.BlockSpec(memory_space=pltpu.SMEM)


def swapped(value, axis, apart):
    mask = 2**apart
    pairs = [(source, source ^ mask) for source in range(lax.axis_size(axis))]
    return lax.ppermute(value, axis, pairs)


def matern(left, right):
    left_f = left.astype(F32)
    right_f = right.astype(F32)
    left_sq = jnp.sum(left_f * left_f, axis=1)
    right_sq = jnp.sum(right_f * right_f, axis=1)
    inner_prod = lax.dot_general(
        left, right, (((1,), (1,)), ((), ())), preferred_element_type=F32
    )
    dist2 = left_sq[:, None] + right_sq[None, :] - 2.0 * inner_prod
    scaled = jnp.sqrt(3.0) * jnp.sqrt(jnp.maximum(dist2, 0.0)) / LENGTH_SCALE
    return (1.0 + scaled) * jnp.exp(-scaled)


def squares(residual):
    return lax.psum(jnp.sum(residual * residual, axis=0), ("leaf", "inner"))


def operate(embed, factors, field):
    piece = lax.all_gather(embed, "inner", axis=0, tiled=True)
    terms = jnp.dot(matern(piece, embed), field, precision=lax.Precision.HIGHEST)
    dense = lax.psum_scatter(terms, "inner", scatter_dimension=0, tiled=True)
    total = dense + 0.5 * field
    levels = factors.shape[0]
    rounded = field.astype(BF16)
    proj = jnp.einsum("lrk,rc->lkc", factors, rounded, preferred_element_type=F32)
    proj = lax.psum(proj, "inner")
    for bit in range(levels - 1):
        upper = proj[bit + 1 :]
        partner = swapped(upper, "leaf", bit)
        proj = jnp.concatenate([proj[: bit + 1], upper + partner], axis=0)
    back = jnp.einsum(
        "lrk,lkc->rc", factors, proj.astype(BF16), preferred_element_type=F32
    )
    return total + back


def stepwise(embed, factors, targets):
    result = jnp.zeros_like(targets)
    residual = targets
    direction = targets
    norm_now = squares(residual)
    for step in range(ITERS):
        image = operate(embed, factors, direction)
        curv = lax.psum(jnp.sum(direction * image, axis=0), ("leaf", "inner"))
        alpha = norm_now / curv
        result = result + alpha * direction
        residual = residual - alpha * image
        if step + 1 < ITERS:
            norm_next = squares(residual)
            direction = residual + norm_next / norm_now * direction
            norm_now = norm_next
    return (result, residual)


def mm(left, right):
    return lax.dot_general(left, right, (((1,), (0,)), ((), ())), preferred_element_type=F32)


def mm_nt(left, right):
    return lax.dot_general(left, right, (((1,), (1,)), ((), ())), preferred_element_type=F32)


def pairs_of(slots):
    return [(i, j) for j in range(slots) for i in range(j + 1)]


def wide(pieces, nrhs):
    count = pieces.shape[0] // nrhs
    return jnp.concatenate([pieces[k * nrhs : (k + 1) * nrhs] for k in range(count)], axis=1)


def project_kernel(factors_ref, field_ref, proj_ref):
    levels = factors_ref.shape[0]
    nrhs = field_ref.shape[0]
    rounded = field_ref[...].astype(BF16)
    for level in range(levels):
        proj_ref[level * nrhs : (level + 1) * nrhs] = mm(rounded, factors_ref[level])


def pack_kernel(starts, field_ref, proj_ref, *refs):
    out_ref = refs[-1]
    nrhs = field_ref.shape[0]
    width = proj_ref.shape[1]
    count = field_ref.shape[1] // width
    for k in range(count):
        out_ref[k * nrhs : (k + 1) * nrhs] = field_ref[:, k * width : (k + 1) * width]
    base = count * nrhs
    levels = proj_ref.shape[0] // nrhs
    for level in range(levels):
        total = proj_ref[level * nrhs : (level + 1) * nrhs]
        for start, ref in zip(starts, refs[:-1]):
            if level >= start:
                total = total + ref[(level - start) * nrhs : (level - start + 1) * nrhs]
        out_ref[base + level * nrhs : base + (level + 1) * nrhs] = total


def kern_kernel(slots, *refs):
    embeds = refs[:slots]
    high_ref, low_ref, column_ref, row_ref = refs[slots:]
    rows, dims = embeds[0].shape
    scale = 3.0 / LENGTH_SCALE**2
    ones = jnp.ones((8, dims), BF16)
    for s in range(slots):
        wide_e = embeds[s][...].astype(F32)
        square = wide_e * wide_e
        column_ref[s] = jnp.broadcast_to(
            scale * jnp.sum(square, axis=1, keepdims=True), (rows, 128)
        )
        first = square.astype(BF16)
        rest = (square - first.astype(F32)).astype(BF16)
        row_ref[s] = scale * (mm_nt(ones, first) + mm_nt(ones, rest))
    chunk = 128
    for index, (i, j) in enumerate(pairs_of(slots)):
        right = embeds[j][...]
        row = row_ref[j, 0:1]

        def part(c, carry, i=i, index=index, right=right, row=row):
            span = pl.ds(pl.multiple_of(c * chunk, chunk), chunk)
            product = mm_nt(embeds[i][span], right)
            column = column_ref[i, span, 0:1]
            dist = jnp.maximum((column + row) - (2.0 * scale) * product, 1e-30)
            scaled = dist * lax.rsqrt(dist)
            value = (1.0 + scaled) * jnp.exp(-scaled)
            high = value.astype(BF16)
            high_ref[index, span] = high
            low_ref[index, span] = (value - high.astype(F32)).astype(BF16)
            return carry

        lax.fori_loop(0, rows // chunk, part, 0)


def main_kernel(slots, is_host_ref, high_ref, low_ref, *refs):
    factors = refs[:slots]
    packs = refs[slots : 2 * slots]
    sums_ref = refs[2 * slots]
    fields_out = refs[2 * slots + 1 :]
    levels, rows, rank = factors[0].shape
    nrhs = packs[0].shape[0] // (rows // rank + levels)
    lead = rows // rank * nrhs
    pairs = pairs_of(slots)
    field = [wide(packs[s][:lead], nrhs) for s in range(slots)]
    proj = packs[0][lead:]
    for s in range(1, slots):
        proj = proj + packs[s][lead:]
    proj = proj.astype(BF16)
    first = [f.astype(BF16) for f in field]
    both = [
        jnp.concatenate([h, (f - h.astype(F32)).astype(BF16)], axis=0)
        for f, h in zip(field, first)
    ]
    image = []
    for s in range(slots):
        total = 0.5 * field[s]
        for level in range(levels):
            total = total + mm_nt(proj[level * nrhs : (level + 1) * nrhs], factors[s][level])
        image.append(total)

    def add(total, stacked, second):
        return total + (stacked[:nrhs] + stacked[nrhs:] + second)

    for index, (i, j) in enumerate(pairs):
        high, low = high_ref[index], low_ref[index]
        image[j] = add(image[j], mm(both[i], high), mm(first[i], low))
        if i != j:
            image[i] = add(image[i], mm_nt(both[j], high), mm_nt(first[j], low))
    mine = is_host_ref[0] == 1

    def own(value, s):
        return jnp.where(mine, value, jnp.zeros_like(value)) if s == 0 else value

    image_b = []
    for s in range(slots):
        high = image[s].astype(BF16)
        image_b.append(high)
        fields_out[s][:nrhs] = own(image[s], s)
    norms = []
    for level in range(levels):
        total = mm(image_b[0], factors[0][level])
        for s in range(1, slots):
            total = total + mm(image_b[s], factors[s][level])
        if level == 0:
            norms.append(jnp.sum(total * total, axis=1, keepdims=True))
        sums_ref[:, level * rank : (level + 1) * rank] = own(total.astype(BF16), 0)
    second = [jnp.zeros((nrhs, rows), F32) for _ in range(slots)]
    for index, (i, j) in enumerate(pairs):
        high = high_ref[index]
        second[j] = second[j] + mm(image_b[i], high)
        if i != j:
            second[i] = second[i] + mm_nt(image_b[j], high)
    for s in range(slots):
        fields_out[s][nrhs:] = own(second[s], s)

    def dots(left, right):
        total = left[0] * right[0]
        for s in range(1, slots):
            total = total + left[s] * right[s]
        return jnp.sum(total, axis=1, keepdims=True)

    scalars = [
        dots(field, field),
        dots(field, image),
        dots(image, image),
        dots(image, second) + norms[0],
    ]
    lane = lax.broadcasted_iota(jnp.int32, (nrhs, 128), 1)
    packed = jnp.zeros((nrhs, 128), F32)
    for k, value in enumerate(scalars):
        value = jnp.broadcast_to(value, (nrhs, 128))
        for piece in range(3):
            rounded = value.astype(BF16).astype(F32)
            packed = jnp.where(lane == 3 * k + piece, rounded, packed)
            value = value - rounded
    sums_ref[:, levels * rank :] = own(packed.astype(BF16), 0)


def finish_kernel(leaves, slots, field_ref, factors_ref, *refs):
    sums = refs[:leaves]
    parts = refs[leaves : leaves + slots]
    solution_ref, residual_ref = refs[leaves + slots :]
    levels, rows, rank = factors_ref.shape
    nrhs = field_ref.shape[0]
    field = field_ref[...]
    total = parts[0][...]
    for s in range(1, slots):
        total = total + parts[s][...]
    image = total[:nrhs]
    second = total[nrhs:] + 0.5 * image
    lane = lax.broadcasted_iota(jnp.int32, (nrhs, 128), 1)
    packed = sums[0][:, levels * rank :].astype(F32)
    for m in range(1, leaves):
        packed = packed + sums[m][:, levels * rank :].astype(F32)

    def scalar(k):
        inside = (lane >= 3 * k) & (lane < 3 * k + 3)
        return jnp.sum(jnp.where(inside, packed, 0.0), axis=1, keepdims=True)

    bb, bw, ww, wu = (scalar(k) for k in range(4))
    wu = wu + 0.5 * ww
    for level in range(levels):
        nodes = {}
        for m in range(leaves):
            value = sums[m][:, level * rank : (level + 1) * rank].astype(F32)
            node = m >> level
            nodes[node] = nodes[node] + value if node in nodes else value
        second = second + mm_nt(nodes[0].astype(BF16), factors_ref[level])
        if level > 0:
            squared = sum(value * value for value in nodes.values())
            wu = wu + jnp.sum(squared, axis=1, keepdims=True)
    alpha0 = bb / bw
    norm1 = alpha0 * alpha0 * ww - bb
    ratio = norm1 / bb
    keep = 1.0 + ratio
    curv = keep * keep * bw - 2.0 * keep * alpha0 * ww + alpha0 * alpha0 * wu
    alpha1 = norm1 / curv
    solution_ref[...] = (alpha0 + alpha1 * keep) * field - (alpha1 * alpha0) * image
    residual_ref[...] = field - (alpha0 + alpha1 * keep) * image + (alpha1 * alpha0) * second


def call(kernel, outs, args, in_smem=0, scratch=(), flops=0, limit=24):
    moved = sum(a.size * a.dtype.itemsize for a in args)
    return pl.pallas_call(
        kernel,
        out_shape=[jax.ShapeDtypeStruct(shape, dtype) for shape, dtype in outs],
        in_specs=[SMEM] * in_smem + [VMEM] * (len(args) - in_smem),
        out_specs=[VMEM] * len(outs),
        scratch_shapes=list(scratch),
        cost_estimate=pl.CostEstimate(flops=flops, bytes_accessed=moved, transcendentals=0),
        compiler_params=pltpu.CompilerParams(vmem_limit_bytes=limit * 2**20),
    )(*args)


def collected(embed, factors, targets):
    leaves, inner = lax.axis_size("leaf"), lax.axis_size("inner")
    levels, rows, rank = factors.shape
    nrhs = targets.shape[1]

    def host(leaf):
        return inner // 2 if leaf % 2 == 0 else (inner - 1) // 2

    def others(leaf):
        sign = 1 if leaf % 2 == 0 else -1
        here = host(leaf)
        return sorted((z for z in range(inner) if z != here), key=lambda z: (abs(z - here), sign * z))

    routes = [
        [(leaf * inner + others(leaf)[k], leaf * inner + host(leaf)) for leaf in range(leaves)]
        for k in range(inner - 1)
    ]

    def to_host(value):
        return [value] + [lax.ppermute(value, ("leaf", "inner"), route) for route in routes]

    def from_host(values):
        back = [
            lax.ppermute(value, ("leaf", "inner"), [(b, a) for a, b in route])
            for value, route in zip(values[1:], routes)
        ]
        return [values[0]] + back

    def over_leaf(value, m):
        return lax.ppermute(value, "leaf", [(i, i ^ m) for i in range(leaves)])

    field = targets.T
    embeds = to_host(embed)
    factor_slots = to_host(factors)
    (proj,) = call(project_kernel, [((levels * nrhs, rank), F32)], [factors, field])
    starts, arrived = [], []
    for m in range(1, leaves):
        start = m.bit_length()
        if start < levels:
            starts.append(start)
            arrived.append(over_leaf(proj[start * nrhs :], m))
    height = rows // rank * nrhs + levels * nrhs
    (pack,) = call(
        functools.partial(pack_kernel, starts), [((height, rank), F32)], [field, proj] + arrived
    )
    packs = to_host(pack)
    pairs = len(pairs_of(inner))
    high, low = call(
        functools.partial(kern_kernel, inner),
        [((pairs, rows, rows), BF16)] * 2,
        embeds,
        scratch=[pltpu.VMEM((inner, rows, 128), F32), pltpu.VMEM((inner, 8, rows), F32)],
        flops=2 * pairs * rows * rows * embed.shape[1],
    )
    leaf = lax.axis_index("leaf")
    here = jnp.where(leaf % 2 == 0, host(0), host(1))
    is_host = (lax.axis_index("inner") == here).astype(jnp.int32).reshape(1)
    results = call(
        functools.partial(main_kernel, inner),
        [((nrhs, levels * rank + 128), BF16)] + [((2 * nrhs, rows), F32)] * inner,
        [is_host, high, low] + factor_slots + packs,
        in_smem=1,
    )
    sums = sum(from_host([results[0]] * inner))
    parts = from_host(results[1:])
    leaf_sums = [sums] + [over_leaf(sums, m) for m in range(1, leaves)]
    result, residual = call(
        functools.partial(finish_kernel, leaves, inner),
        [((nrhs, rows), F32)] * 2,
        [field, factors] + leaf_sums + parts,
    )
    return (result.T, residual.T)


def on_device(embed, factors, targets):
    if embed.shape[0] * lax.axis_size("inner") <= FAST_LEAF:
        return collected(embed, factors, targets)
    return stepwise(embed, factors, targets)


def solution(mesh):
    return jax.shard_map(
        on_device,
        mesh=mesh,
        in_specs=(
            P(("groups", "leaf", "inner"), None),
            P(None, ("groups", "leaf", "inner"), None),
            P(("groups", "leaf", "inner"), None),
        ),
        out_specs=(P(("groups", "leaf", "inner"), None), P(("groups", "leaf", "inner"), None)),
        check_vma=False,
    )
```

time: 214 us -> 56 us (0.26)
  blocking collectives: 147 us -> 0 us
  waiting for transfers between devices: 34.8 us -> 11.4 us
  starting transfers between devices: 3.38 us -> 26.2 us
  Pallas kernels: 0 us -> 14.3 us
  between operations: 14.2 us -> 0.94 us
  matrix products: 10.8 us -> 0 us
  other arithmetic: 2.39 us -> 0.01 us
    psum x5 -> x0, blocking collectives: 129 us -> none  [the longest x2 61.6 us: squares(): return lax.psum(jnp.sum(residual * residual, axis=0), ('leaf', 'inner'))]
    reduce_scatter x2 -> x0, waiting for transfers between devices: 30.4 us -> none  [operate(): dense = lax.psum_scatter(terms, 'inner', scatter_dimension=0, tiled=True)]
    ppermute x4 -> x21, starting transfers between devices: 3.3 us -> 26.2 us  [the longest x9 16.3 us: to_host(): lax.ppermute(value, ('leaf', 'inner'), route)]
    all_gather x1 -> x0, blocking collectives: 18.1 us -> none  [column_gather(): lax.all_gather(embed, 'inner', axis=0, tiled=True)]
    pallas_call x0 -> x5, Pallas kernels: none -> 14.3 us  [call(): pl.pallas_call(kernel, out_shape=[jax.ShapeDtypeStruct(shape, dtype) for...]
    dot_general x7 -> x0, matrix products: 10.8 us -> none  [the longest x2 5.99 us: column_terms(): return jnp.dot(matern(piece, embed), field, precision=lax.Precision.HIGHEST)]
    ppermute x4 -> x21, waiting for transfers between devices: 4.45 us -> 11.4 us  [the longest x6 6.23 us: over_leaf(): return lax.ppermute(value, 'leaf', [(i, i ^ m) for i in range(leaves)])]
  transfers between devices with their start and end apart: 6 -> 21, of which waited for: 4 -> 6; matrix products, arithmetic and copies ran while one was open for 4% -> 0% of each run, Pallas kernels for 0% -> 16%
where the time goes in v1:
time: 56 us; the launch traced here: 55.6 us
  starting transfers between devices  26.2 us (47%)
  Pallas kernels  14.3 us (26%)
  waiting for transfers between devices  11.4 us (20%)
  local copies, waits for them, and re-layouts  2.69 us (5%)
  between operations  0.94 us (2%)
    ppermute x9, starting transfers between devices, to_host(): lax.ppermute(value, ('leaf', 'inner'), route)  16.3 us
    pallas_call x5, Pallas kernels, call(): pl.pallas_call(kernel, out_shape=[jax.ShapeDtypeStruct(shape, dtype) for...  14.3 us
    ppermute x6, waiting for transfers between devices, over_leaf(): return lax.ppermute(value, 'leaf', [(i, i ^ m) for i in range(leaves)])  6.23 us
    ppermute x6, starting transfers between devices, from_host(): lax.ppermute(value, ('leaf', 'inner'), [(b, a) for a, b in route])  5.24 us
    ppermute x6, waiting for transfers between devices, from_host(): lax.ppermute(value, ('leaf', 'inner'), [(b, a) for a, b in route])  5.12 us
    ppermute x6, starting transfers between devices, over_leaf(): return lax.ppermute(value, 'leaf', [(i, i ^ m) for i in range(leaves)])  4.63 us
    unnamed x10, local copies, waits for them, and re-layouts  2.69 us
  transfers between devices with their start and end apart: 21, of which 6 were waited for; matrix products, arithmetic and copies ran while one was open for 0% of the time, Pallas kernels for 16%

profile of v1, /device:TPU:0, one launch (start us, length us, event | category | flops | bytes accessed | tf_op | source)
XLA Modules:
  0.0 55.6 jit_solution(4317965262056658579)
XLA Ops:
  0.6 0.7 %collective-permute-start = (bf16[384,256]{1,0:T(8,128)(2,1)}, bf16[384,256]{1,0:T(8,128)(2,1)S(1)}, u32[]{:S(2)}, u32[]{:S(2)}) collective-permute-start(bf16[384,256]{1,0:T(8,128)(2,1)} %refs_0_.2), channel_id=1, source_target_pairs={{1,2},{6,5},{9,10},{14,13},{17,18},{22,21},{25,26},{30,29}} | collective-permute-start | bytes 589832 | tf_op jit(solution)/shard_map/ppermute | solution.py:314
  1.3 1.0 %copy-done = bf16[3,384,128]{2,1,0:T(8,128)(2,1)S(1)} copy-done((bf16[3,384,128]{2,1,0:T(8,128)(2,1)S(1)}, bf16[3,384,128]{2,1,0:T(8,128)(2,1)}, u32[]{:S(2)}) %copy-start) | copy-done | bytes 294936
  2.3 0.8 %copy-done.2 = f32[384,32]{0,1:T(8,128)S(1)} copy-done((f32[384,32]{0,1:T(8,128)S(1)}, f32[384,32]{0,1:T(8,128)}, u32[]{:S(2)}) %copy-start.2) | copy-done | bytes 49176
  3.1 0.2 shard_map.51.proj_ref
  3.3 0.5 collective-permute-start.6
  3.8 2.6 %collective-permute-start.7 = (f32[32,128]{1,0:T(8,128)S(1)}, f32[32,128]{1,0:T(8,128)S(1)}, u32[]{:S(2)}, u32[]{:S(2)}) collective-permute-start(f32[32,128]{1,0:T(8,128)S(1)} %slice.10), channel_id=1, source_target_pairs={{0,8},{4,12},{8,0},{12,4},{1,9},{5,13},{9,1},{13,5},{2,10},{6,14},... | collective-permute-start | bytes 49160 | tf_op jit(solution)/shard_map/ppermute | solution.py:324
  6.4 1.7 %collective-permute-done.7.refs_1_ = f32[32,128]{1,0:T(8,128)S(1)} collective-permute-done((f32[32,128]{1,0:T(8,128)S(1)}, f32[32,128]{1,0:T(8,128)S(1)}, u32[]{:S(2)}, u32[]{:S(2)}) %collective-permute-start.7) | collective-permute-done | bytes 16416 | tf_op jit(solution)/shard_map/ppermute | solution.py:324
  8.1 1.4 %collective-permute-done.8.refs_2_ = f32[32,128]{1,0:T(8,128)S(1)} collective-permute-done((f32[32,128]{1,0:T(8,128)S(1)}, f32[32,128]{1,0:T(8,128)S(1)}, u32[]{:S(2)}, u32[]{:S(2)}) %collective-permute-start.8) | collective-permute-done | bytes 16416 | tf_op jit(solution)/shard_map/ppermute | solution.py:324
  9.5 0.7 %collective-permute-start.10 = (f32[192,128]{1,0:T(8,128)S(1)}, f32[192,128]{1,0:T(8,128)S(1)}, u32[]{:S(2)}, u32[]{:S(2)}) collective-permute-start(f32[192,128]{1,0:T(8,128)S(1)} %shard_map.52.refs_4_), channel_id=1, source_target_pairs={{3,2},{4,5},{11,10},{12,13},{19,18},{20,21},{27,26},{28,29}} | collective-permute-start | bytes 294920 | tf_op jit(solution)/shard_map/ppermute | solution.py:314
  10.2 0.7 %collective-permute-start.1 = (bf16[384,256]{1,0:T(8,128)(2,1)}, bf16[384,256]{1,0:T(8,128)(2,1)S(1)}, u32[]{:S(2)}, u32[]{:S(2)}) collective-permute-start(bf16[384,256]{1,0:T(8,128)(2,1)} %refs_0_.2), channel_id=1, source_target_pairs={{3,2},{4,5},{11,10},{12,13},{19,18},{20,21},{27,26},{28,29}} | collective-permute-start | bytes 589832 | tf_op jit(solution)/shard_map/ppermute | solution.py:314
  10.9 7.1 %collective-permute-start.2 = (bf16[384,256]{1,0:T(8,128)(2,1)}, bf16[384,256]{1,0:T(8,128)(2,1)S(1)}, u32[]{:S(2)}, u32[]{:S(2)}) collective-permute-start(bf16[384,256]{1,0:T(8,128)(2,1)} %refs_0_.2), channel_id=1, source_target_pairs={{0,2},{7,5},{8,10},{15,13},{16,18},{23,21},{24,26},{31,29}} | collective-permute-start | bytes 589832 | tf_op jit(solution)/shard_map/ppermute | solution.py:314
  18.0 0.7 %collective-permute-start.3 = (bf16[3,384,128]{2,1,0:T(8,128)(2,1)}, bf16[3,384,128]{2,1,0:T(8,128)(2,1)S(1)}, u32[]{:S(2)}, u32[]{:S(2)}) collective-permute-start(bf16[3,384,128]{2,1,0:T(8,128)(2,1)} %factors_ref.3), channel_id=1, source_target_pairs={{1,2},{6,5},{9,10},{14,13},{17,18},{22,21},{25,26},{30,29}} | collective-permute-start | bytes 884744 | tf_op jit(solution)/shard_map/ppermute | solution.py:314
  18.7 0.7 %collective-permute-start.4 = (bf16[3,384,128]{2,1,0:T(8,128)(2,1)}, bf16[3,384,128]{2,1,0:T(8,128)(2,1)S(1)}, u32[]{:S(2)}, u32[]{:S(2)}) collective-permute-start(bf16[3,384,128]{2,1,0:T(8,128)(2,1)} %factors_ref.3), channel_id=1, source_target_pairs={{3,2},{4,5},{11,10},{12,13},{19,18},{20,21},{27,26},{28,29}} | collective-permute-start | bytes 884744 | tf_op jit(solution)/shard_map/ppermute | solution.py:314
  19.4 3.8 %collective-permute-start.5 = (bf16[3,384,128]{2,1,0:T(8,128)(2,1)}, bf16[3,384,128]{2,1,0:T(8,128)(2,1)S(1)}, u32[]{:S(2)}, u32[]{:S(2)}) collective-permute-start(bf16[3,384,128]{2,1,0:T(8,128)(2,1)} %factors_ref.3), channel_id=1, source_target_pairs={{0,2},{7,5},{8,10},{15,13},{16,18},{23,21},{24,26},{31,29}} | collective-permute-start | bytes 884744 | tf_op jit(solution)/shard_map/ppermute | solution.py:314
  23.2 1.4 %collective-permute-start.11 = (f32[192,128]{1,0:T(8,128)S(1)}, f32[192,128]{1,0:T(8,128)S(1)}, u32[]{:S(2)}, u32[]{:S(2)}) collective-permute-start(f32[192,128]{1,0:T(8,128)S(1)} %shard_map.52.refs_4_), channel_id=1, source_target_pairs={{0,2},{7,5},{8,10},{15,13},{16,18},{23,21},{24,26},{31,29}} | collective-permute-start | bytes 294920 | tf_op jit(solution)/shard_map/ppermute | solution.py:314
  24.6 0.7 %collective-permute-start.9 = (f32[192,128]{1,0:T(8,128)S(1)}, f32[192,128]{1,0:T(8,128)S(1)}, u32[]{:S(2)}, u32[]{:S(2)}) collective-permute-start(f32[192,128]{1,0:T(8,128)S(1)} %shard_map.52.refs_4_), channel_id=1, source_target_pairs={{1,2},{6,5},{9,10},{14,13},{17,18},{22,21},{25,26},{30,29}} | collective-permute-start | bytes 294920 | tf_op jit(solution)/shard_map/ppermute | solution.py:314
  25.3 0.9 %copy-done.4 = bf16[384,256]{1,0:T(8,128)(2,1)S(1)} copy-done((bf16[384,256]{1,0:T(8,128)(2,1)S(1)}, bf16[384,256]{1,0:T(8,128)(2,1)}, u32[]{:S(2)}) %copy-start.4) | copy-done | bytes 196632
  26.2 8.7 %shard_map.50 = (bf16[10,384,384]{2,1,0:T(8,128)(2,1)S(1)}, bf16[10,384,384]{2,1,0:T(8,128)(2,1)S(1)}) custom-call(bf16[384,256]{1,0:T(8,128)(2,1)S(1)} %copy-done.4, bf16[384,256]{1,0:T(8,128)(2,1)S(1)} %collective-permute-done.refs_1_, bf16[384,256]{1,0:T(8,128)(2,1)S(1)} %collective-permute-done.1.refs_2_, bf16[384,256]{1,0:T(8,128)(2,1)S(1)} %collective-permute-done.2.refs_3_), custom_call_target="tpu_custom_call" | custom-call | flops 754974720 | bytes 786432 | tf_op jit(solution)/shard_map/pallas_call | solution.py:284
  35.1 4.6 %shard_map.53 = (bf16[32,512]{1,0:T(8,128)(2,1)S(1)}, f32[64,384]{1,0:T(8,128)S(1)}, f32[64,384]{1,0:T(8,128)S(1)}, f32[64,384]{1,0:T(8,128)S(1)}, f32[64,384]{1,0:T(8,128)S(1)}) custom-call(s32[1]{0:T(128)} %bitcast.1.is_host_ref, bf16[10,384,384]{2,1,0:T(8,128)(2,1)S(1)} %get-tuple-element.11.high_ref, ...), custom_call_target="tpu_custom_call" | custom-call | bytes 7471108 | tf_op jit(solution)/shard_map/pallas_call | solution.py:284
  39.6 0.7 %collective-permute-start.12 = (bf16[32,512]{1,0:T(8,128)(2,1)S(1)}, bf16[32,512]{1,0:T(8,128)(2,1)S(1)}, u32[]{:S(2)}, u32[]{:S(2)}) collective-permute-start(bf16[32,512]{1,0:T(8,128)(2,1)S(1)} %get-tuple-element.13), channel_id=1, source_target_pairs={{2,1},{5,6},{10,9},{13,14},{18,17},{21,22},{26,25},{29,30}} | collective-permute-start | bytes 98312 | tf_op jit(solution)/shard_map/ppermute | solution.py:318
  40.3 0.7 %collective-permute-start.13 = (bf16[32,512]{1,0:T(8,128)(2,1)S(1)}, bf16[32,512]{1,0:T(8,128)(2,1)S(1)}, u32[]{:S(2)}, u32[]{:S(2)}) collective-permute-start(bf16[32,512]{1,0:T(8,128)(2,1)S(1)} %get-tuple-element.13), channel_id=1, source_target_pairs={{2,3},{5,4},{10,11},{13,12},{18,19},{21,20},{26,27},{29,28}} | collective-permute-start | bytes 98312 | tf_op jit(solution)/shard_map/ppermute | solution.py:318
  41.0 1.3 %collective-permute-start.14 = (bf16[32,512]{1,0:T(8,128)(2,1)S(1)}, bf16[32,512]{1,0:T(8,128)(2,1)S(1)}, u32[]{:S(2)}, u32[]{:S(2)}) collective-permute-start(bf16[32,512]{1,0:T(8,128)(2,1)S(1)} %get-tuple-element.13), channel_id=1, source_target_pairs={{2,0},{5,7},{10,8},{13,15},{18,16},{21,23},{26,24},{29,31}} | collective-permute-start | bytes 98312 | tf_op jit(solution)/shard_map/ppermute | solution.py:318
  42.3 0.7 %collective-permute-start.18 = (f32[64,384]{1,0:T(8,128)S(1)}, f32[64,384]{1,0:T(8,128)S(1)}, u32[]{:S(2)}, u32[]{:S(2)}) collective-permute-start(f32[64,384]{1,0:T(8,128)S(1)} %get-tuple-element.15), channel_id=1, source_target_pairs={{2,1},{5,6},{10,9},{13,14},{18,17},{21,22},{26,25},{29,30}} | collective-permute-start | bytes 294920 | tf_op jit(solution)/shard_map/ppermute | solution.py:318
  43.0 0.7 %collective-permute-start.19 = (f32[64,384]{1,0:T(8,128)S(1)}, f32[64,384]{1,0:T(8,128)S(1)}, u32[]{:S(2)}, u32[]{:S(2)}) collective-permute-start(f32[64,384]{1,0:T(8,128)S(1)} %get-tuple-element.16), channel_id=1, source_target_pairs={{2,3},{5,4},{10,11},{13,12},{18,19},{21,20},{26,27},{29,28}} | collective-permute-start | bytes 294920 | tf_op jit(solution)/shard_map/ppermute | solution.py:318
  43.6 1.3 %collective-permute-start.20 = (f32[64,384]{1,0:T(8,128)S(1)}, f32[64,384]{1,0:T(8,128)S(1)}, u32[]{:S(2)}, u32[]{:S(2)}) collective-permute-start(f32[64,384]{1,0:T(8,128)S(1)} %get-tuple-element.17), channel_id=1, source_target_pairs={{2,0},{5,7},{10,8},{13,15},{18,16},{21,23},{26,24},{29,31}} | collective-permute-start | bytes 294920 | tf_op jit(solution)/shard_map/ppermute | solution.py:318
  45.0 5.1 %collective-permute-done.14 = bf16[32,512]{1,0:T(8,128)(2,1)S(1)} collective-permute-done((bf16[32,512]{1,0:T(8,128)(2,1)S(1)}, bf16[32,512]{1,0:T(8,128)(2,1)S(1)}, u32[]{:S(2)}, u32[]{:S(2)}) %collective-permute-start.14) | collective-permute-done | bytes 32800 | tf_op jit(solution)/shard_map/ppermute | solution.py:318
  50.1 0.7 %collective-permute-start.16 = (bf16[32,512]{1,0:T(8,128)(2,1)S(1)}, bf16[32,512]{1,0:T(8,128)(2,1)S(1)}, u32[]{:S(2)}, u32[]{:S(2)}) collective-permute-start(bf16[32,512]{1,0:T(8,128)(2,1)S(1)} %add_add_fusion.refs_0_), channel_id=1, source_target_pairs={{0,8},{4,12},{8,0},{12,4},{1,9},{5,13},{9,1},{13,5},{2,10},{6,14},... | collective-permute-start | bytes 98312 | tf_op jit(solution)/shard_map/ppermute | solution.py:324
  50.9 0.5 collective-permute-done.15.refs_1_
  51.3 0.7 %collective-permute-start.17 = (bf16[32,512]{1,0:T(8,128)(2,1)S(1)}, bf16[32,512]{1,0:T(8,128)(2,1)S(1)}, u32[]{:S(2)}, u32[]{:S(2)}) collective-permute-start(bf16[32,512]{1,0:T(8,128)(2,1)S(1)} %add_add_fusion.refs_0_), channel_id=1, source_target_pairs={{0,12},{4,8},{8,4},{12,0},{1,13},{5,9},{9,5},{13,1},{2,14},{6,10},... | collective-permute-start | bytes 98312 | tf_op jit(solution)/shard_map/ppermute | solution.py:324
  52.0 2.1 %collective-permute-done.16.refs_2_ = bf16[32,512]{1,0:T(8,128)(2,1)S(1)} collective-permute-done((bf16[32,512]{1,0:T(8,128)(2,1)S(1)}, bf16[32,512]{1,0:T(8,128)(2,1)S(1)}, u32[]{:S(2)}, u32[]{:S(2)}) %collective-permute-start.16) | collective-permute-done | bytes 32800 | tf_op jit(solution)/shard_map/ppermute | solution.py:324
  54.1 0.6 %collective-permute-done.17.refs_3_ = bf16[32,512]{1,0:T(8,128)(2,1)S(1)} collective-permute-done((bf16[32,512]{1,0:T(8,128)(2,1)S(1)}, bf16[32,512]{1,0:T(8,128)(2,1)S(1)}, u32[]{:S(2)}, u32[]{:S(2)}) %collective-permute-start.17) | collective-permute-done | bytes 32800 | tf_op jit(solution)/shard_map/ppermute | solution.py:324
  54.7 0.8 %shard_map.54 = (f32[32,384]{1,0:T(8,128)}, f32[32,384]{1,0:T(8,128)}) custom-call(f32[32,384]{1,0:T(8,128)S(1)} %bitcast.6, bf16[3,384,128]{2,1,0:T(8,128)(2,1)S(1)} %copy-done.1, bf16[32,512]{1,0:T(8,128)(2,1)S(1)} %add_add_fusion.refs_0_, bf16[32,512]{1,0:T(8,128)(2,1)S(1)} %collective-permute-done.15.refs_1_, ...), custom_call_target="tpu_custom_call" | custom-call | bytes 868352 | tf_op jit(solution)/shard_map/pallas_call | solution.py:284
  (28 shorter events, 0.2 us)
Async XLA Ops:
  0.6 18.7 %collective-permute-start = (bf16[384,256]{1,0:T(8,128)(2,1)}, bf16[384,256]{1,0:T(8,128)(2,1)S(1)}, u32[]{:S(2)}, u32[]{:S(2)}) collective-permute-start(bf16[384,256]{1,0:T(8,128)(2,1)} %refs_0_.2), channel_id=1, source_target_pairs={{1,2},{6,5},{9,10},{14,13},{17,18},{22,21},{25,26},{30,29}} | collective-permute-start | bytes 589832 | tf_op jit(solution)/shard_map/ppermute | solution.py:314
  1.3 1.0 %copy-start = (bf16[3,384,128]{2,1,0:T(8,128)(2,1)S(1)}, bf16[3,384,128]{2,1,0:T(8,128)(2,1)}, u32[]{:S(2)}) copy-start(bf16[3,384,128]{2,1,0:T(8,128)(2,1)} %factors_ref.3) | copy-start | bytes 884740
  2.3 0.8 %copy-start.2 = (f32[384,32]{0,1:T(8,128)S(1)}, f32[384,32]{0,1:T(8,128)}, u32[]{:S(2)}) copy-start(f32[384,32]{0,1:T(8,128)} %param.5) | copy-start | bytes 147460
  3.1 32.0 %copy-start.1 = (bf16[3,384,128]{2,1,0:T(8,128)(2,1)S(1)}, bf16[3,384,128]{2,1,0:T(8,128)(2,1)}, u32[]{:S(2)}) copy-start(bf16[3,384,128]{2,1,0:T(8,128)(2,1)} %factors_ref.3) | copy-start | bytes 884740
  3.3 6.3 %collective-permute-start.6 = (f32[64,128]{1,0:T(8,128)S(1)}, f32[64,128]{1,0:T(8,128)S(1)}, u32[]{:S(2)}, u32[]{:S(2)}) collective-permute-start(f32[64,128]{1,0:T(8,128)S(1)} %slice.9), channel_id=1, source_target_pairs={{0,4},{4,0},{8,12},{12,8},{1,5},{5,1},{9,13},{13,9},{2,6},{6,2},{1... | collective-permute-start | bytes 98312 | tf_op jit(solution)/shard_map/ppermute | solution.py:324
  3.8 4.3 %collective-permute-start.7 = (f32[32,128]{1,0:T(8,128)S(1)}, f32[32,128]{1,0:T(8,128)S(1)}, u32[]{:S(2)}, u32[]{:S(2)}) collective-permute-start(f32[32,128]{1,0:T(8,128)S(1)} %slice.10), channel_id=1, source_target_pairs={{0,8},{4,12},{8,0},{12,4},{1,9},{5,13},{9,1},{13,5},{2,10},{6,14},... | collective-permute-start | bytes 49160 | tf_op jit(solution)/shard_map/ppermute | solution.py:324
  6.3 3.2 %collective-permute-start.8 = (f32[32,128]{1,0:T(8,128)S(1)}, f32[32,128]{1,0:T(8,128)S(1)}, u32[]{:S(2)}, u32[]{:S(2)}) collective-permute-start(f32[32,128]{1,0:T(8,128)S(1)} %slice.10), channel_id=1, source_target_pairs={{0,12},{4,8},{8,4},{12,0},{1,13},{5,9},{9,5},{13,1},{2,14},{6,10},... | collective-permute-start | bytes 49160 | tf_op jit(solution)/shard_map/ppermute | solution.py:324
  9.5 9.1 %collective-permute-start.10 = (f32[192,128]{1,0:T(8,128)S(1)}, f32[192,128]{1,0:T(8,128)S(1)}, u32[]{:S(2)}, u32[]{:S(2)}) collective-permute-start(f32[192,128]{1,0:T(8,128)S(1)} %shard_map.52.refs_4_), channel_id=1, source_target_pairs={{3,2},{4,5},{11,10},{12,13},{19,18},{20,21},{27,26},{28,29}} | collective-permute-start | bytes 294920 | tf_op jit(solution)/shard_map/ppermute | solution.py:314
  10.2 13.0 %collective-permute-start.1 = (bf16[384,256]{1,0:T(8,128)(2,1)}, bf16[384,256]{1,0:T(8,128)(2,1)S(1)}, u32[]{:S(2)}, u32[]{:S(2)}) collective-permute-start(bf16[384,256]{1,0:T(8,128)(2,1)} %refs_0_.2), channel_id=1, source_target_pairs={{3,2},{4,5},{11,10},{12,13},{19,18},{20,21},{27,26},{28,29}} | collective-permute-start | bytes 589832 | tf_op jit(solution)/shard_map/ppermute | solution.py:314
  10.9 13.7 %collective-permute-start.2 = (bf16[384,256]{1,0:T(8,128)(2,1)}, bf16[384,256]{1,0:T(8,128)(2,1)S(1)}, u32[]{:S(2)}, u32[]{:S(2)}) collective-permute-start(bf16[384,256]{1,0:T(8,128)(2,1)} %refs_0_.2), channel_id=1, source_target_pairs={{0,2},{7,5},{8,10},{15,13},{16,18},{23,21},{24,26},{31,29}} | collective-permute-start | bytes 589832 | tf_op jit(solution)/shard_map/ppermute | solution.py:314
  18.0 17.0 %collective-permute-start.3 = (bf16[3,384,128]{2,1,0:T(8,128)(2,1)}, bf16[3,384,128]{2,1,0:T(8,128)(2,1)S(1)}, u32[]{:S(2)}, u32[]{:S(2)}) collective-permute-start(bf16[3,384,128]{2,1,0:T(8,128)(2,1)} %factors_ref.3), channel_id=1, source_target_pairs={{1,2},{6,5},{9,10},{14,13},{17,18},{22,21},{25,26},{30,29}} | collective-permute-start | bytes 884744 | tf_op jit(solution)/shard_map/ppermute | solution.py:314
  18.7 16.3 %collective-permute-start.4 = (bf16[3,384,128]{2,1,0:T(8,128)(2,1)}, bf16[3,384,128]{2,1,0:T(8,128)(2,1)S(1)}, u32[]{:S(2)}, u32[]{:S(2)}) collective-permute-start(bf16[3,384,128]{2,1,0:T(8,128)(2,1)} %factors_ref.3), channel_id=1, source_target_pairs={{3,2},{4,5},{11,10},{12,13},{19,18},{20,21},{27,26},{28,29}} | collective-permute-start | bytes 884744 | tf_op jit(solution)/shard_map/ppermute | solution.py:314
  19.4 15.7 %collective-permute-start.5 = (bf16[3,384,128]{2,1,0:T(8,128)(2,1)}, bf16[3,384,128]{2,1,0:T(8,128)(2,1)S(1)}, u32[]{:S(2)}, u32[]{:S(2)}) collective-permute-start(bf16[3,384,128]{2,1,0:T(8,128)(2,1)} %factors_ref.3), channel_id=1, source_target_pairs={{0,2},{7,5},{8,10},{15,13},{16,18},{23,21},{24,26},{31,29}} | collective-permute-start | bytes 884744 | tf_op jit(solution)/shard_map/ppermute | solution.py:314
  23.2 11.8 %collective-permute-start.11 = (f32[192,128]{1,0:T(8,128)S(1)}, f32[192,128]{1,0:T(8,128)S(1)}, u32[]{:S(2)}, u32[]{:S(2)}) collective-permute-start(f32[192,128]{1,0:T(8,128)S(1)} %shard_map.52.refs_4_), channel_id=1, source_target_pairs={{0,2},{7,5},{8,10},{15,13},{16,18},{23,21},{24,26},{31,29}} | collective-permute-start | bytes 294920 | tf_op jit(solution)/shard_map/ppermute | solution.py:314
  24.6 10.4 %collective-permute-start.9 = (f32[192,128]{1,0:T(8,128)S(1)}, f32[192,128]{1,0:T(8,128)S(1)}, u32[]{:S(2)}, u32[]{:S(2)}) collective-permute-start(f32[192,128]{1,0:T(8,128)S(1)} %shard_map.52.refs_4_), channel_id=1, source_target_pairs={{1,2},{6,5},{9,10},{14,13},{17,18},{22,21},{25,26},{30,29}} | collective-permute-start | bytes 294920 | tf_op jit(solution)/shard_map/ppermute | solution.py:314
  25.3 0.9 %copy-start.4 = (bf16[384,256]{1,0:T(8,128)(2,1)S(1)}, bf16[384,256]{1,0:T(8,128)(2,1)}, u32[]{:S(2)}) copy-start(bf16[384,256]{1,0:T(8,128)(2,1)} %refs_0_.2) | copy-start | bytes 589828
  35.0 19.7 %copy-start.3 = (f32[384,32]{0,1:T(8,128)S(1)}, f32[384,32]{0,1:T(8,128)}, u32[]{:S(2)}) copy-start(f32[384,32]{0,1:T(8,128)} %param.5) | copy-start | bytes 147460
  39.6 4.0 %collective-permute-start.12 = (bf16[32,512]{1,0:T(8,128)(2,1)S(1)}, bf16[32,512]{1,0:T(8,128)(2,1)S(1)}, u32[]{:S(2)}, u32[]{:S(2)}) collective-permute-start(bf16[32,512]{1,0:T(8,128)(2,1)S(1)} %get-tuple-element.13), channel_id=1, source_target_pairs={{2,1},{5,6},{10,9},{13,14},{18,17},{21,22},{26,25},{29,30}} | collective-permute-start | bytes 98312 | tf_op jit(solution)/shard_map/ppermute | solution.py:318
  40.3 4.6 %collective-permute-start.13 = (bf16[32,512]{1,0:T(8,128)(2,1)S(1)}, bf16[32,512]{1,0:T(8,128)(2,1)S(1)}, u32[]{:S(2)}, u32[]{:S(2)}) collective-permute-start(bf16[32,512]{1,0:T(8,128)(2,1)S(1)} %get-tuple-element.13), channel_id=1, source_target_pairs={{2,3},{5,4},{10,11},{13,12},{18,19},{21,20},{26,27},{29,28}} | collective-permute-start | bytes 98312 | tf_op jit(solution)/shard_map/ppermute | solution.py:318
  41.0 9.1 %collective-permute-start.14 = (bf16[32,512]{1,0:T(8,128)(2,1)S(1)}, bf16[32,512]{1,0:T(8,128)(2,1)S(1)}, u32[]{:S(2)}, u32[]{:S(2)}) collective-permute-start(bf16[32,512]{1,0:T(8,128)(2,1)S(1)} %get-tuple-element.13), channel_id=1, source_target_pairs={{2,0},{5,7},{10,8},{13,15},{18,16},{21,23},{26,24},{29,31}} | collective-permute-start | bytes 98312 | tf_op jit(solution)/shard_map/ppermute | solution.py:318
  42.3 12.4 %collective-permute-start.18 = (f32[64,384]{1,0:T(8,128)S(1)}, f32[64,384]{1,0:T(8,128)S(1)}, u32[]{:S(2)}, u32[]{:S(2)}) collective-permute-start(f32[64,384]{1,0:T(8,128)S(1)} %get-tuple-element.15), channel_id=1, source_target_pairs={{2,1},{5,6},{10,9},{13,14},{18,17},{21,22},{26,25},{29,30}} | collective-permute-start | bytes 294920 | tf_op jit(solution)/shard_map/ppermute | solution.py:318
  43.0 11.7 %collective-permute-start.19 = (f32[64,384]{1,0:T(8,128)S(1)}, f32[64,384]{1,0:T(8,128)S(1)}, u32[]{:S(2)}, u32[]{:S(2)}) collective-permute-start(f32[64,384]{1,0:T(8,128)S(1)} %get-tuple-element.16), channel_id=1, source_target_pairs={{2,3},{5,4},{10,11},{13,12},{18,19},{21,20},{26,27},{29,28}} | collective-permute-start | bytes 294920 | tf_op jit(solution)/shard_map/ppermute | solution.py:318
  43.6 11.1 %collective-permute-start.20 = (f32[64,384]{1,0:T(8,128)S(1)}, f32[64,384]{1,0:T(8,128)S(1)}, u32[]{:S(2)}, u32[]{:S(2)}) collective-permute-start(f32[64,384]{1,0:T(8,128)S(1)} %get-tuple-element.17), channel_id=1, source_target_pairs={{2,0},{5,7},{10,8},{13,15},{18,16},{21,23},{26,24},{29,31}} | collective-permute-start | bytes 294920 | tf_op jit(solution)/shard_map/ppermute | solution.py:318
  50.1 1.3 %collective-permute-start.15 = (bf16[32,512]{1,0:T(8,128)(2,1)S(1)}, bf16[32,512]{1,0:T(8,128)(2,1)S(1)}, u32[]{:S(2)}, u32[]{:S(2)}) collective-permute-start(bf16[32,512]{1,0:T(8,128)(2,1)S(1)} %add_add_fusion.refs_0_), channel_id=1, source_target_pairs={{0,4},{4,0},{8,12},{12,8},{1,5},{5,1},{9,13},{13,9},{2,6},{6,2},{1... | collective-permute-start | bytes 98312 | tf_op jit(solution)/shard_map/ppermute | solution.py:324
  50.1 4.0 %collective-permute-start.16 = (bf16[32,512]{1,0:T(8,128)(2,1)S(1)}, bf16[32,512]{1,0:T(8,128)(2,1)S(1)}, u32[]{:S(2)}, u32[]{:S(2)}) collective-permute-start(bf16[32,512]{1,0:T(8,128)(2,1)S(1)} %add_add_fusion.refs_0_), channel_id=1, source_target_pairs={{0,8},{4,12},{8,0},{12,4},{1,9},{5,13},{9,1},{13,5},{2,10},{6,14},... | collective-permute-start | bytes 98312 | tf_op jit(solution)/shard_map/ppermute | solution.py:324
  51.3 3.3 %collective-permute-start.17 = (bf16[32,512]{1,0:T(8,128)(2,1)S(1)}, bf16[32,512]{1,0:T(8,128)(2,1)S(1)}, u32[]{:S(2)}, u32[]{:S(2)}) collective-permute-start(bf16[32,512]{1,0:T(8,128)(2,1)S(1)} %add_add_fusion.refs_0_), channel_id=1, source_target_pairs={{0,12},{4,8},{8,4},{12,0},{1,13},{5,9},{9,5},{13,1},{2,14},{6,10},... | collective-permute-start | bytes 98312 | tf_op jit(solution)/shard_map/ppermute | solution.py:324

commit v2 on v1

v2 whole, which is shorter than its diff:
```python
import functools

import jax
import jax.numpy as jnp
from jax import lax
from jax.experimental import pallas as pl
from jax.experimental.pallas import tpu as pltpu
from jax.sharding import PartitionSpec as P

ITERS = 2
LENGTH_SCALE = 2.3
FAST_LEAF = 2048
NEAR_FLOPS = 2 * 10**9
MAIN_FLOPS = 4 * 10**9
F32, BF16 = jnp.float32, jnp.bfloat16
VMEM = pl.BlockSpec(memory_space=pltpu.VMEM)
SMEM = pl.BlockSpec(memory_space=pltpu.SMEM)


def swapped(value, axis, apart):
    mask = 2**apart
    pairs = [(source, source ^ mask) for source in range(lax.axis_size(axis))]
    return lax.ppermute(value, axis, pairs)


def matern(left, right):
    left_f = left.astype(F32)
    right_f = right.astype(F32)
    left_sq = jnp.sum(left_f * left_f, axis=1)
    right_sq = jnp.sum(right_f * right_f, axis=1)
    inner_prod = lax.dot_general(
        left, right, (((1,), (1,)), ((), ())), preferred_element_type=F32
    )
    dist2 = left_sq[:, None] + right_sq[None, :] - 2.0 * inner_prod
    scaled = jnp.sqrt(3.0) * jnp.sqrt(jnp.maximum(dist2, 0.0)) / LENGTH_SCALE
    return (1.0 + scaled) * jnp.exp(-scaled)


def squares(residual):
    return lax.psum(jnp.sum(residual * residual, axis=0), ("leaf", "inner"))


def operate(embed, factors, field):
    piece = lax.all_gather(embed, "inner", axis=0, tiled=True)
    terms = jnp.dot(matern(piece, embed), field, precision=lax.Precision.HIGHEST)
    dense = lax.psum_scatter(terms, "inner", scatter_dimension=0, tiled=True)
    total = dense + 0.5 * field
    levels = factors.shape[0]
    rounded = field.astype(BF16)
    proj = jnp.einsum("lrk,rc->lkc", factors, rounded, preferred_element_type=F32)
    proj = lax.psum(proj, "inner")
    for bit in range(levels - 1):
        upper = proj[bit + 1 :]
        partner = swapped(upper, "leaf", bit)
        proj = jnp.concatenate([proj[: bit + 1], upper + partner], axis=0)
    back = jnp.einsum(
        "lrk,lkc->rc", factors, proj.astype(BF16), preferred_element_type=F32
    )
    return total + back


def stepwise(embed, factors, targets):
    result = jnp.zeros_like(targets)
    residual = targets
    direction = targets
    norm_now = squares(residual)
    for step in range(ITERS):
        image = operate(embed, factors, direction)
        curv = lax.psum(jnp.sum(direction * image, axis=0), ("leaf", "inner"))
        alpha = norm_now / curv
        result = result + alpha * direction
        residual = residual - alpha * image
        if step + 1 < ITERS:
            norm_next = squares(residual)
            direction = residual + norm_next / norm_now * direction
            norm_now = norm_next
    return (result, residual)


def mm(left, right):
    return lax.dot_general(left, right, (((1,), (0,)), ((), ())), preferred_element_type=F32)


def mm_nt(left, right):
    return lax.dot_general(left, right, (((1,), (1,)), ((), ())), preferred_element_type=F32)


def pairs_of(slots):
    return [(i, j) for j in range(slots) for i in range(j + 1)]


def pack_kernel(embed_hbm, factors_hbm, field_hbm, message_ref, proj_ref, field_ref, sems):
    levels, rows, rank = factors_hbm.shape
    nrhs = field_ref.shape[0]
    lanes = embed_hbm.shape[1] // rank
    copies = [
        pltpu.make_async_copy(field_hbm, field_ref, sems.at[0]),
    ]
    for level in range(levels):
        place = message_ref.at[pl.ds((lanes + level) * rows, rows)]
        copies.append(pltpu.make_async_copy(factors_hbm.at[level], place, sems.at[1 + level]))
    for k in range(lanes):
        piece = embed_hbm.at[:, pl.ds(k * rank, rank)]
        place = message_ref.at[pl.ds(k * rows, rows)]
        copies.append(pltpu.make_async_copy(piece, place, sems.at[1 + levels + k]))
    for copy in copies:
        copy.start()
    copies[0].wait()
    field = field_ref[...]
    high = field.astype(BF16)
    low = (field - high.astype(F32)).astype(BF16)
    base = (lanes + levels) * rows
    for k in range(rows // rank):
        span = slice(k * rank, (k + 1) * rank)
        message_ref[base + 2 * k * nrhs : base + (2 * k + 1) * nrhs] = high[:, span]
        message_ref[base + (2 * k + 1) * nrhs : base + (2 * k + 2) * nrhs] = low[:, span]
    for level in range(levels):
        copies[1 + level].wait()
        factor = message_ref[(lanes + level) * rows : (lanes + level + 1) * rows]
        proj_ref[level * nrhs : (level + 1) * nrhs] = mm(high, factor)
    for k in range(lanes):
        copies[1 + levels + k].wait()


class Message:
    def __init__(self, ref, shape):
        self.ref = ref
        self.rows, self.dims, self.levels, self.rank, self.nrhs = shape
        self.lanes = self.dims // self.rank

    def embed(self):
        rows = self.rows
        return jnp.concatenate(
            [self.ref[k * rows : (k + 1) * rows] for k in range(self.lanes)], axis=1
        )

    def factor(self, level):
        start = (self.lanes + level) * self.rows
        return self.ref[start : start + self.rows]

    def field(self):
        base = (self.lanes + self.levels) * self.rows
        step = 2 * self.nrhs
        return jnp.concatenate(
            [self.ref[base + k * step : base + (k + 1) * step] for k in range(self.rows // self.rank)],
            axis=1,
        )


def norms_of(embed):
    scale = 3.0 / LENGTH_SCALE**2
    wide_e = embed.astype(F32)
    square = wide_e * wide_e
    column = scale * jnp.sum(square, axis=1, keepdims=True)
    first = square.astype(BF16)
    rest = (square - first.astype(F32)).astype(BF16)
    ones = jnp.ones((8, embed.shape[1]), BF16)
    row = scale * (mm_nt(ones, first) + mm_nt(ones, rest))
    return column, row[0:1]


def kern_block(left, right, column, row):
    scale = 3.0 / LENGTH_SCALE**2
    product = mm_nt(left, right)
    dist = jnp.maximum((column + row) - (2.0 * scale) * product, 1e-30)
    scaled = dist * lax.rsqrt(dist)
    value = (1.0 + scaled) * jnp.exp(-scaled)
    high = value.astype(BF16)
    return high, (value - high.astype(F32)).astype(BF16)


def first_products(pairs, messages, high_ref, image_ref):
    nrhs = messages[0].nrhs
    norms = {}
    for index, (i, j) in enumerate(pairs):
        for s in (i, j):
            if s not in norms:
                norms[s] = norms_of(messages[s].embed())
        high, low = kern_block(messages[i].embed(), messages[j].embed(), norms[i][0], norms[j][1])
        high_ref[index] = high
        field = messages[i].field()
        stacked = mm(field, high)
        image_ref[j] += stacked[:nrhs] + stacked[nrhs:] + mm(field[:nrhs], low)
        if i != j:
            field = messages[j].field()
            stacked = mm_nt(field, high)
            image_ref[i] += stacked[:nrhs] + stacked[nrhs:] + mm_nt(field[:nrhs], low)


def near_kernel(near, shape, *refs):
    high_ref, image_ref = refs[near:]
    image_ref[...] = jnp.zeros_like(image_ref)
    messages = [Message(ref, shape) for ref in refs[:near]]
    first_products(pairs_of(near), messages, high_ref, image_ref)


def main_kernel(slots, shape, is_host_ref, near_high_ref, near_image_ref, *refs):
    messages = [Message(ref, shape) for ref in refs[:slots]]
    sums_in = refs[slots : 2 * slots]
    sums_ref = refs[2 * slots]
    fields_out = refs[2 * slots + 1 : -2]
    far_high_ref, image_ref = refs[-2:]
    rows, _, levels, rank, nrhs = shape
    near = near_image_ref.shape[0]
    pairs = pairs_of(slots)
    held = len(pairs_of(near))
    image_ref[:near] = near_image_ref[...]
    image_ref[near:] = jnp.zeros_like(image_ref[near:])
    first_products(pairs[held:], messages, far_high_ref, image_ref)
    proj = sums_in[0][...]
    for s in range(1, slots):
        proj = proj + sums_in[s][...]
    proj = proj.astype(BF16)
    mine = is_host_ref[0] == 1

    def own(value, s):
        return jnp.where(mine, value, jnp.zeros_like(value)) if s == 0 else value

    field, image, image_b = [], [], []
    for s in range(slots):
        halves = messages[s].field().astype(F32)
        field.append(halves[:nrhs] + halves[nrhs:])
        total = image_ref[s] + 0.5 * field[s]
        for level in range(levels):
            total = total + mm_nt(proj[level * nrhs : (level + 1) * nrhs], messages[s].factor(level))
        image.append(total)
        image_b.append(total.astype(BF16))
        fields_out[s][:nrhs] = own(total, s)
    norms = []
    for level in range(levels):
        total = mm(image_b[0], messages[0].factor(level))
        for s in range(1, slots):
            total = total + mm(image_b[s], messages[s].factor(level))
        if level == 0:
            norms.append(jnp.sum(total * total, axis=1, keepdims=True))
        sums_ref[:, level * rank : (level + 1) * rank] = own(total.astype(BF16), 0)
    second = [jnp.zeros((nrhs, rows), F32) for _ in range(slots)]
    for index, (i, j) in enumerate(pairs):
        high = near_high_ref[index] if index < held else far_high_ref[index - held]
        second[j] = second[j] + mm(image_b[i], high)
        if i != j:
            second[i] = second[i] + mm_nt(image_b[j], high)
    for s in range(slots):
        fields_out[s][nrhs:] = own(second[s], s)

    def dots(left, right):
        total = left[0] * right[0]
        for s in range(1, slots):
            total = total + left[s] * right[s]
        return jnp.sum(total, axis=1, keepdims=True)

    scalars = [
        dots(field, field),
        dots(field, image),
        dots(image, image),
        dots(image, second) + norms[0],
    ]
    lane = lax.broadcasted_iota(jnp.int32, (nrhs, 128), 1)
    packed = jnp.zeros((nrhs, 128), F32)
    for k, value in enumerate(scalars):
        value = jnp.broadcast_to(value, (nrhs, 128))
        for piece in range(3):
            rounded = value.astype(BF16).astype(F32)
            packed = jnp.where(lane == 3 * k + piece, rounded, packed)
            value = value - rounded
    sums_ref[:, levels * rank :] = own(packed.astype(BF16), 0)


def finish_kernel(leaves, slots, shape, field_ref, message_ref, *refs):
    sums = refs[:leaves]
    parts = refs[leaves : leaves + slots]
    solution_ref, residual_ref = refs[leaves + slots :]
    rows, _, levels, rank, nrhs = shape
    message = Message(message_ref, shape)
    field = field_ref[...]
    total = parts[0][...]
    for s in range(1, slots):
        total = total + parts[s][...]
    image = total[:nrhs]
    second = total[nrhs:] + 0.5 * image
    lane = lax.broadcasted_iota(jnp.int32, (nrhs, 128), 1)
    packed = sums[0][:, levels * rank :].astype(F32)
    for m in range(1, leaves):
        packed = packed + sums[m][:, levels * rank :].astype(F32)

    def scalar(k):
        inside = (lane >= 3 * k) & (lane < 3 * k + 3)
        return jnp.sum(jnp.where(inside, packed, 0.0), axis=1, keepdims=True)

    bb, bw, ww, wu = (scalar(k) for k in range(4))
    wu = wu + 0.5 * ww
    for level in range(levels):
        nodes = {}
        for m in range(leaves):
            value = sums[m][:, level * rank : (level + 1) * rank].astype(F32)
            node = m >> level
            nodes[node] = nodes[node] + value if node in nodes else value
        second = second + mm_nt(nodes[0].astype(BF16), message.factor(level))
        if level > 0:
            squared = sum(value * value for value in nodes.values())
            wu = wu + jnp.sum(squared, axis=1, keepdims=True)
    alpha0 = bb / bw
    norm1 = alpha0 * alpha0 * ww - bb
    ratio = norm1 / bb
    keep = 1.0 + ratio
    curv = keep * keep * bw - 2.0 * keep * alpha0 * ww + alpha0 * alpha0 * wu
    alpha1 = norm1 / curv
    solution_ref[...] = (alpha0 + alpha1 * keep) * field - (alpha1 * alpha0) * image
    residual_ref[...] = field - (alpha0 + alpha1 * keep) * image + (alpha1 * alpha0) * second


def call(kernel, outs, args, specs, scratch=(), flops=0, limit=24):
    moved = sum(a.size * a.dtype.itemsize for a in args)
    return pl.pallas_call(
        kernel,
        out_shape=[jax.ShapeDtypeStruct(shape, dtype) for shape, dtype in outs],
        in_specs=specs,
        out_specs=[VMEM] * len(outs),
        scratch_shapes=list(scratch),
        cost_estimate=pl.CostEstimate(flops=flops, bytes_accessed=moved, transcendentals=0),
        compiler_params=pltpu.CompilerParams(vmem_limit_bytes=limit * 2**20),
    )(*args)


def collected(embed, factors, targets):
    leaves, inner = lax.axis_size("leaf"), lax.axis_size("inner")
    levels, rows, rank = factors.shape
    dims, nrhs = embed.shape[1], targets.shape[1]
    shape = (rows, dims, levels, rank, nrhs)

    def host(leaf):
        return inner // 2 if leaf % 2 == 0 else (inner - 1) // 2

    def others(leaf):
        sign = 1 if leaf % 2 == 0 else -1
        here = host(leaf)
        return sorted((z for z in range(inner) if z != here), key=lambda z: (abs(z - here), sign * z))

    routes = [
        [(leaf * inner + others(leaf)[k], leaf * inner + host(leaf)) for leaf in range(leaves)]
        for k in range(inner - 1)
    ]

    def to_host(value):
        return [value] + [lax.ppermute(value, ("leaf", "inner"), route) for route in routes]

    def from_host(values):
        back = [
            lax.ppermute(value, ("leaf", "inner"), [(b, a) for a, b in route])
            for value, route in zip(values[1:], routes)
        ]
        return [values[0]] + back

    def over_leaf(value, m):
        return lax.ppermute(value, "leaf", [(i, i ^ m) for i in range(leaves)])

    height = (dims // rank + levels) * rows + 2 * nrhs * (rows // rank)
    message, proj, field = call(
        pack_kernel,
        [((height, rank), BF16), ((levels * nrhs, rank), F32), ((nrhs, rows), F32)],
        [embed, factors, targets.T],
        [pl.BlockSpec(memory_space=pltpu.HBM)] * 3,
        scratch=[pltpu.SemaphoreType.DMA((1 + levels + dims // rank,))],
    )
    messages = to_host(message)
    pieces = [proj[level * nrhs : (level + 1) * nrhs] for level in range(levels)]
    for m in range(1, leaves):
        start = m.bit_length()
        if start < levels:
            arrived = over_leaf(proj[start * nrhs :], m)
            for level in range(start, levels):
                at = (level - start) * nrhs
                pieces[level] = pieces[level] + arrived[at : at + nrhs]
    near = inner - 1
    held = len(pairs_of(near))
    near_high, near_image = call(
        functools.partial(near_kernel, near, shape),
        [((held, rows, rows), BF16), ((near, nrhs, rows), F32)],
        messages[:near],
        [VMEM] * near,
        flops=NEAR_FLOPS,
    )
    partial_sums = to_host(jnp.concatenate(pieces, axis=0))
    leaf = lax.axis_index("leaf")
    here = jnp.where(leaf % 2 == 0, host(0), host(1))
    is_host = (lax.axis_index("inner") == here).astype(jnp.int32).reshape(1)
    results = call(
        functools.partial(main_kernel, inner, shape),
        [((nrhs, levels * rank + 128), BF16)] + [((2 * nrhs, rows), F32)] * inner,
        [is_host, near_high, near_image] + messages + partial_sums,
        [SMEM] + [VMEM] * (2 + 2 * inner),
        scratch=[
            pltpu.VMEM((len(pairs_of(inner)) - held, rows, rows), BF16),
            pltpu.VMEM((inner, nrhs, rows), F32),
        ],
        flops=MAIN_FLOPS,
    )
    sums = sum(from_host([results[0]] * inner))
    parts = from_host(results[1:])
    leaf_sums = [sums] + [over_leaf(sums, m) for m in range(1, leaves)]
    result, residual = call(
        functools.partial(finish_kernel, leaves, inner, shape),
        [((nrhs, rows), F32)] * 2,
        [field, message] + leaf_sums + parts,
        [VMEM] * (2 + leaves + inner),
    )
    return (result.T, residual.T)


def on_device(embed, factors, targets):
    if embed.shape[0] * lax.axis_size("inner") <= FAST_LEAF:
        return collected(embed, factors, targets)
    return stepwise(embed, factors, targets)


def solution(mesh):
    return jax.shard_map(
        on_device,
        mesh=mesh,
        in_specs=(
            P(("groups", "leaf", "inner"), None),
            P(None, ("groups", "leaf", "inner"), None),
            P(("groups", "leaf", "inner"), None),
        ),
        out_specs=(P(("groups", "leaf", "inner"), None), P(("groups", "leaf", "inner"), None)),
        check_vma=False,
    )
```

time: 56 us -> 45.6 us (0.81)
  starting transfers between devices: 26.2 us -> 20.5 us
  Pallas kernels: 14.3 us -> 10.4 us
  waiting for transfers between devices: 11.4 us -> 10.7 us
    ppermute x9 -> x6, starting transfers between devices: 16.3 us -> 8 us  [to_host(): lax.ppermute(value, ('leaf', 'inner'), route)]
    pallas_call x5 -> x4, Pallas kernels: 14.3 us -> 10.4 us  [call(): pl.pallas_call(kernel, out_shape=[jax.ShapeDtypeStruct(shape, dtype) for...]
    ppermute x6, starting transfers between devices: 4.63 us -> 7.26 us  [over_leaf(): return lax.ppermute(value, 'leaf', [(i, i ^ m) for i in range(leaves)])]
    ppermute x9 -> x6, waiting for transfers between devices: 0.02 us -> 1.27 us  [to_host(): lax.ppermute(value, ('leaf', 'inner'), route)]
    ppermute x6, waiting for transfers between devices: 6.23 us -> 5.15 us  [over_leaf(): return lax.ppermute(value, 'leaf', [(i, i ^ m) for i in range(leaves)])]
    ppermute x6, waiting for transfers between devices: 5.12 us -> 4.31 us  [from_host(): lax.ppermute(value, ('leaf', 'inner'), [(b, a) for a, b in route])]
    unnamed x10 -> x6, local copies, waits for them, and re-layouts: 2.69 us -> 2.68 us
  transfers between devices with their start and end apart: 21 -> 18, of which waited for: 6 -> 7; matrix products, arithmetic and copies ran while one was open for 0% -> 0% of each run, Pallas kernels for 16% -> 9%
where the time goes in v2:
time: 45.6 us; the launch traced here: 45.2 us
  starting transfers between devices  20.5 us (45%)
  waiting for transfers between devices  10.7 us (23%)
  Pallas kernels  10.4 us (23%)
  local copies, waits for them, and re-layouts  2.69 us (6%)
  between operations  0.86 us (2%)
    pallas_call x4, Pallas kernels, call(): pl.pallas_call(kernel, out_shape=[jax.ShapeDtypeStruct(shape, dtype) for...  10.4 us
    ppermute x6, starting transfers between devices, to_host(): lax.ppermute(value, ('leaf', 'inner'), route)  8 us
    ppermute x6, starting transfers between devices, over_leaf(): return lax.ppermute(value, 'leaf', [(i, i ^ m) for i in range(leaves)])  7.26 us
    ppermute x6, starting transfers between devices, from_host(): lax.ppermute(value, ('leaf', 'inner'), [(b, a) for a, b in route])  5.23 us
    ppermute x6, waiting for transfers between devices, over_leaf(): return lax.ppermute(value, 'leaf', [(i, i ^ m) for i in range(leaves)])  5.15 us
    ppermute x6, waiting for transfers between devices, from_host(): lax.ppermute(value, ('leaf', 'inner'), [(b, a) for a, b in route])  4.31 us
    unnamed x6, local copies, waits for them, and re-layouts  2.68 us
    ppermute x6, waiting for transfers between devices, to_host(): lax.ppermute(value, ('leaf', 'inner'), route)  1.27 us
  transfers between devices with their start and end apart: 18, of which 7 were waited for; matrix products, arithmetic and copies ran while one was open for 0% of the time, Pallas kernels for 9%

profile of v2, /device:TPU:0, one launch (start us, length us, event | category | flops | bytes accessed | tf_op | source)
XLA Modules:
  0.0 45.2 jit_solution(8805454957398490073)
XLA Ops:
  0.6 1.0 %copy-done = bf16[3,384,128]{2,1,0:T(8,128)(2,1)S(1)} copy-done((bf16[3,384,128]{2,1,0:T(8,128)(2,1)S(1)}, bf16[3,384,128]{2,1,0:T(8,128)(2,1)}, u32[]{:S(2)}) %copy-start) | copy-done | bytes 294936
  1.6 0.9 %copy-done.1 = bf16[384,256]{1,0:T(8,128)(2,1)S(1)} copy-done((bf16[384,256]{1,0:T(8,128)(2,1)S(1)}, bf16[384,256]{1,0:T(8,128)(2,1)}, u32[]{:S(2)}) %copy-start.1) | copy-done | bytes 196632
  2.5 0.8 %copy-done.2 = f32[384,32]{0,1:T(8,128)S(1)} copy-done((f32[384,32]{0,1:T(8,128)S(1)}, f32[384,32]{0,1:T(8,128)}, u32[]{:S(2)}) %copy-start.2) | copy-done | bytes 49176
  3.3 0.9 %shard_map.50 = (bf16[2112,128]{1,0:T(8,128)(2,1)S(1)}, f32[96,128]{1,0:T(8,128)S(1)}, f32[32,384]{1,0:T(8,128)S(1)}) custom-call(bf16[384,256]{1,0:T(8,128)(2,1)S(1)} %copy-done.1, bf16[3,384,128]{2,1,0:T(8,128)(2,1)S(1)} %copy-done, f32[32,384]{1,0:T(8,128)S(1)} %bitcast.4), custom_call_target="tpu_custom_call" | custom-call | bytes 540672 | tf_op jit(solution)/shard_map/pallas_call | solution.py:314
  4.3 0.7 %collective-permute-start.1 = (bf16[2112,128]{1,0:T(8,128)(2,1)S(1)}, bf16[2112,128]{1,0:T(8,128)(2,1)S(1)}, u32[]{:S(2)}, u32[]{:S(2)}) collective-permute-start(bf16[2112,128]{1,0:T(8,128)(2,1)S(1)} %get-tuple-element.15.refs_0_.message_ref), channel_id=1, source_target_pairs={{3,2},{4,5},{11,10},{12,13},{19,18},{20,21},{27,26},{28,29}} | collective-permute-start | bytes 1622024 | tf_op jit(solution)/shard_map/ppermute | solution.py:345
  5.0 0.7 %collective-permute-start = (bf16[2112,128]{1,0:T(8,128)(2,1)S(1)}, bf16[2112,128]{1,0:T(8,128)(2,1)S(1)}, u32[]{:S(2)}, u32[]{:S(2)}) collective-permute-start(bf16[2112,128]{1,0:T(8,128)(2,1)S(1)} %get-tuple-element.15.refs_0_.message_ref), channel_id=1, source_target_pairs={{1,2},{6,5},{9,10},{14,13},{17,18},{22,21},{25,26},{30,29}} | collective-permute-start | bytes 1622024 | tf_op jit(solution)/shard_map/ppermute | solution.py:345
  5.7 3.9 %collective-permute-start.3 = (f32[64,128]{1,0:T(8,128)S(1)}, f32[64,128]{1,0:T(8,128)S(1)}, u32[]{:S(2)}, u32[]{:S(2)}) collective-permute-start(f32[64,128]{1,0:T(8,128)S(1)} %slice.22), channel_id=1, source_target_pairs={{0,4},{4,0},{8,12},{12,8},{1,5},{5,1},{9,13},{13,9},{2,6},{6,2},{1... | collective-permute-start | bytes 98312 | tf_op jit(solution)/shard_map/ppermute | solution.py:355
  9.6 1.5 %collective-permute-start.4 = (f32[32,128]{1,0:T(8,128)S(1)}, f32[32,128]{1,0:T(8,128)S(1)}, u32[]{:S(2)}, u32[]{:S(2)}) collective-permute-start(f32[32,128]{1,0:T(8,128)S(1)} %get-tuple-element.29), channel_id=1, source_target_pairs={{0,8},{4,12},{8,0},{12,4},{1,9},{5,13},{9,1},{13,5},{2,10},{6,14},... | collective-permute-start | bytes 49160 | tf_op jit(solution)/shard_map/ppermute | solution.py:355
  11.1 2.2 %collective-permute-done.4 = f32[32,128]{1,0:T(8,128)S(1)} collective-permute-done((f32[32,128]{1,0:T(8,128)S(1)}, f32[32,128]{1,0:T(8,128)S(1)}, u32[]{:S(2)}, u32[]{:S(2)}) %collective-permute-start.4) | collective-permute-done | bytes 16416 | tf_op jit(solution)/shard_map/ppermute | solution.py:355
  13.3 4.0 %collective-permute-start.2 = (bf16[2112,128]{1,0:T(8,128)(2,1)S(1)}, bf16[2112,128]{1,0:T(8,128)(2,1)S(1)}, u32[]{:S(2)}, u32[]{:S(2)}) collective-permute-start(bf16[2112,128]{1,0:T(8,128)(2,1)S(1)} %get-tuple-element.15.refs_0_.message_ref), channel_id=1, source_target_pairs={{0,2},{7,5},{8,10},{15,13},{16,18},{23,21},{24,26},{31,29}} | collective-permute-start | bytes 1622024 | tf_op jit(solution)/shard_map/ppermute | solution.py:345
  17.4 1.3 %collective-permute-start.8 = (f32[96,128]{1,0:T(8,128)S(1)}, f32[96,128]{1,0:T(8,128)S(1)}, u32[]{:S(2)}, u32[]{:S(2)}) collective-permute-start(f32[96,128]{1,0:T(8,128)S(1)} %pad_maximum_fusion.refs_4_), channel_id=1, source_target_pairs={{0,2},{7,5},{8,10},{15,13},{16,18},{23,21},{24,26},{31,29}} | collective-permute-start | bytes 147464 | tf_op jit(solution)/shard_map/ppermute | solution.py:345
  18.7 0.7 %collective-permute-start.7 = (f32[96,128]{1,0:T(8,128)S(1)}, f32[96,128]{1,0:T(8,128)S(1)}, u32[]{:S(2)}, u32[]{:S(2)}) collective-permute-start(f32[96,128]{1,0:T(8,128)S(1)} %pad_maximum_fusion.refs_4_), channel_id=1, source_target_pairs={{3,2},{4,5},{11,10},{12,13},{19,18},{20,21},{27,26},{28,29}} | collective-permute-start | bytes 147464 | tf_op jit(solution)/shard_map/ppermute | solution.py:345
  19.3 0.0 collective-permute-done.1.refs_2_
  19.4 0.7 %collective-permute-start.6 = (f32[96,128]{1,0:T(8,128)S(1)}, f32[96,128]{1,0:T(8,128)S(1)}, u32[]{:S(2)}, u32[]{:S(2)}) collective-permute-start(f32[96,128]{1,0:T(8,128)S(1)} %pad_maximum_fusion.refs_4_), channel_id=1, source_target_pairs={{1,2},{6,5},{9,10},{14,13},{17,18},{22,21},{25,26},{30,29}} | collective-permute-start | bytes 147464 | tf_op jit(solution)/shard_map/ppermute | solution.py:345
  20.0 3.9 %shard_map.51 = (bf16[6,384,384]{2,1,0:T(8,128)(2,1)S(1)}, f32[3,32,384]{2,1,0:T(8,128)S(1)}) custom-call(bf16[2112,128]{1,0:T(8,128)(2,1)S(1)} %get-tuple-element.15.refs_0_.message_ref, bf16[2112,128]{1,0:T(8,128)(2,1)S(1)} %collective-permute-done.refs_1_, bf16[2112,128]{1,0:T(8,128)(2,1)S(1)} %collective-permute-done.1.refs_2_), custom_call_target="tpu_custom_call" | custom-call | flops 2000000000 | bytes 1622016 | tf_op jit(solution)/shard_map/pallas_call | solution.py:314
  24.0 1.3 %collective-permute-done.8.refs_7_ = f32[96,128]{1,0:T(8,128)S(1)} collective-permute-done((f32[96,128]{1,0:T(8,128)S(1)}, f32[96,128]{1,0:T(8,128)S(1)}, u32[]{:S(2)}, u32[]{:S(2)}) %collective-permute-start.8) | collective-permute-done | bytes 49184 | tf_op jit(solution)/shard_map/ppermute | solution.py:345
  25.2 4.7 %shard_map.52 = (bf16[32,512]{1,0:T(8,128)(2,1)S(1)}, f32[64,384]{1,0:T(8,128)S(1)}, f32[64,384]{1,0:T(8,128)S(1)}, f32[64,384]{1,0:T(8,128)S(1)}, f32[64,384]{1,0:T(8,128)S(1)}) custom-call(s32[1]{0:T(128)} %bitcast.1.is_host_ref, bf16[6,384,384]{2,1,0:T(8,128)(2,1)S(1)} %get-tuple-element.16.near_high_ref, ...), custom_call_target="tpu_custom_call" | custom-call | flops 4000000000 | bytes 4276228 | tf_op jit(solution)/shard_map/pallas_call | solution.py:314
  29.9 1.3 %collective-permute-start.11 = (bf16[32,512]{1,0:T(8,128)(2,1)S(1)}, bf16[32,512]{1,0:T(8,128)(2,1)S(1)}, u32[]{:S(2)}, u32[]{:S(2)}) collective-permute-start(bf16[32,512]{1,0:T(8,128)(2,1)S(1)} %get-tuple-element.19), channel_id=1, source_target_pairs={{2,0},{5,7},{10,8},{13,15},{18,16},{21,23},{26,24},{29,31}} | collective-permute-start | bytes 98312 | tf_op jit(solution)/shard_map/ppermute | solution.py:349
  31.2 0.7 %collective-permute-start.10 = (bf16[32,512]{1,0:T(8,128)(2,1)S(1)}, bf16[32,512]{1,0:T(8,128)(2,1)S(1)}, u32[]{:S(2)}, u32[]{:S(2)}) collective-permute-start(bf16[32,512]{1,0:T(8,128)(2,1)S(1)} %get-tuple-element.19), channel_id=1, source_target_pairs={{2,3},{5,4},{10,11},{13,12},{18,19},{21,20},{26,27},{29,28}} | collective-permute-start | bytes 98312 | tf_op jit(solution)/shard_map/ppermute | solution.py:349
  31.9 0.7 %collective-permute-start.9 = (bf16[32,512]{1,0:T(8,128)(2,1)S(1)}, bf16[32,512]{1,0:T(8,128)(2,1)S(1)}, u32[]{:S(2)}, u32[]{:S(2)}) collective-permute-start(bf16[32,512]{1,0:T(8,128)(2,1)S(1)} %get-tuple-element.19), channel_id=1, source_target_pairs={{2,1},{5,6},{10,9},{13,14},{18,17},{21,22},{26,25},{29,30}} | collective-permute-start | bytes 98312 | tf_op jit(solution)/shard_map/ppermute | solution.py:349
  32.6 0.7 %collective-permute-start.15 = (f32[64,384]{1,0:T(8,128)S(1)}, f32[64,384]{1,0:T(8,128)S(1)}, u32[]{:S(2)}, u32[]{:S(2)}) collective-permute-start(f32[64,384]{1,0:T(8,128)S(1)} %get-tuple-element.21), channel_id=1, source_target_pairs={{2,1},{5,6},{10,9},{13,14},{18,17},{21,22},{26,25},{29,30}} | collective-permute-start | bytes 294920 | tf_op jit(solution)/shard_map/ppermute | solution.py:349
  33.3 0.7 %collective-permute-start.16 = (f32[64,384]{1,0:T(8,128)S(1)}, f32[64,384]{1,0:T(8,128)S(1)}, u32[]{:S(2)}, u32[]{:S(2)}) collective-permute-start(f32[64,384]{1,0:T(8,128)S(1)} %get-tuple-element.22), channel_id=1, source_target_pairs={{2,3},{5,4},{10,11},{13,12},{18,19},{21,20},{26,27},{29,28}} | collective-permute-start | bytes 294920 | tf_op jit(solution)/shard_map/ppermute | solution.py:349
  33.9 3.0 %collective-permute-done.11 = bf16[32,512]{1,0:T(8,128)(2,1)S(1)} collective-permute-done((bf16[32,512]{1,0:T(8,128)(2,1)S(1)}, bf16[32,512]{1,0:T(8,128)(2,1)S(1)}, u32[]{:S(2)}, u32[]{:S(2)}) %collective-permute-start.11) | collective-permute-done | bytes 32800 | tf_op jit(solution)/shard_map/ppermute | solution.py:349
  37.0 1.3 %collective-permute-start.17 = (f32[64,384]{1,0:T(8,128)S(1)}, f32[64,384]{1,0:T(8,128)S(1)}, u32[]{:S(2)}, u32[]{:S(2)}) collective-permute-start(f32[64,384]{1,0:T(8,128)S(1)} %get-tuple-element.23), channel_id=1, source_target_pairs={{2,0},{5,7},{10,8},{13,15},{18,16},{21,23},{26,24},{29,31}} | collective-permute-start | bytes 294920 | tf_op jit(solution)/shard_map/ppermute | solution.py:349
  38.3 0.1 collective-permute-start.14
  38.4 1.7 %collective-permute-start.13 = (bf16[32,512]{1,0:T(8,128)(2,1)S(1)}, bf16[32,512]{1,0:T(8,128)(2,1)S(1)}, u32[]{:S(2)}, u32[]{:S(2)}) collective-permute-start(bf16[32,512]{1,0:T(8,128)(2,1)S(1)} %add_add_fusion.refs_0_), channel_id=1, source_target_pairs={{0,8},{4,12},{8,0},{12,4},{1,9},{5,13},{9,1},{13,5},{2,10},{6,14},... | collective-permute-start | bytes 98312 | tf_op jit(solution)/shard_map/ppermute | solution.py:355
  40.1 1.8 %collective-permute-done.14.refs_3_ = bf16[32,512]{1,0:T(8,128)(2,1)S(1)} collective-permute-done((bf16[32,512]{1,0:T(8,128)(2,1)S(1)}, bf16[32,512]{1,0:T(8,128)(2,1)S(1)}, u32[]{:S(2)}, u32[]{:S(2)}) %collective-permute-start.14) | collective-permute-done | bytes 32800 | tf_op jit(solution)/shard_map/ppermute | solution.py:355
  41.9 0.1 collective-permute-start.12
  42.0 0.4 collective-permute-done.13.refs_2_
  42.4 0.7 %collective-permute-done.12.refs_1_ = bf16[32,512]{1,0:T(8,128)(2,1)S(1)} collective-permute-done((bf16[32,512]{1,0:T(8,128)(2,1)S(1)}, bf16[32,512]{1,0:T(8,128)(2,1)S(1)}, u32[]{:S(2)}, u32[]{:S(2)}) %collective-permute-start.12) | collective-permute-done | bytes 32800 | tf_op jit(solution)/shard_map/ppermute | solution.py:355
  43.1 1.3 %collective-permute-done.17.refs_7_ = f32[64,384]{1,0:T(8,128)S(1)} collective-permute-done((f32[64,384]{1,0:T(8,128)S(1)}, f32[64,384]{1,0:T(8,128)S(1)}, u32[]{:S(2)}, u32[]{:S(2)}) %collective-permute-start.17) | collective-permute-done | bytes 98336 | tf_op jit(solution)/shard_map/ppermute | solution.py:349
  44.4 0.8 %shard_map.53 = (f32[32,384]{1,0:T(8,128)}, f32[32,384]{1,0:T(8,128)}) custom-call(f32[32,384]{1,0:T(8,128)S(1)} %get-tuple-element.14.field_ref, bf16[2112,128]{1,0:T(8,128)(2,1)S(1)} %get-tuple-element.15.refs_0_.message_ref, bf16[32,512]{1,0:T(8,128)(2,1)S(1)} %add_add_fusion.refs_0_, bf16[32,512]{1,0:T(8,128)(2,1)S(1)} %collective-permute-done.12.refs_1_, ...), custom_call_target="tpu_custom_call" | custom-call | bytes 1114112 | tf_op jit(solution)/shard_map/pallas_call | solution.py:314
  (19 shorter events, 0.1 us)
Async XLA Ops:
  0.6 1.0 %copy-start = (bf16[3,384,128]{2,1,0:T(8,128)(2,1)S(1)}, bf16[3,384,128]{2,1,0:T(8,128)(2,1)}, u32[]{:S(2)}) copy-start(bf16[3,384,128]{2,1,0:T(8,128)(2,1)} %factors_hbm.1) | copy-start | bytes 884740
  1.6 0.9 %copy-start.1 = (bf16[384,256]{1,0:T(8,128)(2,1)S(1)}, bf16[384,256]{1,0:T(8,128)(2,1)}, u32[]{:S(2)}) copy-start(bf16[384,256]{1,0:T(8,128)(2,1)} %embed_hbm.1) | copy-start | bytes 589828
  2.5 0.8 %copy-start.2 = (f32[384,32]{0,1:T(8,128)S(1)}, f32[384,32]{0,1:T(8,128)}, u32[]{:S(2)}) copy-start(f32[384,32]{0,1:T(8,128)} %param.5) | copy-start | bytes 147460
  4.3 15.1 %collective-permute-start.1 = (bf16[2112,128]{1,0:T(8,128)(2,1)S(1)}, bf16[2112,128]{1,0:T(8,128)(2,1)S(1)}, u32[]{:S(2)}, u32[]{:S(2)}) collective-permute-start(bf16[2112,128]{1,0:T(8,128)(2,1)S(1)} %get-tuple-element.15.refs_0_.message_ref), channel_id=1, source_target_pairs={{3,2},{4,5},{11,10},{12,13},{19,18},{20,21},{27,26},{28,29}} | collective-permute-start | bytes 1622024 | tf_op jit(solution)/shard_map/ppermute | solution.py:345
  5.0 15.1 %collective-permute-start = (bf16[2112,128]{1,0:T(8,128)(2,1)S(1)}, bf16[2112,128]{1,0:T(8,128)(2,1)S(1)}, u32[]{:S(2)}, u32[]{:S(2)}) collective-permute-start(bf16[2112,128]{1,0:T(8,128)(2,1)S(1)} %get-tuple-element.15.refs_0_.message_ref), channel_id=1, source_target_pairs={{1,2},{6,5},{9,10},{14,13},{17,18},{22,21},{25,26},{30,29}} | collective-permute-start | bytes 1622024 | tf_op jit(solution)/shard_map/ppermute | solution.py:345
  5.7 11.7 %collective-permute-start.3 = (f32[64,128]{1,0:T(8,128)S(1)}, f32[64,128]{1,0:T(8,128)S(1)}, u32[]{:S(2)}, u32[]{:S(2)}) collective-permute-start(f32[64,128]{1,0:T(8,128)S(1)} %slice.22), channel_id=1, source_target_pairs={{0,4},{4,0},{8,12},{12,8},{1,5},{5,1},{9,13},{13,9},{2,6},{6,2},{1... | collective-permute-start | bytes 98312 | tf_op jit(solution)/shard_map/ppermute | solution.py:355
  9.6 3.7 %collective-permute-start.4 = (f32[32,128]{1,0:T(8,128)S(1)}, f32[32,128]{1,0:T(8,128)S(1)}, u32[]{:S(2)}, u32[]{:S(2)}) collective-permute-start(f32[32,128]{1,0:T(8,128)S(1)} %get-tuple-element.29), channel_id=1, source_target_pairs={{0,8},{4,12},{8,0},{12,4},{1,9},{5,13},{9,1},{13,5},{2,10},{6,14},... | collective-permute-start | bytes 49160 | tf_op jit(solution)/shard_map/ppermute | solution.py:355
  11.1 6.3 %collective-permute-start.5 = (f32[32,128]{1,0:T(8,128)S(1)}, f32[32,128]{1,0:T(8,128)S(1)}, u32[]{:S(2)}, u32[]{:S(2)}) collective-permute-start(f32[32,128]{1,0:T(8,128)S(1)} %get-tuple-element.29), channel_id=1, source_target_pairs={{0,12},{4,8},{8,4},{12,0},{1,13},{5,9},{9,5},{13,1},{2,14},{6,10},... | collective-permute-start | bytes 49160 | tf_op jit(solution)/shard_map/ppermute | solution.py:355
  13.3 11.9 %collective-permute-start.2 = (bf16[2112,128]{1,0:T(8,128)(2,1)S(1)}, bf16[2112,128]{1,0:T(8,128)(2,1)S(1)}, u32[]{:S(2)}, u32[]{:S(2)}) collective-permute-start(bf16[2112,128]{1,0:T(8,128)(2,1)S(1)} %get-tuple-element.15.refs_0_.message_ref), channel_id=1, source_target_pairs={{0,2},{7,5},{8,10},{15,13},{16,18},{23,21},{24,26},{31,29}} | collective-permute-start | bytes 1622024 | tf_op jit(solution)/shard_map/ppermute | solution.py:345
  17.4 7.8 %collective-permute-start.8 = (f32[96,128]{1,0:T(8,128)S(1)}, f32[96,128]{1,0:T(8,128)S(1)}, u32[]{:S(2)}, u32[]{:S(2)}) collective-permute-start(f32[96,128]{1,0:T(8,128)S(1)} %pad_maximum_fusion.refs_4_), channel_id=1, source_target_pairs={{0,2},{7,5},{8,10},{15,13},{16,18},{23,21},{24,26},{31,29}} | collective-permute-start | bytes 147464 | tf_op jit(solution)/shard_map/ppermute | solution.py:345
  18.7 6.6 %collective-permute-start.7 = (f32[96,128]{1,0:T(8,128)S(1)}, f32[96,128]{1,0:T(8,128)S(1)}, u32[]{:S(2)}, u32[]{:S(2)}) collective-permute-start(f32[96,128]{1,0:T(8,128)S(1)} %pad_maximum_fusion.refs_4_), channel_id=1, source_target_pairs={{3,2},{4,5},{11,10},{12,13},{19,18},{20,21},{27,26},{28,29}} | collective-permute-start | bytes 147464 | tf_op jit(solution)/shard_map/ppermute | solution.py:345
  19.4 5.9 %collective-permute-start.6 = (f32[96,128]{1,0:T(8,128)S(1)}, f32[96,128]{1,0:T(8,128)S(1)}, u32[]{:S(2)}, u32[]{:S(2)}) collective-permute-start(f32[96,128]{1,0:T(8,128)S(1)} %pad_maximum_fusion.refs_4_), channel_id=1, source_target_pairs={{1,2},{6,5},{9,10},{14,13},{17,18},{22,21},{25,26},{30,29}} | collective-permute-start | bytes 147464 | tf_op jit(solution)/shard_map/ppermute | solution.py:345
  29.9 7.0 %collective-permute-start.11 = (bf16[32,512]{1,0:T(8,128)(2,1)S(1)}, bf16[32,512]{1,0:T(8,128)(2,1)S(1)}, u32[]{:S(2)}, u32[]{:S(2)}) collective-permute-start(bf16[32,512]{1,0:T(8,128)(2,1)S(1)} %get-tuple-element.19), channel_id=1, source_target_pairs={{2,0},{5,7},{10,8},{13,15},{18,16},{21,23},{26,24},{29,31}} | collective-permute-start | bytes 98312 | tf_op jit(solution)/shard_map/ppermute | solution.py:349
  31.2 7.0 %collective-permute-start.10 = (bf16[32,512]{1,0:T(8,128)(2,1)S(1)}, bf16[32,512]{1,0:T(8,128)(2,1)S(1)}, u32[]{:S(2)}, u32[]{:S(2)}) collective-permute-start(bf16[32,512]{1,0:T(8,128)(2,1)S(1)} %get-tuple-element.19), channel_id=1, source_target_pairs={{2,3},{5,4},{10,11},{13,12},{18,19},{21,20},{26,27},{29,28}} | collective-permute-start | bytes 98312 | tf_op jit(solution)/shard_map/ppermute | solution.py:349
  31.9 6.3 %collective-permute-start.9 = (bf16[32,512]{1,0:T(8,128)(2,1)S(1)}, bf16[32,512]{1,0:T(8,128)(2,1)S(1)}, u32[]{:S(2)}, u32[]{:S(2)}) collective-permute-start(bf16[32,512]{1,0:T(8,128)(2,1)S(1)} %get-tuple-element.19), channel_id=1, source_target_pairs={{2,1},{5,6},{10,9},{13,14},{18,17},{21,22},{26,25},{29,30}} | collective-permute-start | bytes 98312 | tf_op jit(solution)/shard_map/ppermute | solution.py:349
  32.6 10.5 %collective-permute-start.15 = (f32[64,384]{1,0:T(8,128)S(1)}, f32[64,384]{1,0:T(8,128)S(1)}, u32[]{:S(2)}, u32[]{:S(2)}) collective-permute-start(f32[64,384]{1,0:T(8,128)S(1)} %get-tuple-element.21), channel_id=1, source_target_pairs={{2,1},{5,6},{10,9},{13,14},{18,17},{21,22},{26,25},{29,30}} | collective-permute-start | bytes 294920 | tf_op jit(solution)/shard_map/ppermute | solution.py:349
  33.3 9.8 %collective-permute-start.16 = (f32[64,384]{1,0:T(8,128)S(1)}, f32[64,384]{1,0:T(8,128)S(1)}, u32[]{:S(2)}, u32[]{:S(2)}) collective-permute-start(f32[64,384]{1,0:T(8,128)S(1)} %get-tuple-element.22), channel_id=1, source_target_pairs={{2,3},{5,4},{10,11},{13,12},{18,19},{21,20},{26,27},{29,28}} | collective-permute-start | bytes 294920 | tf_op jit(solution)/shard_map/ppermute | solution.py:349
  37.0 7.4 %collective-permute-start.17 = (f32[64,384]{1,0:T(8,128)S(1)}, f32[64,384]{1,0:T(8,128)S(1)}, u32[]{:S(2)}, u32[]{:S(2)}) collective-permute-start(f32[64,384]{1,0:T(8,128)S(1)} %get-tuple-element.23), channel_id=1, source_target_pairs={{2,0},{5,7},{10,8},{13,15},{18,16},{21,23},{26,24},{29,31}} | collective-permute-start | bytes 294920 | tf_op jit(solution)/shard_map/ppermute | solution.py:349
  38.3 3.6 %collective-permute-start.14 = (bf16[32,512]{1,0:T(8,128)(2,1)S(1)}, bf16[32,512]{1,0:T(8,128)(2,1)S(1)}, u32[]{:S(2)}, u32[]{:S(2)}) collective-permute-start(bf16[32,512]{1,0:T(8,128)(2,1)S(1)} %add_add_fusion.refs_0_), channel_id=1, source_target_pairs={{0,12},{4,8},{8,4},{12,0},{1,13},{5,9},{9,5},{13,1},{2,14},{6,10},... | collective-permute-start | bytes 98312 | tf_op jit(solution)/shard_map/ppermute | solution.py:355
  38.4 4.0 %collective-permute-start.13 = (bf16[32,512]{1,0:T(8,128)(2,1)S(1)}, bf16[32,512]{1,0:T(8,128)(2,1)S(1)}, u32[]{:S(2)}, u32[]{:S(2)}) collective-permute-start(bf16[32,512]{1,0:T(8,128)(2,1)S(1)} %add_add_fusion.refs_0_), channel_id=1, source_target_pairs={{0,8},{4,12},{8,0},{12,4},{1,9},{5,13},{9,1},{13,5},{2,10},{6,14},... | collective-permute-start | bytes 98312 | tf_op jit(solution)/shard_map/ppermute | solution.py:355
  41.9 1.2 %collective-permute-start.12 = (bf16[32,512]{1,0:T(8,128)(2,1)S(1)}, bf16[32,512]{1,0:T(8,128)(2,1)S(1)}, u32[]{:S(2)}, u32[]{:S(2)}) collective-permute-start(bf16[32,512]{1,0:T(8,128)(2,1)S(1)} %add_add_fusion.refs_0_), channel_id=1, source_target_pairs={{0,4},{4,0},{8,12},{12,8},{1,5},{5,1},{9,13},{13,9},{2,6},{6,2},{1... | collective-permute-start | bytes 98312 | tf_op jit(solution)/shard_map/ppermute | solution.py:355

commit v3 on v2

v3 whole, which is shorter than its diff:
```python
import functools

import jax
import jax.numpy as jnp
from jax import lax
from jax.experimental import pallas as pl
from jax.experimental.pallas import tpu as pltpu
from jax.sharding import PartitionSpec as P

ITERS = 2
LENGTH_SCALE = 2.3
FAST_LEAF = 2048
NEAR_FLOPS = 4 * 10**9
FAR_FLOPS = 3 * 10**9
MAIN_FLOPS = 2 * 10**9
F32, BF16 = jnp.float32, jnp.bfloat16
VMEM = pl.BlockSpec(memory_space=pltpu.VMEM)
SMEM = pl.BlockSpec(memory_space=pltpu.SMEM)


def swapped(value, axis, apart):
    mask = 2**apart
    pairs = [(source, source ^ mask) for source in range(lax.axis_size(axis))]
    return lax.ppermute(value, axis, pairs)


def matern(left, right):
    left_f = left.astype(F32)
    right_f = right.astype(F32)
    left_sq = jnp.sum(left_f * left_f, axis=1)
    right_sq = jnp.sum(right_f * right_f, axis=1)
    inner_prod = lax.dot_general(
        left, right, (((1,), (1,)), ((), ())), preferred_element_type=F32
    )
    dist2 = left_sq[:, None] + right_sq[None, :] - 2.0 * inner_prod
    scaled = jnp.sqrt(3.0) * jnp.sqrt(jnp.maximum(dist2, 0.0)) / LENGTH_SCALE
    return (1.0 + scaled) * jnp.exp(-scaled)


def squares(residual):
    return lax.psum(jnp.sum(residual * residual, axis=0), ("leaf", "inner"))


def operate(embed, factors, field):
    piece = lax.all_gather(embed, "inner", axis=0, tiled=True)
    terms = jnp.dot(matern(piece, embed), field, precision=lax.Precision.HIGHEST)
    dense = lax.psum_scatter(terms, "inner", scatter_dimension=0, tiled=True)
    total = dense + 0.5 * field
    levels = factors.shape[0]
    rounded = field.astype(BF16)
    proj = jnp.einsum("lrk,rc->lkc", factors, rounded, preferred_element_type=F32)
    proj = lax.psum(proj, "inner")
    for bit in range(levels - 1):
        upper = proj[bit + 1 :]
        partner = swapped(upper, "leaf", bit)
        proj = jnp.concatenate([proj[: bit + 1], upper + partner], axis=0)
    back = jnp.einsum(
        "lrk,lkc->rc", factors, proj.astype(BF16), preferred_element_type=F32
    )
    return total + back


def stepwise(embed, factors, targets):
    result = jnp.zeros_like(targets)
    residual = targets
    direction = targets
    norm_now = squares(residual)
    for step in range(ITERS):
        image = operate(embed, factors, direction)
        curv = lax.psum(jnp.sum(direction * image, axis=0), ("leaf", "inner"))
        alpha = norm_now / curv
        result = result + alpha * direction
        residual = residual - alpha * image
        if step + 1 < ITERS:
            norm_next = squares(residual)
            direction = residual + norm_next / norm_now * direction
            norm_now = norm_next
    return (result, residual)


def mm(left, right):
    return lax.dot_general(left, right, (((1,), (0,)), ((), ())), preferred_element_type=F32)


def mm_nt(left, right):
    return lax.dot_general(left, right, (((1,), (1,)), ((), ())), preferred_element_type=F32)


def pairs_of(slots):
    return [(i, j) for j in range(slots) for i in range(j + 1)]


def project_kernel(factors_ref, field_ref, first_ref, upper_ref):
    levels = factors_ref.shape[0]
    nrhs = field_ref.shape[0]
    rounded = field_ref[...].astype(BF16)
    first_ref[...] = mm(rounded, factors_ref[0])
    for level in range(1, levels):
        upper_ref[(level - 1) * nrhs : level * nrhs] = mm(rounded, factors_ref[level])


def pack_kernel(embed_hbm, factors_hbm, field_hbm, message_ref, field_ref, sems):
    levels, rows, rank = factors_hbm.shape
    nrhs = field_ref.shape[0]
    lanes = embed_hbm.shape[1] // rank
    head = lanes * rows + 2 * nrhs * (rows // rank)
    copies = [pltpu.make_async_copy(field_hbm, field_ref, sems.at[0])]
    for k in range(lanes):
        piece = embed_hbm.at[:, pl.ds(k * rank, rank)]
        place = message_ref.at[pl.ds(k * rows, rows)]
        copies.append(pltpu.make_async_copy(piece, place, sems.at[len(copies)]))
    for level in range(levels):
        place = message_ref.at[pl.ds(head + level * rows, rows)]
        copies.append(pltpu.make_async_copy(factors_hbm.at[level], place, sems.at[len(copies)]))
    for copy in copies:
        copy.start()
    copies[0].wait()
    for k in range(rows // rank):
        start = lanes * rows + 2 * k * nrhs
        value = field_ref[:, k * rank : (k + 1) * rank]
        high = value.astype(BF16)
        message_ref[start : start + nrhs] = high
        message_ref[start + nrhs : start + 2 * nrhs] = (value - high.astype(F32)).astype(BF16)
    for copy in copies[1:]:
        copy.wait()


class Message:
    def __init__(self, shape, ref):
        self.rows, self.dims, self.levels, self.rank, self.nrhs = shape
        self.ref = ref

    def embed(self):
        rows = self.rows
        pieces = [self.ref[k * rows : (k + 1) * rows] for k in range(self.dims // self.rank)]
        return jnp.concatenate(pieces, axis=1)

    def field(self):
        base = self.dims // self.rank * self.rows
        step = 2 * self.nrhs
        count = self.rows // self.rank
        pieces = [self.ref[base + k * step : base + (k + 1) * step] for k in range(count)]
        return jnp.concatenate(pieces, axis=1)

    def factor(self, level):
        base = self.dims // self.rank * self.rows + 2 * self.nrhs * (self.rows // self.rank)
        return self.ref[base + level * self.rows : base + (level + 1) * self.rows]

    def project(self, field):
        return jnp.concatenate([mm(field, self.factor(l)) for l in range(self.levels)], axis=0)


def norms_of(embed):
    scale = 3.0 / LENGTH_SCALE**2
    wide_e = embed.astype(F32)
    square = wide_e * wide_e
    column = scale * jnp.sum(square, axis=1, keepdims=True)
    first = square.astype(BF16)
    rest = (square - first.astype(F32)).astype(BF16)
    ones = jnp.ones((8, embed.shape[1]), BF16)
    row = scale * (mm_nt(ones, first) + mm_nt(ones, rest))
    return column, row[0:1]


def kern_block(left, right, column, row):
    scale = 3.0 / LENGTH_SCALE**2
    product = mm_nt(left, right)
    dist = jnp.maximum((column + row) - (2.0 * scale) * product, 1e-30)
    scaled = dist * lax.rsqrt(dist)
    value = (1.0 + scaled) * jnp.exp(-scaled)
    high = value.astype(BF16)
    return high, (value - high.astype(F32)).astype(BF16)


def kern_columns(columns, messages, high_ref, low_ref):
    norms = {}
    index = 0
    for j in columns:
        for i in range(j + 1):
            for s in (i, j):
                if s not in norms:
                    norms[s] = norms_of(messages[s].embed())
            high_ref[index], low_ref[index] = kern_block(
                messages[i].embed(), messages[j].embed(), norms[i][0], norms[j][1]
            )
            index += 1


def add_products(columns, high_ref, low_ref, fields, total):
    nrhs, rows = total[0].shape

    def fold(stacked):
        return stacked[:nrhs] + stacked[nrhs:] if stacked.shape[0] > nrhs else stacked

    at = 0
    for j in columns:
        left = jnp.concatenate(fields[: j + 1], axis=1)
        high = high_ref[at : at + j + 1].reshape((j + 1) * rows, rows)
        down = fold(mm(left, high))
        across = fold(mm_nt(fields[j], high[: j * rows])) if j else None
        if low_ref is not None:
            low = low_ref[at : at + j + 1].reshape((j + 1) * rows, rows)
            down = down + mm(left[:nrhs], low)
            if j:
                across = across + mm_nt(fields[j][:nrhs], low[: j * rows])
        total[j] = total[j] + down
        for i in range(j):
            total[i] = total[i] + across[:, i * rows : (i + 1) * rows]
        at += j + 1


def near_kernel(near, shape, *refs):
    high_ref, image_ref, low_ref = refs[near:]
    messages = [Message(shape, ref) for ref in refs[:near]]
    image = [jnp.zeros(image_ref.shape[1:], F32) for _ in range(near)]
    kern_columns(range(near), messages, high_ref, low_ref)
    add_products(range(near), high_ref, low_ref, [m.field() for m in messages], image)
    for s in range(near):
        image_ref[s] = image[s]


def far_kernel(slots, shape, near_image_ref, *refs):
    high_ref, image_ref, low_ref = refs[slots:]
    near = near_image_ref.shape[0]
    messages = [Message(shape, ref) for ref in refs[:slots]]
    image = [near_image_ref[s] for s in range(near)]
    image += [jnp.zeros(image_ref.shape[1:], F32) for _ in range(near, slots)]
    kern_columns(range(near, slots), messages, high_ref, low_ref)
    add_products(range(near, slots), high_ref, low_ref, [m.field() for m in messages], image)
    for s in range(slots):
        image_ref[s] = image[s]


def main_kernel(slots, shape, is_host_ref, near_high_ref, far_high_ref, image_ref, *refs):
    messages = [Message(shape, ref) for ref in refs[:slots]]
    proj_refs = refs[slots : 2 * slots]
    results = refs[2 * slots :]
    rows, _, levels, rank, nrhs = shape
    near = len(proj_refs) - 1
    mine = is_host_ref[0] == 1

    def put(s, at, value):
        value = jnp.where(mine, value, jnp.zeros_like(value)) if s == 0 else value
        results[s][at * nrhs : (at + 1) * nrhs] = value

    def put_halves(s, at, value):
        high = value.astype(BF16)
        low = (value - high.astype(F32)).astype(BF16)
        for k in range(rows // rank):
            put(s, at + 2 * k, high[:, k * rank : (k + 1) * rank])
            put(s, at + 2 * k + 1, low[:, k * rank : (k + 1) * rank])

    proj = []
    for level in range(levels):
        total = proj_refs[0][level * nrhs : (level + 1) * nrhs]
        for ref in proj_refs[1:]:
            total = total + ref[level * nrhs : (level + 1) * nrhs]
        proj.append(total.astype(BF16))
    fields = [message.field() for message in messages]
    field, image, image_b = [], [], []
    for s in range(slots):
        halves = fields[s].astype(F32)
        field.append(halves[:nrhs] + halves[nrhs:])
        total = image_ref[s] + 0.5 * field[s]
        for level in range(levels):
            total = total + mm_nt(proj[level], messages[s].factor(level))
        image.append(total)
        image_b.append(total.astype(BF16))
        put_halves(s, levels + 1, total)
    total = messages[0].project(image_b[0])
    for s in range(1, slots):
        total = total + messages[s].project(image_b[s])
    leaf_norm = jnp.sum(total[:nrhs] * total[:nrhs], axis=1, keepdims=True)
    for level in range(levels):
        part = total[level * nrhs : (level + 1) * nrhs].astype(BF16)
        for s in range(slots):
            put(s, level, part)
    second = [jnp.zeros((nrhs, rows), F32) for _ in range(slots)]
    add_products(range(near), near_high_ref, None, image_b, second)
    add_products(range(near, slots), far_high_ref, None, image_b, second)
    for s in range(slots):
        put_halves(s, levels + 1 + 2 * (rows // rank), second[s])

    def dots(left, right):
        total = left[0] * right[0]
        for s in range(1, slots):
            total = total + left[s] * right[s]
        return jnp.sum(total, axis=1, keepdims=True)

    scalars = [
        dots(field, field),
        dots(field, image),
        dots(image, image),
        dots(image, second) + leaf_norm,
    ]
    lane = lax.broadcasted_iota(jnp.int32, (nrhs, rank), 1)
    packed = jnp.zeros((nrhs, rank), F32)
    for k, value in enumerate(scalars):
        value = jnp.broadcast_to(value, (nrhs, rank))
        for piece in range(3):
            rounded = value.astype(BF16).astype(F32)
            packed = jnp.where(lane == 3 * k + piece, rounded, packed)
            value = value - rounded
    for s in range(slots):
        put(s, levels, packed.astype(BF16))


def finish_kernel(leaves, field_ref, factors_ref, result_ref, *refs):
    sums = refs[:leaves]
    solution_ref, residual_ref = refs[leaves:]
    levels, rows, rank = factors_ref.shape
    nrhs = field_ref.shape[0]
    field = field_ref[...]

    def halves(at):
        pieces = []
        for k in range(rows // rank):
            start = (at + 2 * k) * nrhs
            piece = result_ref[start : start + 2 * nrhs].astype(F32)
            pieces.append(piece[:nrhs] + piece[nrhs:])
        return jnp.concatenate(pieces, axis=1)

    image = halves(levels + 1)
    second = halves(levels + 1 + 2 * (rows // rank)) + 0.5 * image
    lane = lax.broadcasted_iota(jnp.int32, (nrhs, rank), 1)
    packed = sums[0][levels * nrhs :].astype(F32)
    for m in range(1, leaves):
        packed = packed + sums[m][levels * nrhs :].astype(F32)

    def scalar(k):
        inside = (lane >= 3 * k) & (lane < 3 * k + 3)
        return jnp.sum(jnp.where(inside, packed, 0.0), axis=1, keepdims=True)

    bb, bw, ww, wu = (scalar(k) for k in range(4))
    wu = wu + 0.5 * ww
    for level in range(levels):
        nodes = {}
        for m in range(leaves):
            value = sums[m][level * nrhs : (level + 1) * nrhs].astype(F32)
            node = m >> level
            nodes[node] = nodes[node] + value if node in nodes else value
        second = second + mm_nt(nodes[0].astype(BF16), factors_ref[level])
        if level > 0:
            squared = sum(value * value for value in nodes.values())
            wu = wu + jnp.sum(squared, axis=1, keepdims=True)
    alpha0 = bb / bw
    norm1 = alpha0 * alpha0 * ww - bb
    ratio = norm1 / bb
    keep = 1.0 + ratio
    curv = keep * keep * bw - 2.0 * keep * alpha0 * ww + alpha0 * alpha0 * wu
    alpha1 = norm1 / curv
    solution_ref[...] = (alpha0 + alpha1 * keep) * field - (alpha1 * alpha0) * image
    residual_ref[...] = field - (alpha0 + alpha1 * keep) * image + (alpha1 * alpha0) * second


def call(kernel, outs, args, specs, scratch=(), flops=0, limit=24):
    moved = sum(a.size * a.dtype.itemsize for a in args)
    return pl.pallas_call(
        kernel,
        out_shape=[jax.ShapeDtypeStruct(shape, dtype) for shape, dtype in outs],
        in_specs=specs,
        out_specs=[VMEM] * len(outs),
        scratch_shapes=list(scratch),
        cost_estimate=pl.CostEstimate(flops=flops, bytes_accessed=moved, transcendentals=0),
        compiler_params=pltpu.CompilerParams(vmem_limit_bytes=limit * 2**20),
    )(*args)


def collected(embed, factors, targets):
    leaves, inner = lax.axis_size("leaf"), lax.axis_size("inner")
    levels, rows, rank = factors.shape
    nrhs = targets.shape[1]
    dims = embed.shape[1]
    shape = (rows, dims, levels, rank, nrhs)

    def host(leaf):
        return inner // 2 if leaf % 2 == 0 else (inner - 1) // 2

    def others(leaf):
        sign = 1 if leaf % 2 == 0 else -1
        here = host(leaf)
        return sorted((z for z in range(inner) if z != here), key=lambda z: (abs(z - here), sign * z))

    routes = [
        [(leaf * inner + others(leaf)[k], leaf * inner + host(leaf)) for leaf in range(leaves)]
        for k in range(inner - 1)
    ]

    axes = ("leaf", "inner")

    def from_host(values):
        back = [
            lax.ppermute(value, axes, [(b, a) for a, b in route])
            for value, route in zip(values[1:], routes)
        ]
        return [values[0]] + back

    def to_host(value):
        return [value] + [lax.ppermute(value, axes, route) for route in routes]

    def over_leaf(value, m):
        return lax.ppermute(value, "leaf", [(i, i ^ m) for i in range(leaves)])

    field = targets.T
    height = dims // rank * rows + 2 * nrhs * (rows // rank) + levels * rows
    hbm = pl.BlockSpec(memory_space=pltpu.HBM)
    (message,) = call(
        pack_kernel,
        [((height, rank), BF16)],
        [embed, factors, field],
        [hbm] * 3,
        scratch=[
            pltpu.VMEM((nrhs, rows), F32),
            pltpu.SemaphoreType.DMA((1 + dims // rank + levels,)),
        ],
        limit=60,
    )
    messages = to_host(message)
    first, upper = call(
        project_kernel,
        [((nrhs, rank), F32), (((levels - 1) * nrhs, rank), F32)],
        [factors, field],
        [VMEM] * 2,
    )
    projs = [first]
    for bit in range(levels - 1):
        upper = upper + over_leaf(upper, 2**bit)
        projs.append(upper[:nrhs])
        upper = upper[nrhs:]
    projs = to_host(jnp.concatenate(projs, axis=0))
    near = inner - 1
    held, pairs = len(pairs_of(near)), len(pairs_of(inner))
    near_high, near_image = call(
        functools.partial(near_kernel, near, shape),
        [((held, rows, rows), BF16), ((near, nrhs, rows), F32)],
        messages[:near],
        [VMEM] * near,
        scratch=[pltpu.VMEM((held, rows, rows), BF16)],
        flops=NEAR_FLOPS,
    )
    far_high, image = call(
        functools.partial(far_kernel, inner, shape),
        [((pairs - held, rows, rows), BF16), ((inner, nrhs, rows), F32)],
        [near_image] + messages,
        [VMEM] * (1 + inner),
        scratch=[pltpu.VMEM((pairs - held, rows, rows), BF16)],
        flops=FAR_FLOPS,
    )
    leaf = lax.axis_index("leaf")
    here = jnp.where(leaf % 2 == 0, host(0), host(1))
    is_host = (lax.axis_index("inner") == here).astype(jnp.int32).reshape(1)
    height = (levels + 1 + 4 * (rows // rank)) * nrhs
    results = call(
        functools.partial(main_kernel, inner, shape),
        [((height, rank), BF16)] * inner,
        [is_host, near_high, far_high, image] + messages + projs,
        [SMEM] + [VMEM] * (3 + 2 * inner),
        flops=MAIN_FLOPS,
    )
    result = results[0]
    for value, route in reversed(list(zip(results[1:], routes))):
        result = result + lax.ppermute(value, axes, [(b, a) for a, b in route])
    sums = result[: (levels + 1) * nrhs]
    leaf_sums = [sums] + [over_leaf(sums, m) for m in range(1, leaves)]
    answer, residual = call(
        functools.partial(finish_kernel, leaves),
        [((nrhs, rows), F32)] * 2,
        [field, factors, result] + leaf_sums,
        [VMEM] * (3 + leaves),
    )
    return (answer.T, residual.T)


def on_device(embed, factors, targets):
    if embed.shape[0] * lax.axis_size("inner") <= FAST_LEAF:
        return collected(embed, factors, targets)
    return stepwise(embed, factors, targets)


def solution(mesh):
    return jax.shard_map(
        on_device,
        mesh=mesh,
        in_specs=(
            P(("groups", "leaf", "inner"), None),
            P(None, ("groups", "leaf", "inner"), None),
            P(("groups", "leaf", "inner"), None),
        ),
        out_specs=(P(("groups", "leaf", "inner"), None), P(("groups", "leaf", "inner"), None)),
        check_vma=False,
    )
```

time: 45.6 us -> 43.9 us (0.963)
  waiting for transfers between devices: 10.7 us -> 9.47 us
  starting transfers between devices: 20.5 us -> 19.8 us
    ppermute x12 -> x9, starting transfers between devices: 13.2 us -> 11.5 us  [the longest x6 8.88 us: to_host(): return [value] + [lax.ppermute(value, axes, route) for route in routes]]
    ppermute x6 -> x5, starting transfers between devices: 7.26 us -> 8.25 us  [over_leaf(): return lax.ppermute(value, 'leaf', [(i, i ^ m) for i in range(leaves)])]
    ppermute x6 -> x5, waiting for transfers between devices: 5.15 us -> 4.21 us  [over_leaf(): return lax.ppermute(value, 'leaf', [(i, i ^ m) for i in range(leaves)])]
    ppermute x12 -> x9, waiting for transfers between devices: 5.59 us -> 5.25 us  [the longest x3 5.22 us: collected(): result = result + lax.ppermute(value, axes, [(b, a) for a, b in route])]
    unnamed x6 -> x12, local copies, waits for them, and re-layouts: 2.68 us -> 2.81 us
    pallas_call x4 -> x6, Pallas kernels: 10.4 us -> 10.5 us  [call(): pl.pallas_call(kernel, out_shape=[jax.ShapeDtypeStruct(shape, dtype) for...]
  transfers between devices with their start and end apart: 18 -> 14, of which waited for: 7 -> 4; matrix products, arithmetic and copies ran while one was open for 0% -> 0% of each run, Pallas kernels for 9% -> 14%
where the time goes in v3:
time: 43.9 us; the launch traced here: 43.5 us
  starting transfers between devices  19.8 us (45%)
  Pallas kernels  10.5 us (24%)
  waiting for transfers between devices  9.47 us (22%)
  local copies, waits for them, and re-layouts  2.82 us (6%)
  between operations  0.86 us (2%)
    pallas_call x6, Pallas kernels, call(): pl.pallas_call(kernel, out_shape=[jax.ShapeDtypeStruct(shape, dtype) for...  10.5 us
    ppermute x6, starting transfers between devices, to_host(): return [value] + [lax.ppermute(value, axes, route) for route in routes]  8.88 us
    ppermute x5, starting transfers between devices, over_leaf(): return lax.ppermute(value, 'leaf', [(i, i ^ m) for i in range(leaves)])  8.25 us
    ppermute x3, waiting for transfers between devices, collected(): result = result + lax.ppermute(value, axes, [(b, a) for a, b in route])  5.22 us
    ppermute x5, waiting for transfers between devices, over_leaf(): return lax.ppermute(value, 'leaf', [(i, i ^ m) for i in range(leaves)])  4.21 us
    unnamed x12, local copies, waits for them, and re-layouts  2.81 us
    ppermute x3, starting transfers between devices, collected(): result = result + lax.ppermute(value, axes, [(b, a) for a, b in route])  2.63 us
  transfers between devices with their start and end apart: 14, of which 4 were waited for; matrix products, arithmetic and copies ran while one was open for 0% of the time, Pallas kernels for 14%

profile of v3, /device:TPU:0, one launch (start us, length us, event | category | flops | bytes accessed | tf_op | source)
XLA Modules:
  0.0 43.5 jit_solution(11426275745067346758)
XLA Ops:
  0.6 2.0 %shard_map.50.refs_0_ = bf16[2112,128]{1,0:T(8,128)(2,1)} custom-call(bf16[384,256]{1,0:T(8,128)(2,1)} %embed_hbm.1, bf16[3,384,128]{2,1,0:T(8,128)(2,1)} %factors_ref.3, f32[32,384]{1,0:T(8,128)} %bitcast.4), custom_call_target="tpu_custom_call" | custom-call | bytes 540672 | tf_op jit(solution)/shard_map/pallas_call | solution.py:358
  2.6 0.7 %collective-permute-start.1 = (bf16[2112,128]{1,0:T(8,128)(2,1)}, bf16[2112,128]{1,0:T(8,128)(2,1)S(1)}, u32[]{:S(2)}, u32[]{:S(2)}) collective-permute-start(bf16[2112,128]{1,0:T(8,128)(2,1)} %shard_map.50.refs_0_), channel_id=1, source_target_pairs={{3,2},{4,5},{11,10},{12,13},{19,18},{20,21},{27,26},{28,29}} | collective-permute-start | bytes 1622024 | tf_op jit(solution)/shard_map/ppermute | solution.py:399
  3.3 0.7 %collective-permute-start = (bf16[2112,128]{1,0:T(8,128)(2,1)}, bf16[2112,128]{1,0:T(8,128)(2,1)S(1)}, u32[]{:S(2)}, u32[]{:S(2)}) collective-permute-start(bf16[2112,128]{1,0:T(8,128)(2,1)} %shard_map.50.refs_0_), channel_id=1, source_target_pairs={{1,2},{6,5},{9,10},{14,13},{17,18},{22,21},{25,26},{30,29}} | collective-permute-start | bytes 1622024 | tf_op jit(solution)/shard_map/ppermute | solution.py:399
  4.0 0.0 copy-start
  4.0 1.0 %copy-done = bf16[3,384,128]{2,1,0:T(8,128)(2,1)S(1)} copy-done((bf16[3,384,128]{2,1,0:T(8,128)(2,1)S(1)}, bf16[3,384,128]{2,1,0:T(8,128)(2,1)}, u32[]{:S(2)}) %copy-start) | copy-done | bytes 294936
  5.0 0.8 %copy-done.4 = f32[384,32]{0,1:T(8,128)S(1)} copy-done((f32[384,32]{0,1:T(8,128)S(1)}, f32[384,32]{0,1:T(8,128)}, u32[]{:S(2)}) %copy-start.4) | copy-done | bytes 49176
  5.8 0.2 shard_map.53
  5.9 3.9 %collective-permute-start.3 = (f32[64,128]{1,0:T(8,128)S(1)}, f32[64,128]{1,0:T(8,128)S(1)}, u32[]{:S(2)}, u32[]{:S(2)}) collective-permute-start(f32[64,128]{1,0:T(8,128)S(1)} %get-tuple-element.19), channel_id=1, source_target_pairs={{0,4},{4,0},{8,12},{12,8},{1,5},{5,1},{9,13},{13,9},{2,6},{6,2},{1... | collective-permute-start | bytes 98312 | tf_op jit(solution)/shard_map/ppermute | solution.py:402
  9.8 0.9 %collective-permute-done.3 = f32[64,128]{1,0:T(8,128)S(1)} collective-permute-done((f32[64,128]{1,0:T(8,128)S(1)}, f32[64,128]{1,0:T(8,128)S(1)}, u32[]{:S(2)}, u32[]{:S(2)}) %collective-permute-start.3) | collective-permute-done | bytes 32800 | tf_op jit(solution)/shard_map/ppermute | solution.py:402
  10.7 1.5 %collective-permute-start.4 = (f32[32,128]{1,0:T(8,128)S(1)}, f32[32,128]{1,0:T(8,128)S(1)}, u32[]{:S(2)}, u32[]{:S(2)}) collective-permute-start(f32[32,128]{1,0:T(8,128)S(1)} %slice.13), channel_id=1, source_target_pairs={{0,8},{4,12},{8,0},{12,4},{1,9},{5,13},{9,1},{13,5},{2,10},{6,14},... | collective-permute-start | bytes 49160 | tf_op jit(solution)/shard_map/ppermute | solution.py:402
  12.2 4.0 %collective-permute-start.2 = (bf16[2112,128]{1,0:T(8,128)(2,1)}, bf16[2112,128]{1,0:T(8,128)(2,1)S(1)}, u32[]{:S(2)}, u32[]{:S(2)}) collective-permute-start(bf16[2112,128]{1,0:T(8,128)(2,1)} %shard_map.50.refs_0_), channel_id=1, source_target_pairs={{0,2},{7,5},{8,10},{15,13},{16,18},{23,21},{24,26},{31,29}} | collective-permute-start | bytes 1622024 | tf_op jit(solution)/shard_map/ppermute | solution.py:399
  16.3 0.0 collective-permute-done.4
  16.3 2.2 %collective-permute-start.7 = (f32[96,128]{1,0:T(8,128)S(1)}, f32[96,128]{1,0:T(8,128)S(1)}, u32[]{:S(2)}, u32[]{:S(2)}) collective-permute-start(f32[96,128]{1,0:T(8,128)S(1)} %pad_maximum_fusion.refs_4_), channel_id=1, source_target_pairs={{0,2},{7,5},{8,10},{15,13},{16,18},{23,21},{24,26},{31,29}} | collective-permute-start | bytes 147464 | tf_op jit(solution)/shard_map/ppermute | solution.py:399
  18.5 0.7 %collective-permute-start.6 = (f32[96,128]{1,0:T(8,128)S(1)}, f32[96,128]{1,0:T(8,128)S(1)}, u32[]{:S(2)}, u32[]{:S(2)}) collective-permute-start(f32[96,128]{1,0:T(8,128)S(1)} %pad_maximum_fusion.refs_4_), channel_id=1, source_target_pairs={{3,2},{4,5},{11,10},{12,13},{19,18},{20,21},{27,26},{28,29}} | collective-permute-start | bytes 147464 | tf_op jit(solution)/shard_map/ppermute | solution.py:399
  19.2 0.7 %collective-permute-start.5 = (f32[96,128]{1,0:T(8,128)S(1)}, f32[96,128]{1,0:T(8,128)S(1)}, u32[]{:S(2)}, u32[]{:S(2)}) collective-permute-start(f32[96,128]{1,0:T(8,128)S(1)} %pad_maximum_fusion.refs_4_), channel_id=1, source_target_pairs={{1,2},{6,5},{9,10},{14,13},{17,18},{22,21},{25,26},{30,29}} | collective-permute-start | bytes 147464 | tf_op jit(solution)/shard_map/ppermute | solution.py:399
  19.9 1.0 %copy-done.2 = bf16[2112,128]{1,0:T(8,128)(2,1)S(1)} copy-done((bf16[2112,128]{1,0:T(8,128)(2,1)S(1)}, bf16[2112,128]{1,0:T(8,128)(2,1)}, u32[]{:S(2)}) %copy-start.2) | copy-done | bytes 540696
  20.9 3.2 %shard_map.51 = (bf16[6,384,384]{2,1,0:T(8,128)(2,1)S(1)}, f32[3,32,384]{2,1,0:T(8,128)S(1)}) custom-call(bf16[2112,128]{1,0:T(8,128)(2,1)S(1)} %copy-done.2, bf16[2112,128]{1,0:T(8,128)(2,1)S(1)} %collective-permute-done.refs_1_, bf16[2112,128]{1,0:T(8,128)(2,1)S(1)} %collective-permute-done.1.refs_2_), custom_call_target="tpu_custom_call" | custom-call | flops 4000000000 | bytes 1622016 | tf_op jit(solution)/shard_map/pallas_call | solution.py:358
  24.1 0.0 collective-permute-done.2.refs_3_
  24.2 2.5 %shard_map.52 = (bf16[4,384,384]{2,1,0:T(8,128)(2,1)S(1)}, f32[4,32,384]{2,1,0:T(8,128)S(1)}) custom-call(f32[3,32,384]{2,1,0:T(8,128)S(1)} %get-tuple-element.15.near_image_ref, bf16[2112,128]{1,0:T(8,128)(2,1)S(1)} %copy-done.3, bf16[2112,128]{1,0:T(8,128)(2,1)S(1)} %collective-permute-done.refs_1_, bf16[2112,128]{1,0:T(8,128)(2,1)S(1)} %collective-permute-done.1.refs_2_, ...), custom_call_target="tpu_custom_call" | custom-call | flops 3000000000 | bytes 2310144 | tf_op jit(solution)/shard_map/pallas_call | solution.py:358
  26.6 0.0 collective-permute-done.6.refs_6_
  26.7 0.0 copy-start.1
  26.7 0.0 copy-start.5
  26.7 1.8 %shard_map.54 = (bf16[512,128]{1,0:T(8,128)(2,1)S(1)}, bf16[512,128]{1,0:T(8,128)(2,1)S(1)}, bf16[512,128]{1,0:T(8,128)(2,1)S(1)}, bf16[512,128]{1,0:T(8,128)(2,1)S(1)}) custom-call(s32[1]{0:T(128)} %bitcast.1.is_host_ref, bf16[6,384,384]{2,1,0:T(8,128)(2,1)S(1)} %get-tuple-element.14.near_high_ref, bf16[4,384,384]{2,1,0:T(8,128)(2,1)S(1)} %get-tuple-element.16.far_high_ref, ...), custom_call_target="tpu_custom_call" | custom-call | flops 2000000000 | bytes 5505028 | tf_op jit(solution)/shard_map/pallas_call | solution.py:358
  28.5 1.3 %collective-permute-start.8 = (bf16[512,128]{1,0:T(8,128)(2,1)S(1)}, bf16[512,128]{1,0:T(8,128)(2,1)S(1)}, u32[]{:S(2)}, u32[]{:S(2)}) collective-permute-start(bf16[512,128]{1,0:T(8,128)(2,1)S(1)} %get-tuple-element.21), channel_id=1, source_target_pairs={{2,0},{5,7},{10,8},{13,15},{18,16},{21,23},{26,24},{29,31}} | collective-permute-start | bytes 393224 | tf_op jit(solution)/shard_map/ppermute | solution.py:462
  29.8 0.7 %collective-permute-start.9 = (bf16[512,128]{1,0:T(8,128)(2,1)S(1)}, bf16[512,128]{1,0:T(8,128)(2,1)S(1)}, u32[]{:S(2)}, u32[]{:S(2)}) collective-permute-start(bf16[512,128]{1,0:T(8,128)(2,1)S(1)} %get-tuple-element.22), channel_id=1, source_target_pairs={{2,3},{5,4},{10,11},{13,12},{18,19},{21,20},{26,27},{29,28}} | collective-permute-start | bytes 393224 | tf_op jit(solution)/shard_map/ppermute | solution.py:462
  30.5 0.7 %collective-permute-start.10 = (bf16[512,128]{1,0:T(8,128)(2,1)S(1)}, bf16[512,128]{1,0:T(8,128)(2,1)S(1)}, u32[]{:S(2)}, u32[]{:S(2)}) collective-permute-start(bf16[512,128]{1,0:T(8,128)(2,1)S(1)} %get-tuple-element.23), channel_id=1, source_target_pairs={{2,1},{5,6},{10,9},{13,14},{18,17},{21,22},{26,25},{29,30}} | collective-permute-start | bytes 393224 | tf_op jit(solution)/shard_map/ppermute | solution.py:462
  31.2 5.2 %collective-permute-done.8 = bf16[512,128]{1,0:T(8,128)(2,1)S(1)} collective-permute-done((bf16[512,128]{1,0:T(8,128)(2,1)S(1)}, bf16[512,128]{1,0:T(8,128)(2,1)S(1)}, u32[]{:S(2)}, u32[]{:S(2)}) %collective-permute-start.8) | collective-permute-done | bytes 131104 | tf_op jit(solution)/shard_map/ppermute | solution.py:462
  36.4 2.3 %collective-permute-start.13 = (bf16[128,128]{1,0:T(8,128)(2,1)S(1)}, bf16[128,128]{1,0:T(8,128)(2,1)S(1)}, u32[]{:S(2)}, u32[]{:S(2)}) collective-permute-start(bf16[128,128]{1,0:T(8,128)(2,1)S(1)} %slice.14.refs_0_), channel_id=1, source_target_pairs={{0,12},{4,8},{8,4},{12,0},{1,13},{5,9},{9,5},{13,1},{2,14},{6,10},... | collective-permute-start | bytes 98312 | tf_op jit(solution)/shard_map/ppermute | solution.py:402
  38.7 0.6 %collective-permute-start.12 = (bf16[128,128]{1,0:T(8,128)(2,1)S(1)}, bf16[128,128]{1,0:T(8,128)(2,1)S(1)}, u32[]{:S(2)}, u32[]{:S(2)}) collective-permute-start(bf16[128,128]{1,0:T(8,128)(2,1)S(1)} %slice.14.refs_0_), channel_id=1, source_target_pairs={{0,8},{4,12},{8,0},{12,4},{1,9},{5,13},{9,1},{13,5},{2,10},{6,14},... | collective-permute-start | bytes 98312 | tf_op jit(solution)/shard_map/ppermute | solution.py:402
  39.2 1.0 %collective-permute-done.13.refs_3_ = bf16[128,128]{1,0:T(8,128)(2,1)S(1)} collective-permute-done((bf16[128,128]{1,0:T(8,128)(2,1)S(1)}, bf16[128,128]{1,0:T(8,128)(2,1)S(1)}, u32[]{:S(2)}, u32[]{:S(2)}) %collective-permute-start.13) | collective-permute-done | bytes 32800 | tf_op jit(solution)/shard_map/ppermute | solution.py:402
  40.3 2.3 %collective-permute-done.12.refs_2_ = bf16[128,128]{1,0:T(8,128)(2,1)S(1)} collective-permute-done((bf16[128,128]{1,0:T(8,128)(2,1)S(1)}, bf16[128,128]{1,0:T(8,128)(2,1)S(1)}, u32[]{:S(2)}, u32[]{:S(2)}) %collective-permute-start.12) | collective-permute-done | bytes 32800 | tf_op jit(solution)/shard_map/ppermute | solution.py:402
  42.6 0.8 %shard_map.55 = (f32[32,384]{1,0:T(8,128)}, f32[32,384]{1,0:T(8,128)}) custom-call(f32[32,384]{1,0:T(8,128)S(1)} %bitcast.6, bf16[3,384,128]{2,1,0:T(8,128)(2,1)S(1)} %copy-done.1, bf16[512,128]{1,0:T(8,128)(2,1)S(1)} %add_add_fusion.result_ref, bf16[128,128]{1,0:T(8,128)(2,1)S(1)} %slice.14.refs_0_, bf16[128,128]{1,0:T(8,128)(2,1)S(1)} %collective-permute-done.11.refs_1_, ...), custom_call_target="tpu_custom_call" | custom-call | bytes 606208 | tf_op jit(solution)/shard_map/pallas_call | solution.py:358
  (20 shorter events, 0.1 us)
Async XLA Ops:
  2.6 16.6 %collective-permute-start.1 = (bf16[2112,128]{1,0:T(8,128)(2,1)}, bf16[2112,128]{1,0:T(8,128)(2,1)S(1)}, u32[]{:S(2)}, u32[]{:S(2)}) collective-permute-start(bf16[2112,128]{1,0:T(8,128)(2,1)} %shard_map.50.refs_0_), channel_id=1, source_target_pairs={{3,2},{4,5},{11,10},{12,13},{19,18},{20,21},{27,26},{28,29}} | collective-permute-start | bytes 1622024 | tf_op jit(solution)/shard_map/ppermute | solution.py:399
  3.3 16.5 %collective-permute-start = (bf16[2112,128]{1,0:T(8,128)(2,1)}, bf16[2112,128]{1,0:T(8,128)(2,1)S(1)}, u32[]{:S(2)}, u32[]{:S(2)}) collective-permute-start(bf16[2112,128]{1,0:T(8,128)(2,1)} %shard_map.50.refs_0_), channel_id=1, source_target_pairs={{1,2},{6,5},{9,10},{14,13},{17,18},{22,21},{25,26},{30,29}} | collective-permute-start | bytes 1622024 | tf_op jit(solution)/shard_map/ppermute | solution.py:399
  4.0 1.0 %copy-start = (bf16[3,384,128]{2,1,0:T(8,128)(2,1)S(1)}, bf16[3,384,128]{2,1,0:T(8,128)(2,1)}, u32[]{:S(2)}) copy-start(bf16[3,384,128]{2,1,0:T(8,128)(2,1)} %factors_ref.3) | copy-start | bytes 884740
  5.0 0.8 %copy-start.4 = (f32[384,32]{0,1:T(8,128)S(1)}, f32[384,32]{0,1:T(8,128)}, u32[]{:S(2)}) copy-start(f32[384,32]{0,1:T(8,128)} %param.5) | copy-start | bytes 147460
  5.9 4.7 %collective-permute-start.3 = (f32[64,128]{1,0:T(8,128)S(1)}, f32[64,128]{1,0:T(8,128)S(1)}, u32[]{:S(2)}, u32[]{:S(2)}) collective-permute-start(f32[64,128]{1,0:T(8,128)S(1)} %get-tuple-element.19), channel_id=1, source_target_pairs={{0,4},{4,0},{8,12},{12,8},{1,5},{5,1},{9,13},{13,9},{2,6},{6,2},{1... | collective-permute-start | bytes 98312 | tf_op jit(solution)/shard_map/ppermute | solution.py:402
  10.7 5.6 %collective-permute-start.4 = (f32[32,128]{1,0:T(8,128)S(1)}, f32[32,128]{1,0:T(8,128)S(1)}, u32[]{:S(2)}, u32[]{:S(2)}) collective-permute-start(f32[32,128]{1,0:T(8,128)S(1)} %slice.13), channel_id=1, source_target_pairs={{0,8},{4,12},{8,0},{12,4},{1,9},{5,13},{9,1},{13,5},{2,10},{6,14},... | collective-permute-start | bytes 49160 | tf_op jit(solution)/shard_map/ppermute | solution.py:402
  12.2 11.9 %collective-permute-start.2 = (bf16[2112,128]{1,0:T(8,128)(2,1)}, bf16[2112,128]{1,0:T(8,128)(2,1)S(1)}, u32[]{:S(2)}, u32[]{:S(2)}) collective-permute-start(bf16[2112,128]{1,0:T(8,128)(2,1)} %shard_map.50.refs_0_), channel_id=1, source_target_pairs={{0,2},{7,5},{8,10},{15,13},{16,18},{23,21},{24,26},{31,29}} | collective-permute-start | bytes 1622024 | tf_op jit(solution)/shard_map/ppermute | solution.py:399
  16.3 10.4 %collective-permute-start.7 = (f32[96,128]{1,0:T(8,128)S(1)}, f32[96,128]{1,0:T(8,128)S(1)}, u32[]{:S(2)}, u32[]{:S(2)}) collective-permute-start(f32[96,128]{1,0:T(8,128)S(1)} %pad_maximum_fusion.refs_4_), channel_id=1, source_target_pairs={{0,2},{7,5},{8,10},{15,13},{16,18},{23,21},{24,26},{31,29}} | collective-permute-start | bytes 147464 | tf_op jit(solution)/shard_map/ppermute | solution.py:399
  18.5 8.2 %collective-permute-start.6 = (f32[96,128]{1,0:T(8,128)S(1)}, f32[96,128]{1,0:T(8,128)S(1)}, u32[]{:S(2)}, u32[]{:S(2)}) collective-permute-start(f32[96,128]{1,0:T(8,128)S(1)} %pad_maximum_fusion.refs_4_), channel_id=1, source_target_pairs={{3,2},{4,5},{11,10},{12,13},{19,18},{20,21},{27,26},{28,29}} | collective-permute-start | bytes 147464 | tf_op jit(solution)/shard_map/ppermute | solution.py:399
  19.2 7.5 %collective-permute-start.5 = (f32[96,128]{1,0:T(8,128)S(1)}, f32[96,128]{1,0:T(8,128)S(1)}, u32[]{:S(2)}, u32[]{:S(2)}) collective-permute-start(f32[96,128]{1,0:T(8,128)S(1)} %pad_maximum_fusion.refs_4_), channel_id=1, source_target_pairs={{1,2},{6,5},{9,10},{14,13},{17,18},{22,21},{25,26},{30,29}} | collective-permute-start | bytes 147464 | tf_op jit(solution)/shard_map/ppermute | solution.py:399
  19.8 1.0 %copy-start.2 = (bf16[2112,128]{1,0:T(8,128)(2,1)S(1)}, bf16[2112,128]{1,0:T(8,128)(2,1)}, u32[]{:S(2)}) copy-start(bf16[2112,128]{1,0:T(8,128)(2,1)} %shard_map.50.refs_0_) | copy-start | bytes 1622020
  20.9 3.3 %copy-start.3 = (bf16[2112,128]{1,0:T(8,128)(2,1)S(1)}, bf16[2112,128]{1,0:T(8,128)(2,1)}, u32[]{:S(2)}) copy-start(bf16[2112,128]{1,0:T(8,128)(2,1)} %shard_map.50.refs_0_) | copy-start | bytes 1622020
  26.7 15.9 %copy-start.1 = (bf16[3,384,128]{2,1,0:T(8,128)(2,1)S(1)}, bf16[3,384,128]{2,1,0:T(8,128)(2,1)}, u32[]{:S(2)}) copy-start(bf16[3,384,128]{2,1,0:T(8,128)(2,1)} %factors_ref.3) | copy-start | bytes 884740
  26.7 15.9 %copy-start.5 = (f32[384,32]{0,1:T(8,128)S(1)}, f32[384,32]{0,1:T(8,128)}, u32[]{:S(2)}) copy-start(f32[384,32]{0,1:T(8,128)} %param.5) | copy-start | bytes 147460
  28.5 7.9 %collective-permute-start.8 = (bf16[512,128]{1,0:T(8,128)(2,1)S(1)}, bf16[512,128]{1,0:T(8,128)(2,1)S(1)}, u32[]{:S(2)}, u32[]{:S(2)}) collective-permute-start(bf16[512,128]{1,0:T(8,128)(2,1)S(1)} %get-tuple-element.21), channel_id=1, source_target_pairs={{2,0},{5,7},{10,8},{13,15},{18,16},{21,23},{26,24},{29,31}} | collective-permute-start | bytes 393224 | tf_op jit(solution)/shard_map/ppermute | solution.py:462
  29.8 6.6 %collective-permute-start.9 = (bf16[512,128]{1,0:T(8,128)(2,1)S(1)}, bf16[512,128]{1,0:T(8,128)(2,1)S(1)}, u32[]{:S(2)}, u32[]{:S(2)}) collective-permute-start(bf16[512,128]{1,0:T(8,128)(2,1)S(1)} %get-tuple-element.22), channel_id=1, source_target_pairs={{2,3},{5,4},{10,11},{13,12},{18,19},{21,20},{26,27},{29,28}} | collective-permute-start | bytes 393224 | tf_op jit(solution)/shard_map/ppermute | solution.py:462
  30.5 5.9 %collective-permute-start.10 = (bf16[512,128]{1,0:T(8,128)(2,1)S(1)}, bf16[512,128]{1,0:T(8,128)(2,1)S(1)}, u32[]{:S(2)}, u32[]{:S(2)}) collective-permute-start(bf16[512,128]{1,0:T(8,128)(2,1)S(1)} %get-tuple-element.23), channel_id=1, source_target_pairs={{2,1},{5,6},{10,9},{13,14},{18,17},{21,22},{26,25},{29,30}} | collective-permute-start | bytes 393224 | tf_op jit(solution)/shard_map/ppermute | solution.py:462
  36.4 3.9 %collective-permute-start.13 = (bf16[128,128]{1,0:T(8,128)(2,1)S(1)}, bf16[128,128]{1,0:T(8,128)(2,1)S(1)}, u32[]{:S(2)}, u32[]{:S(2)}) collective-permute-start(bf16[128,128]{1,0:T(8,128)(2,1)S(1)} %slice.14.refs_0_), channel_id=1, source_target_pairs={{0,12},{4,8},{8,4},{12,0},{1,13},{5,9},{9,5},{13,1},{2,14},{6,10},... | collective-permute-start | bytes 98312 | tf_op jit(solution)/shard_map/ppermute | solution.py:402
  38.7 3.9 %collective-permute-start.12 = (bf16[128,128]{1,0:T(8,128)(2,1)S(1)}, bf16[128,128]{1,0:T(8,128)(2,1)S(1)}, u32[]{:S(2)}, u32[]{:S(2)}) collective-permute-start(bf16[128,128]{1,0:T(8,128)(2,1)S(1)} %slice.14.refs_0_), channel_id=1, source_target_pairs={{0,8},{4,12},{8,0},{12,4},{1,9},{5,13},{9,1},{13,5},{2,10},{6,14},... | collective-permute-start | bytes 98312 | tf_op jit(solution)/shard_map/ppermute | solution.py:402
  39.2 3.4 %collective-permute-start.11 = (bf16[128,128]{1,0:T(8,128)(2,1)S(1)}, bf16[128,128]{1,0:T(8,128)(2,1)S(1)}, u32[]{:S(2)}, u32[]{:S(2)}) collective-permute-start(bf16[128,128]{1,0:T(8,128)(2,1)S(1)} %slice.14.refs_0_), channel_id=1, source_target_pairs={{0,4},{4,0},{8,12},{12,8},{1,5},{5,1},{9,13},{13,9},{2,6},{6,2},{1... | collective-permute-start | bytes 98312 | tf_op jit(solution)/shard_map/ppermute | solution.py:402

commit v4 on v3

--- a/solution.py
+++ b/solution.py
@@ -90,61 +90,62 @@
     return [(i, j) for j in range(slots) for i in range(j + 1)]
 
 
-def project_kernel(factors_ref, field_ref, first_ref, upper_ref):
-    levels = factors_ref.shape[0]
+def put_halves(ref, start, value):
+    rows = value.shape[0]
+    high = value.astype(BF16)
+    ref[start : start + rows] = high
+    ref[start + rows : start + 2 * rows] = (value - high.astype(F32)).astype(BF16)
+
+
+def pack_kernel(embed_ref, factors_ref, field_ref, head_ref, tail_ref, first_ref, upper_ref):
+    levels, rows, rank = factors_ref.shape
     nrhs = field_ref.shape[0]
+    lanes = embed_ref.shape[1] // rank
     rounded = field_ref[...].astype(BF16)
     first_ref[...] = mm(rounded, factors_ref[0])
     for level in range(1, levels):
         upper_ref[(level - 1) * nrhs : level * nrhs] = mm(rounded, factors_ref[level])
-
-
-def pack_kernel(embed_hbm, factors_hbm, field_hbm, message_ref, field_ref, sems):
-    levels, rows, rank = factors_hbm.shape
-    nrhs = field_ref.shape[0]
-    lanes = embed_hbm.shape[1] // rank
-    head = lanes * rows + 2 * nrhs * (rows // rank)
-    copies = [pltpu.make_async_copy(field_hbm, field_ref, sems.at[0])]
     for k in range(lanes):
-        piece = embed_hbm.at[:, pl.ds(k * rank, rank)]
-        place = message_ref.at[pl.ds(k * rows, rows)]
-        copies.append(pltpu.make_async_copy(piece, place, sems.at[len(copies)]))
+        head_ref[k * rows : (k + 1) * rows] = embed_ref[:, k * rank : (k + 1) * rank]
+    for k in range(rows // rank):
+        put_halves(head_ref, lanes * rows + 2 * k * nrhs, field_ref[:, k * rank : (k + 1) * rank])
     for level in range(levels):
-        place = message_ref.at[pl.ds(head + level * rows, rows)]
-        copies.append(pltpu.make_async_copy(factors_hbm.at[level], place, sems.at[len(copies)]))
-    for copy in copies:
-        copy.start()
-    copies[0].wait()
-    for k in range(rows // rank):
-        start = lanes * rows + 2 * k * nrhs
-        value = field_ref[:, k * rank : (k + 1) * rank]
-        high = value.astype(BF16)
-        message_ref[start : start + nrhs] = high
-        message_ref[start + nrhs : start + 2 * nrhs] = (value - high.astype(F32)).astype(BF16)
-    for copy in copies[1:]:
-        copy.wait()
+        tail_ref[level * rows : (level + 1) * rows] = factors_ref[level]
+
+
+def tail_kernel(start, tail_in, *refs):
+    del tail_in
+    *proj_refs, tail_ref = refs
+    for ref in proj_refs:
+        put_halves(tail_ref, start, ref[...])
+        start += 2 * ref.shape[0]
 
 
 class Message:
-    def __init__(self, shape, ref):
+    def __init__(self, shape, head_ref=None, tail_ref=None):
         self.rows, self.dims, self.levels, self.rank, self.nrhs = shape
-        self.ref = ref
+        self.head = head_ref
+        self.tail = tail_ref
 
     def embed(self):
         rows = self.rows
-        pieces = [self.ref[k * rows : (k + 1) * rows] for k in range(self.dims // self.rank)]
+        pieces = [self.head[k * rows : (k + 1) * rows] for k in range(self.dims // self.rank)]
         return jnp.concatenate(pieces, axis=1)
 
     def field(self):
         base = self.dims // self.rank * self.rows
         step = 2 * self.nrhs
         count = self.rows // self.rank
-        pieces = [self.ref[base + k * step : base + (k + 1) * step] for k in range(count)]
+        pieces = [self.head[base + k * step : base + (k + 1) * step] for k in range(count)]
         return jnp.concatenate(pieces, axis=1)
 
     def factor(self, level):
-        base = self.dims // self.rank * self.rows + 2 * self.nrhs * (self.rows // self.rank)
-        return self.ref[base + level * self.rows : base + (level + 1) * self.rows]
+        return self.tail[level * self.rows : (level + 1) * self.rows]
+
+    def proj(self, level):
+        base = self.levels * self.rows + 2 * level * self.nrhs
+        halves = self.tail[base : base + 2 * self.nrhs].astype(F32)
+        return halves[: self.nrhs] + halves[self.nrhs :]
 
     def project(self, field):
         return jnp.concatenate([mm(field, self.factor(l)) for l in range(self.levels)], axis=0)
@@ -232,11 +233,10 @@
 
 
 def main_kernel(slots, shape, is_host_ref, near_high_ref, far_high_ref, image_ref, *refs):
-    messages = [Message(shape, ref) for ref in refs[:slots]]
-    proj_refs = refs[slots : 2 * slots]
+    messages = [Message(shape, refs[s], refs[slots + s]) for s in range(slots)]
     results = refs[2 * slots :]
     rows, _, levels, rank, nrhs = shape
-    near = len(proj_refs) - 1
+    near = slots - 1
     mine = is_host_ref[0] == 1
 
     def put(s, at, value):
@@ -252,9 +252,9 @@
 
     proj = []
     for level in range(levels):
-        total = proj_refs[0][level * nrhs : (level + 1) * nrhs]
-        for ref in proj_refs[1:]:
-            total = total + ref[level * nrhs : (level + 1) * nrhs]
+        total = messages[0].proj(level)
+        for message in messages[1:]:
+            total = total + message.proj(level)
         proj.append(total.astype(BF16))
     fields = [message.field() for message in messages]
     field, image, image_b = [], [], []
@@ -353,7 +353,7 @@
     residual_ref[...] = field - (alpha0 + alpha1 * keep) * image + (alpha1 * alpha0) * second
 
 
-def call(kernel, outs, args, specs, scratch=(), flops=0, limit=24):
+def call(kernel, outs, args, specs, scratch=(), flops=0, limit=24, aliases={}):
     moved = sum(a.size * a.dtype.itemsize for a in args)
     return pl.pallas_call(
         kernel,
@@ -361,6 +361,7 @@
         in_specs=specs,
         out_specs=[VMEM] * len(outs),
         scratch_shapes=list(scratch),
+        input_output_aliases=aliases,
         cost_estimate=pl.CostEstimate(flops=flops, bytes_accessed=moved, transcendentals=0),
         compiler_params=pltpu.CompilerParams(vmem_limit_bytes=limit * 2**20),
     )(*args)
@@ -369,8 +370,7 @@
 def collected(embed, factors, targets):
     leaves, inner = lax.axis_size("leaf"), lax.axis_size("inner")
     levels, rows, rank = factors.shape
-    nrhs = targets.shape[1]
-    dims = embed.shape[1]
+    dims, nrhs = embed.shape[1], targets.shape[1]
     shape = (rows, dims, levels, rank, nrhs)
 
     def host(leaf):
@@ -402,38 +402,33 @@
         return lax.ppermute(value, "leaf", [(i, i ^ m) for i in range(leaves)])
 
     field = targets.T
-    height = dims // rank * rows + 2 * nrhs * (rows // rank) + levels * rows
-    hbm = pl.BlockSpec(memory_space=pltpu.HBM)
-    (message,) = call(
-        pack_kernel,
-        [((height, rank), BF16)],
-        [embed, factors, field],
-        [hbm] * 3,
-        scratch=[
-            pltpu.VMEM((nrhs, rows), F32),
-            pltpu.SemaphoreType.DMA((1 + dims // rank + levels,)),
-        ],
-        limit=60,
-    )
-    messages = to_host(message)
-    first, upper = call(
-        project_kernel,
-        [((nrhs, rank), F32), (((levels - 1) * nrhs, rank), F32)],
-        [factors, field],
-        [VMEM] * 2,
-    )
-    projs = [first]
+    near = inner - 1
+    held, pairs = len(pairs_of(near)), len(pairs_of(inner))
+    head = dims // rank * rows + 2 * nrhs * (rows // rank)
+    tail = levels * (rows + 2 * nrhs)
+    sizes = [((head, rank), BF16), ((tail, rank), BF16)]
+    sizes += [((nrhs, rank), F32), (((levels - 1) * nrhs, rank), F32)]
+    first_part, second_part, first, upper = call(
+        pack_kernel, sizes, [embed, factors, targets.T], [VMEM] * 3
+    )
+    heads = to_host(first_part)
+    proj = [first]
     for bit in range(levels - 1):
         upper = upper + over_leaf(upper, 2**bit)
-        projs.append(upper[:nrhs])
+        proj.append(upper[:nrhs])
         upper = upper[nrhs:]
-    projs = to_host(jnp.concatenate(projs, axis=0))
-    near = inner - 1
-    held, pairs = len(pairs_of(near)), len(pairs_of(inner))
+    (second_part,) = call(
+        functools.partial(tail_kernel, levels * rows),
+        [sizes[1]],
+        [second_part] + proj,
+        [VMEM] * (1 + levels),
+        aliases={0: 0},
+    )
+    tails = to_host(second_part)
     near_high, near_image = call(
         functools.partial(near_kernel, near, shape),
         [((held, rows, rows), BF16), ((near, nrhs, rows), F32)],
-        messages[:near],
+        heads[:near],
         [VMEM] * near,
         scratch=[pltpu.VMEM((held, rows, rows), BF16)],
         flops=NEAR_FLOPS,
@@ -441,7 +436,7 @@
     far_high, image = call(
         functools.partial(far_kernel, inner, shape),
         [((pairs - held, rows, rows), BF16), ((inner, nrhs, rows), F32)],
-        [near_image] + messages,
+        [near_image] + heads,
         [VMEM] * (1 + inner),
         scratch=[pltpu.VMEM((pairs - held, rows, rows), BF16)],
         flops=FAR_FLOPS,
@@ -453,7 +448,7 @@
     results = call(
         functools.partial(main_kernel, inner, shape),
         [((height, rank), BF16)] * inner,
-        [is_host, near_high, far_high, image] + messages + projs,
+        [is_host, near_high, far_high, image] + heads + tails,
         [SMEM] + [VMEM] * (3 + 2 * inner),
         flops=MAIN_FLOPS,
     )

time: 43.9 us -> 41.3 us (0.941)
  Pallas kernels: 10.5 us -> 8.58 us
  starting transfers between devices: 19.8 us -> 18.3 us
  waiting for transfers between devices: 9.47 us -> 10.3 us
    ppermute x5, starting transfers between devices: 8.25 us -> 5.01 us  [over_leaf(): return lax.ppermute(value, 'leaf', [(i, i ^ m) for i in range(leaves)])]
    ppermute x5, waiting for transfers between devices: 4.21 us -> 2.19 us  [over_leaf(): return lax.ppermute(value, 'leaf', [(i, i ^ m) for i in range(leaves)])]
    pallas_call x6, Pallas kernels: 10.5 us -> 8.58 us  [call(): pl.pallas_call(kernel, out_shape=[jax.ShapeDtypeStruct(shape, dtype) for...]
    ppermute x6, starting transfers between devices: 8.88 us -> 10.6 us  [to_host(): return [value] + [lax.ppermute(value, axes, route) for route in routes]]
    ppermute x6, waiting for transfers between devices: 0.04 us -> 1.71 us  [to_host(): return [value] + [lax.ppermute(value, axes, route) for route in routes]]
    ppermute x3, waiting for transfers between devices: 5.22 us -> 6.43 us  [collected(): result = result + lax.ppermute(value, axes, [(b, a) for a, b in route])]
    unnamed x12 -> x10, local copies, waits for them, and re-layouts: 2.81 us -> 2.69 us
where the time goes in v4:
time: 41.3 us; the launch traced here: 40.8 us
  starting transfers between devices  18.3 us (44%)
  waiting for transfers between devices  10.3 us (25%)
  Pallas kernels  8.58 us (21%)
  local copies, waits for them, and re-layouts  2.7 us (7%)
  between operations  0.85 us (2%)
    ppermute x6, starting transfers between devices, to_host(): return [value] + [lax.ppermute(value, axes, route) for route in routes]  10.6 us
    pallas_call x6, Pallas kernels, call(): pl.pallas_call(kernel, out_shape=[jax.ShapeDtypeStruct(shape, dtype) for...  8.58 us
    ppermute x3, waiting for transfers between devices, collected(): result = result + lax.ppermute(value, axes, [(b, a) for a, b in route])  6.43 us
    ppermute x5, starting transfers between devices, over_leaf(): return lax.ppermute(value, 'leaf', [(i, i ^ m) for i in range(leaves)])  5.01 us
    unnamed x10, local copies, waits for them, and re-layouts  2.69 us
    ppermute x3, starting transfers between devices, collected(): result = result + lax.ppermute(value, axes, [(b, a) for a, b in route])  2.63 us
    ppermute x5, waiting for transfers between devices, over_leaf(): return lax.ppermute(value, 'leaf', [(i, i ^ m) for i in range(leaves)])  2.19 us
    ppermute x6, waiting for transfers between devices, to_host(): return [value] + [lax.ppermute(value, axes, route) for route in routes]  1.71 us
  transfers between devices with their start and end apart: 14, of which 4 were waited for; matrix products, arithmetic and copies ran while one was open for 0% of the time, Pallas kernels for 14%

profile of v4, /device:TPU:0, one launch (start us, length us, event | category | flops | bytes accessed | tf_op | source)
XLA Modules:
  0.0 40.8 jit_solution(2973213273141877960)
XLA Ops:
  0.6 0.0 copy-start
  0.6 1.0 %copy-done = bf16[3,384,128]{2,1,0:T(8,128)(2,1)S(1)} copy-done((bf16[3,384,128]{2,1,0:T(8,128)(2,1)S(1)}, bf16[3,384,128]{2,1,0:T(8,128)(2,1)}, u32[]{:S(2)}) %copy-start) | copy-done | bytes 294936
  1.6 0.8 %copy-done.2 = f32[384,32]{0,1:T(8,128)S(1)} copy-done((f32[384,32]{0,1:T(8,128)S(1)}, f32[384,32]{0,1:T(8,128)}, u32[]{:S(2)}) %copy-start.2) | copy-done | bytes 49176
  2.4 0.9 %copy-done.4 = bf16[384,256]{1,0:T(8,128)(2,1)S(1)} copy-done((bf16[384,256]{1,0:T(8,128)(2,1)S(1)}, bf16[384,256]{1,0:T(8,128)(2,1)}, u32[]{:S(2)}) %copy-start.4) | copy-done | bytes 196632
  3.3 0.2 shard_map.50
  3.5 0.5 %collective-permute-start.3 = (f32[64,128]{1,0:T(8,128)S(1)}, f32[64,128]{1,0:T(8,128)S(1)}, u32[]{:S(2)}, u32[]{:S(2)}) collective-permute-start(f32[64,128]{1,0:T(8,128)S(1)} %get-tuple-element.23), channel_id=1, source_target_pairs={{0,4},{4,0},{8,12},{12,8},{1,5},{5,1},{9,13},{13,9},{2,6},{6,2},{1... | collective-permute-start | bytes 98312 | tf_op jit(solution)/shard_map/ppermute | solution.py:402
  4.0 0.7 %collective-permute-start.1 = (bf16[960,128]{1,0:T(8,128)(2,1)S(1)}, bf16[960,128]{1,0:T(8,128)(2,1)S(1)}, u32[]{:S(2)}, u32[]{:S(2)}) collective-permute-start(bf16[960,128]{1,0:T(8,128)(2,1)S(1)} %get-tuple-element.16.refs_0_), channel_id=1, source_target_pairs={{3,2},{4,5},{11,10},{12,13},{19,18},{20,21},{27,26},{28,29}} | collective-permute-start | bytes 737288 | tf_op jit(solution)/shard_map/ppermute | solution.py:399
  4.7 0.7 %collective-permute-start = (bf16[960,128]{1,0:T(8,128)(2,1)S(1)}, bf16[960,128]{1,0:T(8,128)(2,1)S(1)}, u32[]{:S(2)}, u32[]{:S(2)}) collective-permute-start(bf16[960,128]{1,0:T(8,128)(2,1)S(1)} %get-tuple-element.16.refs_0_), channel_id=1, source_target_pairs={{1,2},{6,5},{9,10},{14,13},{17,18},{22,21},{25,26},{30,29}} | collective-permute-start | bytes 737288 | tf_op jit(solution)/shard_map/ppermute | solution.py:399
  5.4 2.6 %collective-permute-start.4 = (f32[32,128]{1,0:T(8,128)S(1)}, f32[32,128]{1,0:T(8,128)S(1)}, u32[]{:S(2)}, u32[]{:S(2)}) collective-permute-start(f32[32,128]{1,0:T(8,128)S(1)} %slice.13), channel_id=1, source_target_pairs={{0,8},{4,12},{8,0},{12,4},{1,9},{5,13},{9,1},{13,5},{2,10},{6,14},... | collective-permute-start | bytes 49160 | tf_op jit(solution)/shard_map/ppermute | solution.py:402
  8.0 5.7 %collective-permute-start.2 = (bf16[960,128]{1,0:T(8,128)(2,1)S(1)}, bf16[960,128]{1,0:T(8,128)(2,1)S(1)}, u32[]{:S(2)}, u32[]{:S(2)}) collective-permute-start(bf16[960,128]{1,0:T(8,128)(2,1)S(1)} %get-tuple-element.16.refs_0_), channel_id=1, source_target_pairs={{0,2},{7,5},{8,10},{15,13},{16,18},{23,21},{24,26},{31,29}} | collective-permute-start | bytes 737288 | tf_op jit(solution)/shard_map/ppermute | solution.py:399
  13.8 0.0 collective-permute-done.4
  13.8 2.2 %collective-permute-start.7 = (bf16[1344,128]{1,0:T(8,128)(2,1)S(1)}, bf16[1344,128]{1,0:T(8,128)(2,1)S(1)}, u32[]{:S(2)}, u32[]{:S(2)}) collective-permute-start(bf16[1344,128]{1,0:T(8,128)(2,1)S(1)} %shard_map.53.refs_4_), channel_id=1, source_target_pairs={{0,2},{7,5},{8,10},{15,13},{16,18},{23,21},{24,26},{31,29}} | collective-permute-start | bytes 1032200 | tf_op jit(solution)/shard_map/ppermute | solution.py:399
  16.0 0.7 %collective-permute-start.6 = (bf16[1344,128]{1,0:T(8,128)(2,1)S(1)}, bf16[1344,128]{1,0:T(8,128)(2,1)S(1)}, u32[]{:S(2)}, u32[]{:S(2)}) collective-permute-start(bf16[1344,128]{1,0:T(8,128)(2,1)S(1)} %shard_map.53.refs_4_), channel_id=1, source_target_pairs={{3,2},{4,5},{11,10},{12,13},{19,18},{20,21},{27,26},{28,29}} | collective-permute-start | bytes 1032200 | tf_op jit(solution)/shard_map/ppermute | solution.py:399
  16.7 0.0 collective-permute-done.1.refs_2_
  16.7 0.7 %collective-permute-start.5 = (bf16[1344,128]{1,0:T(8,128)(2,1)S(1)}, bf16[1344,128]{1,0:T(8,128)(2,1)S(1)}, u32[]{:S(2)}, u32[]{:S(2)}) collective-permute-start(bf16[1344,128]{1,0:T(8,128)(2,1)S(1)} %shard_map.53.refs_4_), channel_id=1, source_target_pairs={{1,2},{6,5},{9,10},{14,13},{17,18},{22,21},{25,26},{30,29}} | collective-permute-start | bytes 1032200 | tf_op jit(solution)/shard_map/ppermute | solution.py:399
  17.4 3.2 %shard_map.51 = (bf16[6,384,384]{2,1,0:T(8,128)(2,1)S(1)}, f32[3,32,384]{2,1,0:T(8,128)S(1)}) custom-call(bf16[960,128]{1,0:T(8,128)(2,1)S(1)} %get-tuple-element.16.refs_0_, bf16[960,128]{1,0:T(8,128)(2,1)S(1)} %collective-permute-done.refs_1_, bf16[960,128]{1,0:T(8,128)(2,1)S(1)} %collective-permute-done.1.refs_2_), custom_call_target="tpu_custom_call" | custom-call | flops 4000000000 | bytes 737280 | tf_op jit(solution)/shard_map/pallas_call | solution.py:358
  20.6 0.0 collective-permute-done.2.refs_3_
  20.7 2.5 %shard_map.52 = (bf16[4,384,384]{2,1,0:T(8,128)(2,1)S(1)}, f32[4,32,384]{2,1,0:T(8,128)S(1)}) custom-call(f32[3,32,384]{2,1,0:T(8,128)S(1)} %get-tuple-element.18.near_image_ref, bf16[960,128]{1,0:T(8,128)(2,1)S(1)} %get-tuple-element.16.refs_0_, bf16[960,128]{1,0:T(8,128)(2,1)S(1)} %collective-permute-done.refs_1_, ...), custom_call_target="tpu_custom_call" | custom-call | flops 3000000000 | bytes 1130496 | tf_op jit(solution)/shard_map/pallas_call | solution.py:358
  23.1 1.7 %collective-permute-done.7.refs_7_ = bf16[1344,128]{1,0:T(8,128)(2,1)S(1)} collective-permute-done((bf16[1344,128]{1,0:T(8,128)(2,1)S(1)}, bf16[1344,128]{1,0:T(8,128)(2,1)S(1)}, u32[]{:S(2)}, u32[]{:S(2)}) %collective-permute-start.7) | collective-permute-done | bytes 344096 | tf_op jit(solution)/shard_map/ppermute | solution.py:399
  24.8 0.0 collective-permute-done.6.refs_6_
  24.8 0.0 collective-permute-done.5.refs_5_
  24.9 1.8 %shard_map.54 = (bf16[512,128]{1,0:T(8,128)(2,1)S(1)}, bf16[512,128]{1,0:T(8,128)(2,1)S(1)}, bf16[512,128]{1,0:T(8,128)(2,1)S(1)}, bf16[512,128]{1,0:T(8,128)(2,1)S(1)}) custom-call(s32[1]{0:T(128)} %bitcast.1.is_host_ref, bf16[6,384,384]{2,1,0:T(8,128)(2,1)S(1)} %get-tuple-element.17.near_high_ref, bf16[4,384,384]{2,1,0:T(8,128)(2,1)S(1)} %get-tuple-element.19.far_high_ref, ...), custom_call_target="tpu_custom_call" | custom-call | flops 2000000000 | bytes 5505028 | tf_op jit(solution)/shard_map/pallas_call | solution.py:358
  26.7 1.3 %collective-permute-start.8 = (bf16[512,128]{1,0:T(8,128)(2,1)S(1)}, bf16[512,128]{1,0:T(8,128)(2,1)S(1)}, u32[]{:S(2)}, u32[]{:S(2)}) collective-permute-start(bf16[512,128]{1,0:T(8,128)(2,1)S(1)} %get-tuple-element.25), channel_id=1, source_target_pairs={{2,0},{5,7},{10,8},{13,15},{18,16},{21,23},{26,24},{29,31}} | collective-permute-start | bytes 393224 | tf_op jit(solution)/shard_map/ppermute | solution.py:457
  28.0 0.7 %collective-permute-start.9 = (bf16[512,128]{1,0:T(8,128)(2,1)S(1)}, bf16[512,128]{1,0:T(8,128)(2,1)S(1)}, u32[]{:S(2)}, u32[]{:S(2)}) collective-permute-start(bf16[512,128]{1,0:T(8,128)(2,1)S(1)} %get-tuple-element.26), channel_id=1, source_target_pairs={{2,3},{5,4},{10,11},{13,12},{18,19},{21,20},{26,27},{29,28}} | collective-permute-start | bytes 393224 | tf_op jit(solution)/shard_map/ppermute | solution.py:457
  28.7 0.7 %collective-permute-start.10 = (bf16[512,128]{1,0:T(8,128)(2,1)S(1)}, bf16[512,128]{1,0:T(8,128)(2,1)S(1)}, u32[]{:S(2)}, u32[]{:S(2)}) collective-permute-start(bf16[512,128]{1,0:T(8,128)(2,1)S(1)} %get-tuple-element.27), channel_id=1, source_target_pairs={{2,1},{5,6},{10,9},{13,14},{18,17},{21,22},{26,25},{29,30}} | collective-permute-start | bytes 393224 | tf_op jit(solution)/shard_map/ppermute | solution.py:457
  29.3 6.4 %collective-permute-done.8 = bf16[512,128]{1,0:T(8,128)(2,1)S(1)} collective-permute-done((bf16[512,128]{1,0:T(8,128)(2,1)S(1)}, bf16[512,128]{1,0:T(8,128)(2,1)S(1)}, u32[]{:S(2)}, u32[]{:S(2)}) %collective-permute-start.8) | collective-permute-done | bytes 131104 | tf_op jit(solution)/shard_map/ppermute | solution.py:457
  35.8 0.1 collective-permute-start.13
  35.9 0.6 %collective-permute-start.12 = (bf16[128,128]{1,0:T(8,128)(2,1)S(1)}, bf16[128,128]{1,0:T(8,128)(2,1)S(1)}, u32[]{:S(2)}, u32[]{:S(2)}) collective-permute-start(bf16[128,128]{1,0:T(8,128)(2,1)S(1)} %slice.14.refs_0_), channel_id=1, source_target_pairs={{0,8},{4,12},{8,0},{12,4},{1,9},{5,13},{9,1},{13,5},{2,10},{6,14},... | collective-permute-start | bytes 98312 | tf_op jit(solution)/shard_map/ppermute | solution.py:402
  36.4 1.3 %collective-permute-start.11 = (bf16[128,128]{1,0:T(8,128)(2,1)S(1)}, bf16[128,128]{1,0:T(8,128)(2,1)S(1)}, u32[]{:S(2)}, u32[]{:S(2)}) collective-permute-start(bf16[128,128]{1,0:T(8,128)(2,1)S(1)} %slice.14.refs_0_), channel_id=1, source_target_pairs={{0,4},{4,0},{8,12},{12,8},{1,5},{5,1},{9,13},{13,9},{2,6},{6,2},{1... | collective-permute-start | bytes 98312 | tf_op jit(solution)/shard_map/ppermute | solution.py:402
  37.7 1.5 %collective-permute-done.13.refs_3_ = bf16[128,128]{1,0:T(8,128)(2,1)S(1)} collective-permute-done((bf16[128,128]{1,0:T(8,128)(2,1)S(1)}, bf16[128,128]{1,0:T(8,128)(2,1)S(1)}, u32[]{:S(2)}, u32[]{:S(2)}) %collective-permute-start.13) | collective-permute-done | bytes 32800 | tf_op jit(solution)/shard_map/ppermute | solution.py:402
  39.2 0.7 %collective-permute-done.12.refs_2_ = bf16[128,128]{1,0:T(8,128)(2,1)S(1)} collective-permute-done((bf16[128,128]{1,0:T(8,128)(2,1)S(1)}, bf16[128,128]{1,0:T(8,128)(2,1)S(1)}, u32[]{:S(2)}, u32[]{:S(2)}) %collective-permute-start.12) | collective-permute-done | bytes 32800 | tf_op jit(solution)/shard_map/ppermute | solution.py:402
  39.9 0.9 %shard_map.55 = (f32[32,384]{1,0:T(8,128)}, f32[32,384]{1,0:T(8,128)}) custom-call(f32[32,384]{1,0:T(8,128)S(1)} %bitcast.5, bf16[3,384,128]{2,1,0:T(8,128)(2,1)S(1)} %copy-done.1, bf16[512,128]{1,0:T(8,128)(2,1)S(1)} %add_add_fusion.result_ref, bf16[128,128]{1,0:T(8,128)(2,1)S(1)} %slice.14.refs_0_, bf16[128,128]{1,0:T(8,128)(2,1)S(1)} %collective-permute-done.11.refs_1_, ...), custom_call_target="tpu_custom_call" | custom-call | bytes 606208 | tf_op jit(solution)/shard_map/pallas_call | solution.py:358
  (17 shorter events, 0.1 us)
Async XLA Ops:
  0.6 1.0 %copy-start = (bf16[3,384,128]{2,1,0:T(8,128)(2,1)S(1)}, bf16[3,384,128]{2,1,0:T(8,128)(2,1)}, u32[]{:S(2)}) copy-start(bf16[3,384,128]{2,1,0:T(8,128)(2,1)} %factors_ref.3) | copy-start | bytes 884740
  1.6 0.8 %copy-start.2 = (f32[384,32]{0,1:T(8,128)S(1)}, f32[384,32]{0,1:T(8,128)}, u32[]{:S(2)}) copy-start(f32[384,32]{0,1:T(8,128)} %param.5) | copy-start | bytes 147460
  2.4 0.9 %copy-start.4 = (bf16[384,256]{1,0:T(8,128)(2,1)S(1)}, bf16[384,256]{1,0:T(8,128)(2,1)}, u32[]{:S(2)}) copy-start(bf16[384,256]{1,0:T(8,128)(2,1)} %embed_ref.1) | copy-start | bytes 589828
  3.5 1.9 %collective-permute-start.3 = (f32[64,128]{1,0:T(8,128)S(1)}, f32[64,128]{1,0:T(8,128)S(1)}, u32[]{:S(2)}, u32[]{:S(2)}) collective-permute-start(f32[64,128]{1,0:T(8,128)S(1)} %get-tuple-element.23), channel_id=1, source_target_pairs={{0,4},{4,0},{8,12},{12,8},{1,5},{5,1},{9,13},{13,9},{2,6},{6,2},{1... | collective-permute-start | bytes 98312 | tf_op jit(solution)/shard_map/ppermute | solution.py:402
  4.0 12.7 %collective-permute-start.1 = (bf16[960,128]{1,0:T(8,128)(2,1)S(1)}, bf16[960,128]{1,0:T(8,128)(2,1)S(1)}, u32[]{:S(2)}, u32[]{:S(2)}) collective-permute-start(bf16[960,128]{1,0:T(8,128)(2,1)S(1)} %get-tuple-element.16.refs_0_), channel_id=1, source_target_pairs={{3,2},{4,5},{11,10},{12,13},{19,18},{20,21},{27,26},{28,29}} | collective-permute-start | bytes 737288 | tf_op jit(solution)/shard_map/ppermute | solution.py:399
  4.7 12.7 %collective-permute-start = (bf16[960,128]{1,0:T(8,128)(2,1)S(1)}, bf16[960,128]{1,0:T(8,128)(2,1)S(1)}, u32[]{:S(2)}, u32[]{:S(2)}) collective-permute-start(bf16[960,128]{1,0:T(8,128)(2,1)S(1)} %get-tuple-element.16.refs_0_), channel_id=1, source_target_pairs={{1,2},{6,5},{9,10},{14,13},{17,18},{22,21},{25,26},{30,29}} | collective-permute-start | bytes 737288 | tf_op jit(solution)/shard_map/ppermute | solution.py:399
  5.4 8.3 %collective-permute-start.4 = (f32[32,128]{1,0:T(8,128)S(1)}, f32[32,128]{1,0:T(8,128)S(1)}, u32[]{:S(2)}, u32[]{:S(2)}) collective-permute-start(f32[32,128]{1,0:T(8,128)S(1)} %slice.13), channel_id=1, source_target_pairs={{0,8},{4,12},{8,0},{12,4},{1,9},{5,13},{9,1},{13,5},{2,10},{6,14},... | collective-permute-start | bytes 49160 | tf_op jit(solution)/shard_map/ppermute | solution.py:402
  8.0 12.7 %collective-permute-start.2 = (bf16[960,128]{1,0:T(8,128)(2,1)S(1)}, bf16[960,128]{1,0:T(8,128)(2,1)S(1)}, u32[]{:S(2)}, u32[]{:S(2)}) collective-permute-start(bf16[960,128]{1,0:T(8,128)(2,1)S(1)} %get-tuple-element.16.refs_0_), channel_id=1, source_target_pairs={{0,2},{7,5},{8,10},{15,13},{16,18},{23,21},{24,26},{31,29}} | collective-permute-start | bytes 737288 | tf_op jit(solution)/shard_map/ppermute | solution.py:399
  13.8 11.0 %collective-permute-start.7 = (bf16[1344,128]{1,0:T(8,128)(2,1)S(1)}, bf16[1344,128]{1,0:T(8,128)(2,1)S(1)}, u32[]{:S(2)}, u32[]{:S(2)}) collective-permute-start(bf16[1344,128]{1,0:T(8,128)(2,1)S(1)} %shard_map.53.refs_4_), channel_id=1, source_target_pairs={{0,2},{7,5},{8,10},{15,13},{16,18},{23,21},{24,26},{31,29}} | collective-permute-start | bytes 1032200 | tf_op jit(solution)/shard_map/ppermute | solution.py:399
  16.0 8.8 %collective-permute-start.6 = (bf16[1344,128]{1,0:T(8,128)(2,1)S(1)}, bf16[1344,128]{1,0:T(8,128)(2,1)S(1)}, u32[]{:S(2)}, u32[]{:S(2)}) collective-permute-start(bf16[1344,128]{1,0:T(8,128)(2,1)S(1)} %shard_map.53.refs_4_), channel_id=1, source_target_pairs={{3,2},{4,5},{11,10},{12,13},{19,18},{20,21},{27,26},{28,29}} | collective-permute-start | bytes 1032200 | tf_op jit(solution)/shard_map/ppermute | solution.py:399
  16.7 8.1 %collective-permute-start.5 = (bf16[1344,128]{1,0:T(8,128)(2,1)S(1)}, bf16[1344,128]{1,0:T(8,128)(2,1)S(1)}, u32[]{:S(2)}, u32[]{:S(2)}) collective-permute-start(bf16[1344,128]{1,0:T(8,128)(2,1)S(1)} %shard_map.53.refs_4_), channel_id=1, source_target_pairs={{1,2},{6,5},{9,10},{14,13},{17,18},{22,21},{25,26},{30,29}} | collective-permute-start | bytes 1032200 | tf_op jit(solution)/shard_map/ppermute | solution.py:399
  24.8 15.1 %copy-start.1 = (bf16[3,384,128]{2,1,0:T(8,128)(2,1)S(1)}, bf16[3,384,128]{2,1,0:T(8,128)(2,1)}, u32[]{:S(2)}) copy-start(bf16[3,384,128]{2,1,0:T(8,128)(2,1)} %factors_ref.3) | copy-start | bytes 884740
  24.8 15.1 %copy-start.3 = (f32[384,32]{0,1:T(8,128)S(1)}, f32[384,32]{0,1:T(8,128)}, u32[]{:S(2)}) copy-start(f32[384,32]{0,1:T(8,128)} %param.5) | copy-start | bytes 147460
  26.7 9.1 %collective-permute-start.8 = (bf16[512,128]{1,0:T(8,128)(2,1)S(1)}, bf16[512,128]{1,0:T(8,128)(2,1)S(1)}, u32[]{:S(2)}, u32[]{:S(2)}) collective-permute-start(bf16[512,128]{1,0:T(8,128)(2,1)S(1)} %get-tuple-element.25), channel_id=1, source_target_pairs={{2,0},{5,7},{10,8},{13,15},{18,16},{21,23},{26,24},{29,31}} | collective-permute-start | bytes 393224 | tf_op jit(solution)/shard_map/ppermute | solution.py:457
  28.0 7.8 %collective-permute-start.9 = (bf16[512,128]{1,0:T(8,128)(2,1)S(1)}, bf16[512,128]{1,0:T(8,128)(2,1)S(1)}, u32[]{:S(2)}, u32[]{:S(2)}) collective-permute-start(bf16[512,128]{1,0:T(8,128)(2,1)S(1)} %get-tuple-element.26), channel_id=1, source_target_pairs={{2,3},{5,4},{10,11},{13,12},{18,19},{21,20},{26,27},{29,28}} | collective-permute-start | bytes 393224 | tf_op jit(solution)/shard_map/ppermute | solution.py:457
  28.7 7.1 %collective-permute-start.10 = (bf16[512,128]{1,0:T(8,128)(2,1)S(1)}, bf16[512,128]{1,0:T(8,128)(2,1)S(1)}, u32[]{:S(2)}, u32[]{:S(2)}) collective-permute-start(bf16[512,128]{1,0:T(8,128)(2,1)S(1)} %get-tuple-element.27), channel_id=1, source_target_pairs={{2,1},{5,6},{10,9},{13,14},{18,17},{21,22},{26,25},{29,30}} | collective-permute-start | bytes 393224 | tf_op jit(solution)/shard_map/ppermute | solution.py:457
  35.8 3.4 %collective-permute-start.13 = (bf16[128,128]{1,0:T(8,128)(2,1)S(1)}, bf16[128,128]{1,0:T(8,128)(2,1)S(1)}, u32[]{:S(2)}, u32[]{:S(2)}) collective-permute-start(bf16[128,128]{1,0:T(8,128)(2,1)S(1)} %slice.14.refs_0_), channel_id=1, source_target_pairs={{0,12},{4,8},{8,4},{12,0},{1,13},{5,9},{9,5},{13,1},{2,14},{6,10},... | collective-permute-start | bytes 98312 | tf_op jit(solution)/shard_map/ppermute | solution.py:402
  35.9 4.0 %collective-permute-start.12 = (bf16[128,128]{1,0:T(8,128)(2,1)S(1)}, bf16[128,128]{1,0:T(8,128)(2,1)S(1)}, u32[]{:S(2)}, u32[]{:S(2)}) collective-permute-start(bf16[128,128]{1,0:T(8,128)(2,1)S(1)} %slice.14.refs_0_), channel_id=1, source_target_pairs={{0,8},{4,12},{8,0},{12,4},{1,9},{5,13},{9,1},{13,5},{2,10},{6,14},... | collective-permute-start | bytes 98312 | tf_op jit(solution)/shard_map/ppermute | solution.py:402
  36.4 3.5 %collective-permute-start.11 = (bf16[128,128]{1,0:T(8,128)(2,1)S(1)}, bf16[128,128]{1,0:T(8,128)(2,1)S(1)}, u32[]{:S(2)}, u32[]{:S(2)}) collective-permute-start(bf16[128,128]{1,0:T(8,128)(2,1)S(1)} %slice.14.refs_0_), channel_id=1, source_target_pairs={{0,4},{4,0},{8,12},{12,8},{1,5},{5,1},{9,13},{13,9},{2,6},{6,2},{1... | collective-permute-start | bytes 98312 | tf_op jit(solution)/shard_map/ppermute | solution.py:402

commit v5 on v4

--- a/solution.py
+++ b/solution.py
@@ -210,99 +210,119 @@
         at += j + 1
 
 
-def near_kernel(near, shape, *refs):
-    high_ref, image_ref, low_ref = refs[near:]
-    messages = [Message(shape, ref) for ref in refs[:near]]
-    image = [jnp.zeros(image_ref.shape[1:], F32) for _ in range(near)]
-    kern_columns(range(near), messages, high_ref, low_ref)
-    add_products(range(near), high_ref, low_ref, [m.field() for m in messages], image)
-    for s in range(near):
-        image_ref[s] = image[s]
-
-
-def far_kernel(slots, shape, near_image_ref, *refs):
-    high_ref, image_ref, low_ref = refs[slots:]
-    near = near_image_ref.shape[0]
-    messages = [Message(shape, ref) for ref in refs[:slots]]
-    image = [near_image_ref[s] for s in range(near)]
-    image += [jnp.zeros(image_ref.shape[1:], F32) for _ in range(near, slots)]
-    kern_columns(range(near, slots), messages, high_ref, low_ref)
-    add_products(range(near, slots), high_ref, low_ref, [m.field() for m in messages], image)
-    for s in range(slots):
-        image_ref[s] = image[s]
+def near_kernel(near, shape, is_host_ref, *refs):
+    @pl.when(is_host_ref[0] == 1)
+    def _():
+        high_ref, image_ref, low_ref = refs[near:]
+        messages = [Message(shape, ref) for ref in refs[:near]]
+        image = [jnp.zeros(image_ref.shape[1:], F32) for _ in range(near)]
+        kern_columns(range(near), messages, high_ref, low_ref)
+        add_products(range(near), high_ref, low_ref, [m.field() for m in messages], image)
+        for s in range(near):
+            image_ref[s] = image[s]
+
+
+def far_kernel(slots, shape, is_host_ref, near_image_ref, *refs):
+    @pl.when(is_host_ref[0] == 1)
+    def _():
+        high_ref, image_ref, low_ref = refs[slots:]
+        near = near_image_ref.shape[0]
+        messages = [Message(shape, ref) for ref in refs[:slots]]
+        image = [near_image_ref[s] for s in range(near)]
+        image += [jnp.zeros(image_ref.shape[1:], F32) for _ in range(near, slots)]
+        kern_columns(range(near, slots), messages, high_ref, low_ref)
+        add_products(range(near, slots), high_ref, low_ref, [m.field() for m in messages], image)
+        for s in range(slots):
+            image_ref[s] = image[s]
+
+
+def sending_order(slots):
+    count = slots - 1
+    return [1, 0] + list(range(2, count)) if count > 1 else list(range(count))
+
+
+def tail_order(slots):
+    sent = sorted(range(1, slots), key=lambda slot: sending_order(slots)[slot - 1])
+    return [0] + sent[::-1]
 
 
 def main_kernel(slots, shape, is_host_ref, near_high_ref, far_high_ref, image_ref, *refs):
-    messages = [Message(shape, refs[s], refs[slots + s]) for s in range(slots)]
     results = refs[2 * slots :]
-    rows, _, levels, rank, nrhs = shape
-    near = slots - 1
-    mine = is_host_ref[0] == 1
-
-    def put(s, at, value):
-        value = jnp.where(mine, value, jnp.zeros_like(value)) if s == 0 else value
-        results[s][at * nrhs : (at + 1) * nrhs] = value
-
-    def put_halves(s, at, value):
-        high = value.astype(BF16)
-        low = (value - high.astype(F32)).astype(BF16)
-        for k in range(rows // rank):
-            put(s, at + 2 * k, high[:, k * rank : (k + 1) * rank])
-            put(s, at + 2 * k + 1, low[:, k * rank : (k + 1) * rank])
-
-    proj = []
-    for level in range(levels):
-        total = messages[0].proj(level)
-        for message in messages[1:]:
-            total = total + message.proj(level)
-        proj.append(total.astype(BF16))
-    fields = [message.field() for message in messages]
-    field, image, image_b = [], [], []
-    for s in range(slots):
-        halves = fields[s].astype(F32)
-        field.append(halves[:nrhs] + halves[nrhs:])
-        total = image_ref[s] + 0.5 * field[s]
+
+    @pl.when(is_host_ref[0] == 0)
+    def _():
+        results[0][...] = jnp.zeros_like(results[0])
+
+    @pl.when(is_host_ref[0] == 1)
+    def _():
+        order = tail_order(slots)
+        messages = [Message(shape, refs[s], refs[slots + order.index(s)]) for s in range(slots)]
+        rows, _, levels, rank, nrhs = shape
+        near = slots - 1
+
+        def put(s, at, value):
+            results[s][at * nrhs : (at + 1) * nrhs] = value
+
+        def put_halves(s, at, value):
+            high = value.astype(BF16)
+            low = (value - high.astype(F32)).astype(BF16)
+            for k in range(rows // rank):
+                put(s, at + 2 * k, high[:, k * rank : (k + 1) * rank])
+                put(s, at + 2 * k + 1, low[:, k * rank : (k + 1) * rank])
+
+        proj = []
         for level in range(levels):
-            total = total + mm_nt(proj[level], messages[s].factor(level))
-        image.append(total)
-        image_b.append(total.astype(BF16))
-        put_halves(s, levels + 1, total)
-    total = messages[0].project(image_b[0])
-    for s in range(1, slots):
-        total = total + messages[s].project(image_b[s])
-    leaf_norm = jnp.sum(total[:nrhs] * total[:nrhs], axis=1, keepdims=True)
-    for level in range(levels):
-        part = total[level * nrhs : (level + 1) * nrhs].astype(BF16)
+            total = messages[0].proj(level)
+            for message in messages[1:]:
+                total = total + message.proj(level)
+            proj.append(total.astype(BF16))
+        fields = [message.field() for message in messages]
+        field, image, image_b = [], [], []
         for s in range(slots):
-            put(s, level, part)
-    second = [jnp.zeros((nrhs, rows), F32) for _ in range(slots)]
-    add_products(range(near), near_high_ref, None, image_b, second)
-    add_products(range(near, slots), far_high_ref, None, image_b, second)
-    for s in range(slots):
-        put_halves(s, levels + 1 + 2 * (rows // rank), second[s])
-
-    def dots(left, right):
-        total = left[0] * right[0]
+            halves = fields[s].astype(F32)
+            field.append(halves[:nrhs] + halves[nrhs:])
+            total = image_ref[s] + 0.5 * field[s]
+            for level in range(levels):
+                total = total + mm_nt(proj[level], messages[s].factor(level))
+            image.append(total)
+            image_b.append(total.astype(BF16))
+            put_halves(s, levels + 1, total)
+        total = messages[0].project(image_b[0])
         for s in range(1, slots):
-            total = total + left[s] * right[s]
-        return jnp.sum(total, axis=1, keepdims=True)
-
-    scalars = [
-        dots(field, field),
-        dots(field, image),
-        dots(image, image),
-        dots(image, second) + leaf_norm,
-    ]
-    lane = lax.broadcasted_iota(jnp.int32, (nrhs, rank), 1)
-    packed = jnp.zeros((nrhs, rank), F32)
-    for k, value in enumerate(scalars):
-        value = jnp.broadcast_to(value, (nrhs, rank))
-        for piece in range(3):
-            rounded = value.astype(BF16).astype(F32)
-            packed = jnp.where(lane == 3 * k + piece, rounded, packed)
-            value = value - rounded
-    for s in range(slots):
-        put(s, levels, packed.astype(BF16))
+            total = total + messages[s].project(image_b[s])
+        leaf_norm = jnp.sum(total[:nrhs] * total[:nrhs], axis=1, keepdims=True)
+        for level in range(levels):
+            part = total[level * nrhs : (level + 1) * nrhs].astype(BF16)
+            for s in range(slots):
+                put(s, level, part)
+        second = [jnp.zeros((nrhs, rows), F32) for _ in range(slots)]
+        add_products(range(near), near_high_ref, None, image_b, second)
+        add_products(range(near, slots), far_high_ref, None, image_b, second)
+        for s in range(slots):
+            put_halves(s, levels + 1 + 2 * (rows // rank), second[s])
+
+        def dots(left, right):
+            total = left[0] * right[0]
+            for s in range(1, slots):
+                total = total + left[s] * right[s]
+            return jnp.sum(total, axis=1, keepdims=True)
+
+        scalars = [
+            dots(field, field),
+            dots(field, image),
+            dots(image, image),
+            dots(image, second) + leaf_norm,
+        ]
+        lane = lax.broadcasted_iota(jnp.int32, (nrhs, rank), 1)
+        packed = jnp.zeros((nrhs, rank), F32)
+        for k, value in enumerate(scalars):
+            value = jnp.broadcast_to(value, (nrhs, rank))
+            for piece in range(3):
+                rounded = value.astype(BF16).astype(F32)
+                packed = jnp.where(lane == 3 * k + piece, rounded, packed)
+                value = value - rounded
+        for s in range(slots):
+            put(s, levels, packed.astype(BF16))
 
 
 def finish_kernel(leaves, field_ref, factors_ref, result_ref, *refs):
@@ -379,7 +399,11 @@
     def others(leaf):
         sign = 1 if leaf % 2 == 0 else -1
         here = host(leaf)
-        return sorted((z for z in range(inner) if z != here), key=lambda z: (abs(z - here), sign * z))
+        places = [z for z in range(inner) if z != here]
+        places.sort(key=lambda z: (-abs(z - here), sign * z))
+        if leaf % 2:
+            places = places[-1:] + places[:-1]
+        return [places[slot] for slot in sending_order(inner)]
 
     routes = [
         [(leaf * inner + others(leaf)[k], leaf * inner + host(leaf)) for leaf in range(leaves)]
@@ -425,36 +449,37 @@
         aliases={0: 0},
     )
     tails = to_host(second_part)
+    leaf = lax.axis_index("leaf")
+    here = jnp.where(leaf % 2 == 0, host(0), host(1))
+    is_host = (lax.axis_index("inner") == here).astype(jnp.int32).reshape(1)
     near_high, near_image = call(
         functools.partial(near_kernel, near, shape),
         [((held, rows, rows), BF16), ((near, nrhs, rows), F32)],
-        heads[:near],
-        [VMEM] * near,
+        [is_host] + heads[:near],
+        [SMEM] + [VMEM] * near,
         scratch=[pltpu.VMEM((held, rows, rows), BF16)],
         flops=NEAR_FLOPS,
     )
     far_high, image = call(
         functools.partial(far_kernel, inner, shape),
         [((pairs - held, rows, rows), BF16), ((inner, nrhs, rows), F32)],
-        [near_image] + heads,
-        [VMEM] * (1 + inner),
+        [is_host, near_image] + heads,
+        [SMEM] + [VMEM] * (1 + inner),
         scratch=[pltpu.VMEM((pairs - held, rows, rows), BF16)],
         flops=FAR_FLOPS,
     )
-    leaf = lax.axis_index("leaf")
-    here = jnp.where(leaf % 2 == 0, host(0), host(1))
-    is_host = (lax.axis_index("inner") == here).astype(jnp.int32).reshape(1)
     height = (levels + 1 + 4 * (rows // rank)) * nrhs
     results = call(
         functools.partial(main_kernel, inner, shape),
         [((height, rank), BF16)] * inner,
-        [is_host, near_high, far_high, image] + heads + tails,
+        [is_host, near_high, far_high, image] + heads + [tails[s] for s in tail_order(inner)],
         [SMEM] + [VMEM] * (3 + 2 * inner),
         flops=MAIN_FLOPS,
     )
     result = results[0]
-    for value, route in reversed(list(zip(results[1:], routes))):
-        result = result + lax.ppermute(value, axes, [(b, a) for a, b in route])
+    for slot in tail_order(inner)[:0:-1]:
+        route = [(b, a) for a, b in routes[slot - 1]]
+        result = result + lax.ppermute(results[slot], axes, route)
     sums = result[: (levels + 1) * nrhs]
     leaf_sums = [sums] + [over_leaf(sums, m) for m in range(1, leaves)]
     answer, residual = call(

time: 41.3 us -> 39.5 us (0.956)
  Pallas kernels: 8.58 us -> 1.11 us
  waiting for transfers between devices: 10.3 us -> 17.5 us
  starting transfers between devices: 18.3 us -> 16.9 us
    pallas_call x6, Pallas kernels: 8.58 us -> 1.11 us  [call(): pl.pallas_call(kernel, out_shape=[jax.ShapeDtypeStruct(shape, dtype) for...]
    ppermute x3, waiting for transfers between devices: 6.43 us -> 9.41 us  [collected(): result = result + lax.ppermute(results[slot], axes, route)]
    ppermute x6, waiting for transfers between devices: 1.71 us -> 4.38 us  [to_host(): return [value] + [lax.ppermute(value, axes, route) for route in routes]]
    ppermute x5, waiting for transfers between devices: 2.19 us -> 3.74 us  [over_leaf(): return lax.ppermute(value, 'leaf', [(i, i ^ m) for i in range(leaves)])]
    ppermute x5, starting transfers between devices: 5.01 us -> 3.99 us  [over_leaf(): return lax.ppermute(value, 'leaf', [(i, i ^ m) for i in range(leaves)])]
    ppermute x6, starting transfers between devices: 10.6 us -> 10.1 us  [to_host(): return [value] + [lax.ppermute(value, axes, route) for route in routes]]
  transfers between devices with their start and end apart: 14 -> 14, of which waited for: 4 -> 5; matrix products, arithmetic and copies ran while one was open for 0% -> 0% of each run, Pallas kernels for 14% -> 0%
where the time goes in v5:
time: 39.5 us; the launch traced here: 39.1 us
  waiting for transfers between devices  17.5 us (44%)
  starting transfers between devices  16.9 us (43%)
  local copies, waits for them, and re-layouts  2.7 us (7%)
  Pallas kernels  1.11 us (3%)
  between operations  0.84 us (2%)
    ppermute x6, starting transfers between devices, to_host(): return [value] + [lax.ppermute(value, axes, route) for route in routes]  10.1 us
    ppermute x3, waiting for transfers between devices, collected(): result = result + lax.ppermute(results[slot], axes, route)  9.41 us
    ppermute x6, waiting for transfers between devices, to_host(): return [value] + [lax.ppermute(value, axes, route) for route in routes]  4.38 us
    ppermute x5, starting transfers between devices, over_leaf(): return lax.ppermute(value, 'leaf', [(i, i ^ m) for i in range(leaves)])  3.99 us
    ppermute x5, waiting for transfers between devices, over_leaf(): return lax.ppermute(value, 'leaf', [(i, i ^ m) for i in range(leaves)])  3.74 us
    ppermute x3, starting transfers between devices, collected(): result = result + lax.ppermute(results[slot], axes, route)  2.76 us
    unnamed x10, local copies, waits for them, and re-layouts  2.69 us
    pallas_call x6, Pallas kernels, call(): pl.pallas_call(kernel, out_shape=[jax.ShapeDtypeStruct(shape, dtype) for...  1.11 us
  transfers between devices with their start and end apart: 14, of which 5 were waited for; matrix products, arithmetic and copies ran while one was open for 0% of the time, Pallas kernels for 0%

profile of v5, /device:TPU:0, one launch (start us, length us, event | category | flops | bytes accessed | tf_op | source)
XLA Modules:
  0.0 39.1 jit_solution(2102414575464412873)
XLA Ops:
  0.6 0.0 copy-start
  0.6 1.0 %copy-done = bf16[3,384,128]{2,1,0:T(8,128)(2,1)S(1)} copy-done((bf16[3,384,128]{2,1,0:T(8,128)(2,1)S(1)}, bf16[3,384,128]{2,1,0:T(8,128)(2,1)}, u32[]{:S(2)}) %copy-start) | copy-done | bytes 294936
  1.6 0.8 %copy-done.2 = f32[384,32]{0,1:T(8,128)S(1)} copy-done((f32[384,32]{0,1:T(8,128)S(1)}, f32[384,32]{0,1:T(8,128)}, u32[]{:S(2)}) %copy-start.2) | copy-done | bytes 49176
  2.4 0.9 %copy-done.4 = bf16[384,256]{1,0:T(8,128)(2,1)S(1)} copy-done((bf16[384,256]{1,0:T(8,128)(2,1)S(1)}, bf16[384,256]{1,0:T(8,128)(2,1)}, u32[]{:S(2)}) %copy-start.4) | copy-done | bytes 196632
  3.3 0.2 shard_map.50
  3.5 0.5 %collective-permute-start.3 = (f32[64,128]{1,0:T(8,128)S(1)}, f32[64,128]{1,0:T(8,128)S(1)}, u32[]{:S(2)}, u32[]{:S(2)}) collective-permute-start(f32[64,128]{1,0:T(8,128)S(1)} %get-tuple-element.23), channel_id=1, source_target_pairs={{0,4},{4,0},{8,12},{12,8},{1,5},{5,1},{9,13},{13,9},{2,6},{6,2},{1... | collective-permute-start | bytes 98312 | tf_op jit(solution)/shard_map/ppermute | solution.py:426
  4.0 5.5 %collective-permute-start.1 = (bf16[960,128]{1,0:T(8,128)(2,1)S(1)}, bf16[960,128]{1,0:T(8,128)(2,1)S(1)}, u32[]{:S(2)}, u32[]{:S(2)}) collective-permute-start(bf16[960,128]{1,0:T(8,128)(2,1)S(1)} %get-tuple-element.16.refs_0_), channel_id=1, source_target_pairs={{0,2},{4,5},{8,10},{12,13},{16,18},{20,21},{24,26},{28,29}} | collective-permute-start | bytes 737288 | tf_op jit(solution)/shard_map/ppermute | solution.py:423
  9.6 0.7 %collective-permute-start = (bf16[960,128]{1,0:T(8,128)(2,1)S(1)}, bf16[960,128]{1,0:T(8,128)(2,1)S(1)}, u32[]{:S(2)}, u32[]{:S(2)}) collective-permute-start(bf16[960,128]{1,0:T(8,128)(2,1)S(1)} %get-tuple-element.16.refs_0_), channel_id=1, source_target_pairs={{1,2},{7,5},{9,10},{15,13},{17,18},{23,21},{25,26},{31,29}} | collective-permute-start | bytes 737288 | tf_op jit(solution)/shard_map/ppermute | solution.py:423
  10.2 0.0 collective-permute-done.3
  10.3 1.6 %collective-permute-start.4 = (f32[32,128]{1,0:T(8,128)S(1)}, f32[32,128]{1,0:T(8,128)S(1)}, u32[]{:S(2)}, u32[]{:S(2)}) collective-permute-start(f32[32,128]{1,0:T(8,128)S(1)} %slice.13), channel_id=1, source_target_pairs={{0,8},{4,12},{8,0},{12,4},{1,9},{5,13},{9,1},{13,5},{2,10},{6,14},... | collective-permute-start | bytes 49160 | tf_op jit(solution)/shard_map/ppermute | solution.py:426
  11.8 0.7 %collective-permute-start.2 = (bf16[960,128]{1,0:T(8,128)(2,1)S(1)}, bf16[960,128]{1,0:T(8,128)(2,1)S(1)}, u32[]{:S(2)}, u32[]{:S(2)}) collective-permute-start(bf16[960,128]{1,0:T(8,128)(2,1)S(1)} %get-tuple-element.16.refs_0_), channel_id=1, source_target_pairs={{3,2},{6,5},{11,10},{14,13},{19,18},{22,21},{27,26},{30,29}} | collective-permute-start | bytes 737288 | tf_op jit(solution)/shard_map/ppermute | solution.py:423
  12.5 1.6 %collective-permute-done.4 = f32[32,128]{1,0:T(8,128)S(1)} collective-permute-done((f32[32,128]{1,0:T(8,128)S(1)}, f32[32,128]{1,0:T(8,128)S(1)}, u32[]{:S(2)}, u32[]{:S(2)}) %collective-permute-start.4) | collective-permute-done | bytes 16416 | tf_op jit(solution)/shard_map/ppermute | solution.py:426
  14.1 1.9 %collective-permute-start.7 = (bf16[1344,128]{1,0:T(8,128)(2,1)S(1)}, bf16[1344,128]{1,0:T(8,128)(2,1)S(1)}, u32[]{:S(2)}, u32[]{:S(2)}) collective-permute-start(bf16[1344,128]{1,0:T(8,128)(2,1)S(1)} %shard_map.53.refs_4_), channel_id=1, source_target_pairs={{0,2},{4,5},{8,10},{12,13},{16,18},{20,21},{24,26},{28,29}} | collective-permute-start | bytes 1032200 | tf_op jit(solution)/shard_map/ppermute | solution.py:423
  16.0 0.7 %collective-permute-start.6 = (bf16[1344,128]{1,0:T(8,128)(2,1)S(1)}, bf16[1344,128]{1,0:T(8,128)(2,1)S(1)}, u32[]{:S(2)}, u32[]{:S(2)}) collective-permute-start(bf16[1344,128]{1,0:T(8,128)(2,1)S(1)} %shard_map.53.refs_4_), channel_id=1, source_target_pairs={{1,2},{7,5},{9,10},{15,13},{17,18},{23,21},{25,26},{31,29}} | collective-permute-start | bytes 1032200 | tf_op jit(solution)/shard_map/ppermute | solution.py:423
  16.7 0.0 collective-permute-done.1.refs_2_
  16.7 0.7 %collective-permute-start.5 = (bf16[1344,128]{1,0:T(8,128)(2,1)S(1)}, bf16[1344,128]{1,0:T(8,128)(2,1)S(1)}, u32[]{:S(2)}, u32[]{:S(2)}) collective-permute-start(bf16[1344,128]{1,0:T(8,128)(2,1)S(1)} %shard_map.53.refs_4_), channel_id=1, source_target_pairs={{3,2},{6,5},{11,10},{14,13},{19,18},{22,21},{27,26},{30,29}} | collective-permute-start | bytes 1032200 | tf_op jit(solution)/shard_map/ppermute | solution.py:423
  17.4 0.0 collective-permute-done.refs_1_
  17.4 0.0 collective-permute-done.2.refs_3_
  17.5 4.4 %collective-permute-done.7.refs_7_ = bf16[1344,128]{1,0:T(8,128)(2,1)S(1)} collective-permute-done((bf16[1344,128]{1,0:T(8,128)(2,1)S(1)}, bf16[1344,128]{1,0:T(8,128)(2,1)S(1)}, u32[]{:S(2)}, u32[]{:S(2)}) %collective-permute-start.7) | collective-permute-done | bytes 344096 | tf_op jit(solution)/shard_map/ppermute | solution.py:423
  21.9 1.4 %collective-permute-start.8 = (bf16[512,128]{1,0:T(8,128)(2,1)S(1)}, bf16[512,128]{1,0:T(8,128)(2,1)S(1)}, u32[]{:S(2)}, u32[]{:S(2)}) collective-permute-start(bf16[512,128]{1,0:T(8,128)(2,1)S(1)} %get-tuple-element.25), channel_id=1, source_target_pairs={{2,0},{5,4},{10,8},{13,12},{18,16},{21,20},{26,24},{29,28}} | collective-permute-start | bytes 393224 | tf_op jit(solution)/shard_map/ppermute | solution.py:482
  23.3 0.7 %collective-permute-start.9 = (bf16[512,128]{1,0:T(8,128)(2,1)S(1)}, bf16[512,128]{1,0:T(8,128)(2,1)S(1)}, u32[]{:S(2)}, u32[]{:S(2)}) collective-permute-start(bf16[512,128]{1,0:T(8,128)(2,1)S(1)} %get-tuple-element.26), channel_id=1, source_target_pairs={{2,1},{5,7},{10,9},{13,15},{18,17},{21,23},{26,25},{29,31}} | collective-permute-start | bytes 393224 | tf_op jit(solution)/shard_map/ppermute | solution.py:482
  24.0 0.7 %collective-permute-start.10 = (bf16[512,128]{1,0:T(8,128)(2,1)S(1)}, bf16[512,128]{1,0:T(8,128)(2,1)S(1)}, u32[]{:S(2)}, u32[]{:S(2)}) collective-permute-start(bf16[512,128]{1,0:T(8,128)(2,1)S(1)} %get-tuple-element.27), channel_id=1, source_target_pairs={{2,3},{5,6},{10,11},{13,14},{18,19},{21,22},{26,27},{29,30}} | collective-permute-start | bytes 393224 | tf_op jit(solution)/shard_map/ppermute | solution.py:482
  24.7 9.4 %collective-permute-done.8 = bf16[512,128]{1,0:T(8,128)(2,1)S(1)} collective-permute-done((bf16[512,128]{1,0:T(8,128)(2,1)S(1)}, bf16[512,128]{1,0:T(8,128)(2,1)S(1)}, u32[]{:S(2)}, u32[]{:S(2)}) %collective-permute-start.8) | collective-permute-done | bytes 131104 | tf_op jit(solution)/shard_map/ppermute | solution.py:482
  34.1 0.0 collective-permute-done.9
  34.1 0.0 collective-permute-done.10
  34.1 0.1 collective-permute-start.13
  34.2 1.6 %collective-permute-start.12 = (bf16[128,128]{1,0:T(8,128)(2,1)S(1)}, bf16[128,128]{1,0:T(8,128)(2,1)S(1)}, u32[]{:S(2)}, u32[]{:S(2)}) collective-permute-start(bf16[128,128]{1,0:T(8,128)(2,1)S(1)} %slice.14.refs_0_), channel_id=1, source_target_pairs={{0,8},{4,12},{8,0},{12,4},{1,9},{5,13},{9,1},{13,5},{2,10},{6,14},... | collective-permute-start | bytes 98312 | tf_op jit(solution)/shard_map/ppermute | solution.py:426
  35.8 0.3 collective-permute-start.11
  36.1 1.8 %collective-permute-done.13.refs_3_ = bf16[128,128]{1,0:T(8,128)(2,1)S(1)} collective-permute-done((bf16[128,128]{1,0:T(8,128)(2,1)S(1)}, bf16[128,128]{1,0:T(8,128)(2,1)S(1)}, u32[]{:S(2)}, u32[]{:S(2)}) %collective-permute-start.13) | collective-permute-done | bytes 32800 | tf_op jit(solution)/shard_map/ppermute | solution.py:426
  37.8 0.4 %collective-permute-done.12.refs_2_ = bf16[128,128]{1,0:T(8,128)(2,1)S(1)} collective-permute-done((bf16[128,128]{1,0:T(8,128)(2,1)S(1)}, bf16[128,128]{1,0:T(8,128)(2,1)S(1)}, u32[]{:S(2)}, u32[]{:S(2)}) %collective-permute-start.12) | collective-permute-done | bytes 32800 | tf_op jit(solution)/shard_map/ppermute | solution.py:426
  38.2 0.0 collective-permute-done.11.refs_1_
  38.3 0.9 %shard_map.55 = (f32[32,384]{1,0:T(8,128)}, f32[32,384]{1,0:T(8,128)}) custom-call(f32[32,384]{1,0:T(8,128)S(1)} %bitcast.5, bf16[3,384,128]{2,1,0:T(8,128)(2,1)S(1)} %copy-done.1, bf16[512,128]{1,0:T(8,128)(2,1)S(1)} %add_add_fusion.result_ref, bf16[128,128]{1,0:T(8,128)(2,1)S(1)} %slice.14.refs_0_, bf16[128,128]{1,0:T(8,128)(2,1)S(1)} %collective-permute-done.11.refs_1_, ...), custom_call_target="tpu_custom_call" | custom-call | bytes 606208 | tf_op jit(solution)/shard_map/pallas_call | solution.py:378
  (17 shorter events, 0.1 us)
Async XLA Ops:
  0.6 1.0 %copy-start = (bf16[3,384,128]{2,1,0:T(8,128)(2,1)S(1)}, bf16[3,384,128]{2,1,0:T(8,128)(2,1)}, u32[]{:S(2)}) copy-start(bf16[3,384,128]{2,1,0:T(8,128)(2,1)} %factors_ref.3) | copy-start | bytes 884740
  1.6 0.8 %copy-start.2 = (f32[384,32]{0,1:T(8,128)S(1)}, f32[384,32]{0,1:T(8,128)}, u32[]{:S(2)}) copy-start(f32[384,32]{0,1:T(8,128)} %param.5) | copy-start | bytes 147460
  2.4 0.9 %copy-start.4 = (bf16[384,256]{1,0:T(8,128)(2,1)S(1)}, bf16[384,256]{1,0:T(8,128)(2,1)}, u32[]{:S(2)}) copy-start(bf16[384,256]{1,0:T(8,128)(2,1)} %embed_ref.1) | copy-start | bytes 589828
  3.5 6.7 %collective-permute-start.3 = (f32[64,128]{1,0:T(8,128)S(1)}, f32[64,128]{1,0:T(8,128)S(1)}, u32[]{:S(2)}, u32[]{:S(2)}) collective-permute-start(f32[64,128]{1,0:T(8,128)S(1)} %get-tuple-element.23), channel_id=1, source_target_pairs={{0,4},{4,0},{8,12},{12,8},{1,5},{5,1},{9,13},{13,9},{2,6},{6,2},{1... | collective-permute-start | bytes 98312 | tf_op jit(solution)/shard_map/ppermute | solution.py:426
  4.0 12.7 %collective-permute-start.1 = (bf16[960,128]{1,0:T(8,128)(2,1)S(1)}, bf16[960,128]{1,0:T(8,128)(2,1)S(1)}, u32[]{:S(2)}, u32[]{:S(2)}) collective-permute-start(bf16[960,128]{1,0:T(8,128)(2,1)S(1)} %get-tuple-element.16.refs_0_), channel_id=1, source_target_pairs={{0,2},{4,5},{8,10},{12,13},{16,18},{20,21},{24,26},{28,29}} | collective-permute-start | bytes 737288 | tf_op jit(solution)/shard_map/ppermute | solution.py:423
  9.6 7.9 %collective-permute-start = (bf16[960,128]{1,0:T(8,128)(2,1)S(1)}, bf16[960,128]{1,0:T(8,128)(2,1)S(1)}, u32[]{:S(2)}, u32[]{:S(2)}) collective-permute-start(bf16[960,128]{1,0:T(8,128)(2,1)S(1)} %get-tuple-element.16.refs_0_), channel_id=1, source_target_pairs={{1,2},{7,5},{9,10},{15,13},{17,18},{23,21},{25,26},{31,29}} | collective-permute-start | bytes 737288 | tf_op jit(solution)/shard_map/ppermute | solution.py:423
  10.3 3.8 %collective-permute-start.4 = (f32[32,128]{1,0:T(8,128)S(1)}, f32[32,128]{1,0:T(8,128)S(1)}, u32[]{:S(2)}, u32[]{:S(2)}) collective-permute-start(f32[32,128]{1,0:T(8,128)S(1)} %slice.13), channel_id=1, source_target_pairs={{0,8},{4,12},{8,0},{12,4},{1,9},{5,13},{9,1},{13,5},{2,10},{6,14},... | collective-permute-start | bytes 49160 | tf_op jit(solution)/shard_map/ppermute | solution.py:426
  11.8 5.6 %collective-permute-start.2 = (bf16[960,128]{1,0:T(8,128)(2,1)S(1)}, bf16[960,128]{1,0:T(8,128)(2,1)S(1)}, u32[]{:S(2)}, u32[]{:S(2)}) collective-permute-start(bf16[960,128]{1,0:T(8,128)(2,1)S(1)} %get-tuple-element.16.refs_0_), channel_id=1, source_target_pairs={{3,2},{6,5},{11,10},{14,13},{19,18},{22,21},{27,26},{30,29}} | collective-permute-start | bytes 737288 | tf_op jit(solution)/shard_map/ppermute | solution.py:423
  14.1 7.7 %collective-permute-start.7 = (bf16[1344,128]{1,0:T(8,128)(2,1)S(1)}, bf16[1344,128]{1,0:T(8,128)(2,1)S(1)}, u32[]{:S(2)}, u32[]{:S(2)}) collective-permute-start(bf16[1344,128]{1,0:T(8,128)(2,1)S(1)} %shard_map.53.refs_4_), channel_id=1, source_target_pairs={{0,2},{4,5},{8,10},{12,13},{16,18},{20,21},{24,26},{28,29}} | collective-permute-start | bytes 1032200 | tf_op jit(solution)/shard_map/ppermute | solution.py:423
  16.0 5.8 %collective-permute-start.6 = (bf16[1344,128]{1,0:T(8,128)(2,1)S(1)}, bf16[1344,128]{1,0:T(8,128)(2,1)S(1)}, u32[]{:S(2)}, u32[]{:S(2)}) collective-permute-start(bf16[1344,128]{1,0:T(8,128)(2,1)S(1)} %shard_map.53.refs_4_), channel_id=1, source_target_pairs={{1,2},{7,5},{9,10},{15,13},{17,18},{23,21},{25,26},{31,29}} | collective-permute-start | bytes 1032200 | tf_op jit(solution)/shard_map/ppermute | solution.py:423
  16.7 5.1 %collective-permute-start.5 = (bf16[1344,128]{1,0:T(8,128)(2,1)S(1)}, bf16[1344,128]{1,0:T(8,128)(2,1)S(1)}, u32[]{:S(2)}, u32[]{:S(2)}) collective-permute-start(bf16[1344,128]{1,0:T(8,128)(2,1)S(1)} %shard_map.53.refs_4_), channel_id=1, source_target_pairs={{3,2},{6,5},{11,10},{14,13},{19,18},{22,21},{27,26},{30,29}} | collective-permute-start | bytes 1032200 | tf_op jit(solution)/shard_map/ppermute | solution.py:423
  21.8 16.4 %copy-start.1 = (bf16[3,384,128]{2,1,0:T(8,128)(2,1)S(1)}, bf16[3,384,128]{2,1,0:T(8,128)(2,1)}, u32[]{:S(2)}) copy-start(bf16[3,384,128]{2,1,0:T(8,128)(2,1)} %factors_ref.3) | copy-start | bytes 884740
  21.8 16.4 %copy-start.3 = (f32[384,32]{0,1:T(8,128)S(1)}, f32[384,32]{0,1:T(8,128)}, u32[]{:S(2)}) copy-start(f32[384,32]{0,1:T(8,128)} %param.5) | copy-start | bytes 147460
  21.9 12.2 %collective-permute-start.8 = (bf16[512,128]{1,0:T(8,128)(2,1)S(1)}, bf16[512,128]{1,0:T(8,128)(2,1)S(1)}, u32[]{:S(2)}, u32[]{:S(2)}) collective-permute-start(bf16[512,128]{1,0:T(8,128)(2,1)S(1)} %get-tuple-element.25), channel_id=1, source_target_pairs={{2,0},{5,4},{10,8},{13,12},{18,16},{21,20},{26,24},{29,28}} | collective-permute-start | bytes 393224 | tf_op jit(solution)/shard_map/ppermute | solution.py:482
  23.3 10.8 %collective-permute-start.9 = (bf16[512,128]{1,0:T(8,128)(2,1)S(1)}, bf16[512,128]{1,0:T(8,128)(2,1)S(1)}, u32[]{:S(2)}, u32[]{:S(2)}) collective-permute-start(bf16[512,128]{1,0:T(8,128)(2,1)S(1)} %get-tuple-element.26), channel_id=1, source_target_pairs={{2,1},{5,7},{10,9},{13,15},{18,17},{21,23},{26,25},{29,31}} | collective-permute-start | bytes 393224 | tf_op jit(solution)/shard_map/ppermute | solution.py:482
  24.0 10.1 %collective-permute-start.10 = (bf16[512,128]{1,0:T(8,128)(2,1)S(1)}, bf16[512,128]{1,0:T(8,128)(2,1)S(1)}, u32[]{:S(2)}, u32[]{:S(2)}) collective-permute-start(bf16[512,128]{1,0:T(8,128)(2,1)S(1)} %get-tuple-element.27), channel_id=1, source_target_pairs={{2,3},{5,6},{10,11},{13,14},{18,19},{21,22},{26,27},{29,30}} | collective-permute-start | bytes 393224 | tf_op jit(solution)/shard_map/ppermute | solution.py:482
  34.1 3.7 %collective-permute-start.13 = (bf16[128,128]{1,0:T(8,128)(2,1)S(1)}, bf16[128,128]{1,0:T(8,128)(2,1)S(1)}, u32[]{:S(2)}, u32[]{:S(2)}) collective-permute-start(bf16[128,128]{1,0:T(8,128)(2,1)S(1)} %slice.14.refs_0_), channel_id=1, source_target_pairs={{0,12},{4,8},{8,4},{12,0},{1,13},{5,9},{9,5},{13,1},{2,14},{6,10},... | collective-permute-start | bytes 98312 | tf_op jit(solution)/shard_map/ppermute | solution.py:426
  34.2 4.0 %collective-permute-start.12 = (bf16[128,128]{1,0:T(8,128)(2,1)S(1)}, bf16[128,128]{1,0:T(8,128)(2,1)S(1)}, u32[]{:S(2)}, u32[]{:S(2)}) collective-permute-start(bf16[128,128]{1,0:T(8,128)(2,1)S(1)} %slice.14.refs_0_), channel_id=1, source_target_pairs={{0,8},{4,12},{8,0},{12,4},{1,9},{5,13},{9,1},{13,5},{2,10},{6,14},... | collective-permute-start | bytes 98312 | tf_op jit(solution)/shard_map/ppermute | solution.py:426
  35.8 2.5 %collective-permute-start.11 = (bf16[128,128]{1,0:T(8,128)(2,1)S(1)}, bf16[128,128]{1,0:T(8,128)(2,1)S(1)}, u32[]{:S(2)}, u32[]{:S(2)}) collective-permute-start(bf16[128,128]{1,0:T(8,128)(2,1)S(1)} %slice.14.refs_0_), channel_id=1, source_target_pairs={{0,4},{4,0},{8,12},{12,8},{1,5},{5,1},{9,13},{13,9},{2,6},{6,2},{1... | collective-permute-start | bytes 98312 | tf_op jit(solution)/shard_map/ppermute | solution.py:426

commit v6 on v5

--- a/solution.py
+++ b/solution.py
@@ -147,9 +147,6 @@
         halves = self.tail[base : base + 2 * self.nrhs].astype(F32)
         return halves[: self.nrhs] + halves[self.nrhs :]
 
-    def project(self, field):
-        return jnp.concatenate([mm(field, self.factor(l)) for l in range(self.levels)], axis=0)
-
 
 def norms_of(embed):
     scale = 3.0 / LENGTH_SCALE**2
@@ -222,11 +219,12 @@
             image_ref[s] = image[s]
 
 
-def far_kernel(slots, shape, is_host_ref, near_image_ref, *refs):
+def far_kernel(slots, shape, is_host_ref, near_high_ref, near_image_ref, *refs):
     @pl.when(is_host_ref[0] == 1)
     def _():
-        high_ref, image_ref, low_ref = refs[slots:]
+        full_ref, image_ref, high_ref, low_ref = refs[slots:]
         near = near_image_ref.shape[0]
+        rows = shape[0]
         messages = [Message(shape, ref) for ref in refs[:slots]]
         image = [near_image_ref[s] for s in range(near)]
         image += [jnp.zeros(image_ref.shape[1:], F32) for _ in range(near, slots)]
@@ -234,19 +232,15 @@
         add_products(range(near, slots), high_ref, low_ref, [m.field() for m in messages], image)
         for s in range(slots):
             image_ref[s] = image[s]
-
-
-def sending_order(slots):
-    count = slots - 1
-    return [1, 0] + list(range(2, count)) if count > 1 else list(range(count))
-
-
-def tail_order(slots):
-    sent = sorted(range(1, slots), key=lambda slot: sending_order(slots)[slot - 1])
-    return [0] + sent[::-1]
-
-
-def main_kernel(slots, shape, is_host_ref, near_high_ref, far_high_ref, image_ref, *refs):
+        held = near_high_ref.shape[0]
+        for index, (i, j) in enumerate(pairs_of(slots)):
+            block = near_high_ref[index] if index < held else high_ref[index - held]
+            full_ref[i * rows : (i + 1) * rows, j * rows : (j + 1) * rows] = block
+            if i != j:
+                full_ref[j * rows : (j + 1) * rows, i * rows : (i + 1) * rows] = block.T
+
+
+def main_kernel(slots, shape, is_host_ref, full_ref, image_ref, *refs):
     results = refs[2 * slots :]
 
     @pl.when(is_host_ref[0] == 0)
@@ -255,10 +249,8 @@
 
     @pl.when(is_host_ref[0] == 1)
     def _():
-        order = tail_order(slots)
-        messages = [Message(shape, refs[s], refs[slots + order.index(s)]) for s in range(slots)]
+        messages = [Message(shape, refs[s], refs[slots + s]) for s in range(slots)]
         rows, _, levels, rank, nrhs = shape
-        near = slots - 1
 
         def put(s, at, value):
             results[s][at * nrhs : (at + 1) * nrhs] = value
@@ -276,28 +268,31 @@
             for message in messages[1:]:
                 total = total + message.proj(level)
             proj.append(total.astype(BF16))
+        def factors():
+            wide = [
+                jnp.concatenate([message.factor(level) for level in range(levels)], axis=1)
+                for message in messages
+            ]
+            return jnp.concatenate(wide, axis=0)
+
+        low_rank = mm_nt(jnp.concatenate(proj, axis=1), factors())
         fields = [message.field() for message in messages]
         field, image, image_b = [], [], []
         for s in range(slots):
             halves = fields[s].astype(F32)
             field.append(halves[:nrhs] + halves[nrhs:])
-            total = image_ref[s] + 0.5 * field[s]
-            for level in range(levels):
-                total = total + mm_nt(proj[level], messages[s].factor(level))
+            total = image_ref[s] + 0.5 * field[s] + low_rank[:, s * rows : (s + 1) * rows]
             image.append(total)
             image_b.append(total.astype(BF16))
             put_halves(s, levels + 1, total)
-        total = messages[0].project(image_b[0])
-        for s in range(1, slots):
-            total = total + messages[s].project(image_b[s])
-        leaf_norm = jnp.sum(total[:nrhs] * total[:nrhs], axis=1, keepdims=True)
+        total = mm(jnp.concatenate(image_b, axis=1), factors())
+        leaf_norm = jnp.sum(total[:, :rank] * total[:, :rank], axis=1, keepdims=True)
         for level in range(levels):
-            part = total[level * nrhs : (level + 1) * nrhs].astype(BF16)
+            part = total[:, level * rank : (level + 1) * rank].astype(BF16)
             for s in range(slots):
                 put(s, level, part)
-        second = [jnp.zeros((nrhs, rows), F32) for _ in range(slots)]
-        add_products(range(near), near_high_ref, None, image_b, second)
-        add_products(range(near, slots), far_high_ref, None, image_b, second)
+        whole = mm(jnp.concatenate(image_b, axis=1), full_ref[...])
+        second = [whole[:, s * rows : (s + 1) * rows] for s in range(slots)]
         for s in range(slots):
             put_halves(s, levels + 1 + 2 * (rows // rank), second[s])
 
@@ -326,7 +321,7 @@
 
 
 def finish_kernel(leaves, field_ref, factors_ref, result_ref, *refs):
-    sums = refs[:leaves]
+    sums = [refs[-m % leaves] for m in range(leaves)]
     solution_ref, residual_ref = refs[leaves:]
     levels, rows, rank = factors_ref.shape
     nrhs = field_ref.shape[0]
@@ -403,7 +398,7 @@
         places.sort(key=lambda z: (-abs(z - here), sign * z))
         if leaf % 2:
             places = places[-1:] + places[:-1]
-        return [places[slot] for slot in sending_order(inner)]
+        return places
 
     routes = [
         [(leaf * inner + others(leaf)[k], leaf * inner + host(leaf)) for leaf in range(leaves)]
@@ -411,13 +406,6 @@
     ]
 
     axes = ("leaf", "inner")
-
-    def from_host(values):
-        back = [
-            lax.ppermute(value, axes, [(b, a) for a, b in route])
-            for value, route in zip(values[1:], routes)
-        ]
-        return [values[0]] + back
 
     def to_host(value):
         return [value] + [lax.ppermute(value, axes, route) for route in routes]
@@ -433,7 +421,7 @@
     sizes = [((head, rank), BF16), ((tail, rank), BF16)]
     sizes += [((nrhs, rank), F32), (((levels - 1) * nrhs, rank), F32)]
     first_part, second_part, first, upper = call(
-        pack_kernel, sizes, [embed, factors, targets.T], [VMEM] * 3
+        pack_kernel, sizes, [embed, factors, field], [VMEM] * 3
     )
     heads = to_host(first_part)
     proj = [first]
@@ -460,28 +448,28 @@
         scratch=[pltpu.VMEM((held, rows, rows), BF16)],
         flops=NEAR_FLOPS,
     )
-    far_high, image = call(
+    full, image = call(
         functools.partial(far_kernel, inner, shape),
-        [((pairs - held, rows, rows), BF16), ((inner, nrhs, rows), F32)],
-        [is_host, near_image] + heads,
-        [SMEM] + [VMEM] * (1 + inner),
-        scratch=[pltpu.VMEM((pairs - held, rows, rows), BF16)],
+        [((inner * rows, inner * rows), BF16), ((inner, nrhs, rows), F32)],
+        [is_host, near_high, near_image] + heads,
+        [SMEM] + [VMEM] * (2 + inner),
+        scratch=[pltpu.VMEM((pairs - held, rows, rows), BF16)] * 2,
         flops=FAR_FLOPS,
     )
     height = (levels + 1 + 4 * (rows // rank)) * nrhs
     results = call(
         functools.partial(main_kernel, inner, shape),
         [((height, rank), BF16)] * inner,
-        [is_host, near_high, far_high, image] + heads + [tails[s] for s in tail_order(inner)],
-        [SMEM] + [VMEM] * (3 + 2 * inner),
+        [is_host, full, image] + heads + tails,
+        [SMEM] + [VMEM] * (2 + 2 * inner),
         flops=MAIN_FLOPS,
     )
     result = results[0]
-    for slot in tail_order(inner)[:0:-1]:
+    for slot in [*range(2, inner), 1][: inner - 1]:
         route = [(b, a) for a, b in routes[slot - 1]]
         result = result + lax.ppermute(results[slot], axes, route)
     sums = result[: (levels + 1) * nrhs]
-    leaf_sums = [sums] + [over_leaf(sums, m) for m in range(1, leaves)]
+    leaf_sums = [sums] + [over_leaf(sums, m) for m in range(leaves - 1, 0, -1)]
     answer, residual = call(
         functools.partial(finish_kernel, leaves),
         [((nrhs, rows), F32)] * 2,
@@ -492,7 +480,9 @@
 
 
 def on_device(embed, factors, targets):
-    if embed.shape[0] * lax.axis_size("inner") <= FAST_LEAF:
+    _, rows, rank = factors.shape
+    whole = rows % rank == 0 and embed.shape[1] % rank == 0
+    if whole and rows * lax.axis_size("inner") <= FAST_LEAF:
         return collected(embed, factors, targets)
     return stepwise(embed, factors, targets)
 

time: 39.5 us -> 39 us (0.987)
  no operation moved by 1% of the time
where the time goes in v6:
time: 39 us; the launch traced here: 38.7 us
  waiting for transfers between devices  17.2 us (44%)
  starting transfers between devices  16.8 us (43%)
  local copies, waits for them, and re-layouts  2.7 us (7%)
  Pallas kernels  1.1 us (3%)
  between operations  0.85 us (2%)
    ppermute x6, starting transfers between devices, to_host(): return [value] + [lax.ppermute(value, axes, route) for route in routes]  10.1 us
    ppermute x3, waiting for transfers between devices, collected(): result = result + lax.ppermute(results[slot], axes, route)  9.15 us
    ppermute x6, waiting for transfers between devices, to_host(): return [value] + [lax.ppermute(value, axes, route) for route in routes]  4.35 us
    ppermute x5, starting transfers between devices, over_leaf(): return lax.ppermute(value, 'leaf', [(i, i ^ m) for i in range(leaves)])  3.99 us
    ppermute x5, waiting for transfers between devices, over_leaf(): return lax.ppermute(value, 'leaf', [(i, i ^ m) for i in range(leaves)])  3.74 us
    unnamed x10, local copies, waits for them, and re-layouts  2.69 us
    ppermute x3, starting transfers between devices, collected(): result = result + lax.ppermute(results[slot], axes, route)  2.63 us
    pallas_call x6, Pallas kernels, call(): pl.pallas_call(kernel, out_shape=[jax.ShapeDtypeStruct(shape, dtype) for...  1.1 us
  transfers between devices with their start and end apart: 14, of which 5 were waited for; matrix products, arithmetic and copies ran while one was open for 0% of the time, Pallas kernels for 0%

profile of v6, /device:TPU:0, one launch (start us, length us, event | category | flops | bytes accessed | tf_op | source)
XLA Modules:
  0.0 38.7 jit_solution(3817599974904793522)
XLA Ops:
  0.6 0.0 copy-start
  0.6 1.0 %copy-done = bf16[3,384,128]{2,1,0:T(8,128)(2,1)S(1)} copy-done((bf16[3,384,128]{2,1,0:T(8,128)(2,1)S(1)}, bf16[3,384,128]{2,1,0:T(8,128)(2,1)}, u32[]{:S(2)}) %copy-start) | copy-done | bytes 294936
  1.6 0.8 %copy-done.2 = f32[384,32]{0,1:T(8,128)S(1)} copy-done((f32[384,32]{0,1:T(8,128)S(1)}, f32[384,32]{0,1:T(8,128)}, u32[]{:S(2)}) %copy-start.2) | copy-done | bytes 49176
  2.4 0.9 %copy-done.4 = bf16[384,256]{1,0:T(8,128)(2,1)S(1)} copy-done((bf16[384,256]{1,0:T(8,128)(2,1)S(1)}, bf16[384,256]{1,0:T(8,128)(2,1)}, u32[]{:S(2)}) %copy-start.4) | copy-done | bytes 196632
  3.3 0.2 shard_map.50
  3.5 0.5 %collective-permute-start.3 = (f32[64,128]{1,0:T(8,128)S(1)}, f32[64,128]{1,0:T(8,128)S(1)}, u32[]{:S(2)}, u32[]{:S(2)}) collective-permute-start(f32[64,128]{1,0:T(8,128)S(1)} %get-tuple-element.23), channel_id=1, source_target_pairs={{0,4},{4,0},{8,12},{12,8},{1,5},{5,1},{9,13},{13,9},{2,6},{6,2},{1... | collective-permute-start | bytes 98312 | tf_op jit(solution)/shard_map/ppermute | solution.py:414
  4.0 5.5 %collective-permute-start = (bf16[960,128]{1,0:T(8,128)(2,1)S(1)}, bf16[960,128]{1,0:T(8,128)(2,1)S(1)}, u32[]{:S(2)}, u32[]{:S(2)}) collective-permute-start(bf16[960,128]{1,0:T(8,128)(2,1)S(1)} %get-tuple-element.16.refs_0_), channel_id=1, source_target_pairs={{0,2},{4,5},{8,10},{12,13},{16,18},{20,21},{24,26},{28,29}} | collective-permute-start | bytes 737288 | tf_op jit(solution)/shard_map/ppermute | solution.py:411
  9.6 0.7 %collective-permute-start.1 = (bf16[960,128]{1,0:T(8,128)(2,1)S(1)}, bf16[960,128]{1,0:T(8,128)(2,1)S(1)}, u32[]{:S(2)}, u32[]{:S(2)}) collective-permute-start(bf16[960,128]{1,0:T(8,128)(2,1)S(1)} %get-tuple-element.16.refs_0_), channel_id=1, source_target_pairs={{1,2},{7,5},{9,10},{15,13},{17,18},{23,21},{25,26},{31,29}} | collective-permute-start | bytes 737288 | tf_op jit(solution)/shard_map/ppermute | solution.py:411
  10.2 0.0 collective-permute-done.3
  10.3 1.6 %collective-permute-start.4 = (f32[32,128]{1,0:T(8,128)S(1)}, f32[32,128]{1,0:T(8,128)S(1)}, u32[]{:S(2)}, u32[]{:S(2)}) collective-permute-start(f32[32,128]{1,0:T(8,128)S(1)} %slice.13), channel_id=1, source_target_pairs={{0,8},{4,12},{8,0},{12,4},{1,9},{5,13},{9,1},{13,5},{2,10},{6,14},... | collective-permute-start | bytes 49160 | tf_op jit(solution)/shard_map/ppermute | solution.py:414
  11.8 0.7 %collective-permute-start.2 = (bf16[960,128]{1,0:T(8,128)(2,1)S(1)}, bf16[960,128]{1,0:T(8,128)(2,1)S(1)}, u32[]{:S(2)}, u32[]{:S(2)}) collective-permute-start(bf16[960,128]{1,0:T(8,128)(2,1)S(1)} %get-tuple-element.16.refs_0_), channel_id=1, source_target_pairs={{3,2},{6,5},{11,10},{14,13},{19,18},{22,21},{27,26},{30,29}} | collective-permute-start | bytes 737288 | tf_op jit(solution)/shard_map/ppermute | solution.py:411
  12.5 1.6 %collective-permute-done.4 = f32[32,128]{1,0:T(8,128)S(1)} collective-permute-done((f32[32,128]{1,0:T(8,128)S(1)}, f32[32,128]{1,0:T(8,128)S(1)}, u32[]{:S(2)}, u32[]{:S(2)}) %collective-permute-start.4) | collective-permute-done | bytes 16416 | tf_op jit(solution)/shard_map/ppermute | solution.py:414
  14.1 1.9 %collective-permute-start.5 = (bf16[1344,128]{1,0:T(8,128)(2,1)S(1)}, bf16[1344,128]{1,0:T(8,128)(2,1)S(1)}, u32[]{:S(2)}, u32[]{:S(2)}) collective-permute-start(bf16[1344,128]{1,0:T(8,128)(2,1)S(1)} %shard_map.53.refs_4_), channel_id=1, source_target_pairs={{0,2},{4,5},{8,10},{12,13},{16,18},{20,21},{24,26},{28,29}} | collective-permute-start | bytes 1032200 | tf_op jit(solution)/shard_map/ppermute | solution.py:411
  16.0 0.7 %collective-permute-start.6 = (bf16[1344,128]{1,0:T(8,128)(2,1)S(1)}, bf16[1344,128]{1,0:T(8,128)(2,1)S(1)}, u32[]{:S(2)}, u32[]{:S(2)}) collective-permute-start(bf16[1344,128]{1,0:T(8,128)(2,1)S(1)} %shard_map.53.refs_4_), channel_id=1, source_target_pairs={{1,2},{7,5},{9,10},{15,13},{17,18},{23,21},{25,26},{31,29}} | collective-permute-start | bytes 1032200 | tf_op jit(solution)/shard_map/ppermute | solution.py:411
  16.7 0.0 collective-permute-done.refs_1_
  16.7 0.7 %collective-permute-start.7 = (bf16[1344,128]{1,0:T(8,128)(2,1)S(1)}, bf16[1344,128]{1,0:T(8,128)(2,1)S(1)}, u32[]{:S(2)}, u32[]{:S(2)}) collective-permute-start(bf16[1344,128]{1,0:T(8,128)(2,1)S(1)} %shard_map.53.refs_4_), channel_id=1, source_target_pairs={{3,2},{6,5},{11,10},{14,13},{19,18},{22,21},{27,26},{30,29}} | collective-permute-start | bytes 1032200 | tf_op jit(solution)/shard_map/ppermute | solution.py:411
  17.4 0.0 collective-permute-done.1.refs_2_
  17.4 0.0 collective-permute-done.2.refs_3_
  17.5 0.0 copy-start.1
  17.5 0.0 copy-start.3
  17.5 4.3 %collective-permute-done.5.refs_5_ = bf16[1344,128]{1,0:T(8,128)(2,1)S(1)} collective-permute-done((bf16[1344,128]{1,0:T(8,128)(2,1)S(1)}, bf16[1344,128]{1,0:T(8,128)(2,1)S(1)}, u32[]{:S(2)}, u32[]{:S(2)}) %collective-permute-start.5) | collective-permute-done | bytes 344096 | tf_op jit(solution)/shard_map/ppermute | solution.py:411
  21.8 0.0 collective-permute-done.6.refs_6_
  21.9 1.3 %collective-permute-start.10 = (bf16[512,128]{1,0:T(8,128)(2,1)S(1)}, bf16[512,128]{1,0:T(8,128)(2,1)S(1)}, u32[]{:S(2)}, u32[]{:S(2)}) collective-permute-start(bf16[512,128]{1,0:T(8,128)(2,1)S(1)} %get-tuple-element.27), channel_id=1, source_target_pairs={{2,0},{5,4},{10,8},{13,12},{18,16},{21,20},{26,24},{29,28}} | collective-permute-start | bytes 393224 | tf_op jit(solution)/shard_map/ppermute | solution.py:470
  23.2 0.7 %collective-permute-start.8 = (bf16[512,128]{1,0:T(8,128)(2,1)S(1)}, bf16[512,128]{1,0:T(8,128)(2,1)S(1)}, u32[]{:S(2)}, u32[]{:S(2)}) collective-permute-start(bf16[512,128]{1,0:T(8,128)(2,1)S(1)} %get-tuple-element.25), channel_id=1, source_target_pairs={{2,1},{5,7},{10,9},{13,15},{18,17},{21,23},{26,25},{29,31}} | collective-permute-start | bytes 393224 | tf_op jit(solution)/shard_map/ppermute | solution.py:470
  23.8 0.7 %collective-permute-start.9 = (bf16[512,128]{1,0:T(8,128)(2,1)S(1)}, bf16[512,128]{1,0:T(8,128)(2,1)S(1)}, u32[]{:S(2)}, u32[]{:S(2)}) collective-permute-start(bf16[512,128]{1,0:T(8,128)(2,1)S(1)} %get-tuple-element.26), channel_id=1, source_target_pairs={{2,3},{5,6},{10,11},{13,14},{18,19},{21,22},{26,27},{29,30}} | collective-permute-start | bytes 393224 | tf_op jit(solution)/shard_map/ppermute | solution.py:470
  24.5 9.1 %collective-permute-done.10 = bf16[512,128]{1,0:T(8,128)(2,1)S(1)} collective-permute-done((bf16[512,128]{1,0:T(8,128)(2,1)S(1)}, bf16[512,128]{1,0:T(8,128)(2,1)S(1)}, u32[]{:S(2)}, u32[]{:S(2)}) %collective-permute-start.10) | collective-permute-done | bytes 131104 | tf_op jit(solution)/shard_map/ppermute | solution.py:470
  33.7 0.1 collective-permute-start.11
  33.8 1.6 %collective-permute-start.12 = (bf16[128,128]{1,0:T(8,128)(2,1)S(1)}, bf16[128,128]{1,0:T(8,128)(2,1)S(1)}, u32[]{:S(2)}, u32[]{:S(2)}) collective-permute-start(bf16[128,128]{1,0:T(8,128)(2,1)S(1)} %slice.14.refs_0_), channel_id=1, source_target_pairs={{0,8},{4,12},{8,0},{12,4},{1,9},{5,13},{9,1},{13,5},{2,10},{6,14},... | collective-permute-start | bytes 98312 | tf_op jit(solution)/shard_map/ppermute | solution.py:414
  35.4 0.3 collective-permute-start.13
  35.6 1.8 %collective-permute-done.11.refs_1_ = bf16[128,128]{1,0:T(8,128)(2,1)S(1)} collective-permute-done((bf16[128,128]{1,0:T(8,128)(2,1)S(1)}, bf16[128,128]{1,0:T(8,128)(2,1)S(1)}, u32[]{:S(2)}, u32[]{:S(2)}) %collective-permute-start.11) | collective-permute-done | bytes 32800 | tf_op jit(solution)/shard_map/ppermute | solution.py:414
  37.4 0.4 %collective-permute-done.12.refs_2_ = bf16[128,128]{1,0:T(8,128)(2,1)S(1)} collective-permute-done((bf16[128,128]{1,0:T(8,128)(2,1)S(1)}, bf16[128,128]{1,0:T(8,128)(2,1)S(1)}, u32[]{:S(2)}, u32[]{:S(2)}) %collective-permute-start.12) | collective-permute-done | bytes 32800 | tf_op jit(solution)/shard_map/ppermute | solution.py:414
  37.8 0.9 %shard_map.55 = (f32[32,384]{1,0:T(8,128)}, f32[32,384]{1,0:T(8,128)}) custom-call(f32[32,384]{1,0:T(8,128)S(1)} %bitcast.5, bf16[3,384,128]{2,1,0:T(8,128)(2,1)S(1)} %copy-done.1, bf16[512,128]{1,0:T(8,128)(2,1)S(1)} %add_add_fusion.result_ref, bf16[128,128]{1,0:T(8,128)(2,1)S(1)} %slice.14.refs_0_, bf16[128,128]{1,0:T(8,128)(2,1)S(1)} %collective-permute-done.11.refs_1_, ...), custom_call_target="tpu_custom_call" | custom-call | bytes 606208 | tf_op jit(solution)/shard_map/pallas_call | solution.py:373
  (17 shorter events, 0.1 us)
Async XLA Ops:
  0.6 1.0 %copy-start = (bf16[3,384,128]{2,1,0:T(8,128)(2,1)S(1)}, bf16[3,384,128]{2,1,0:T(8,128)(2,1)}, u32[]{:S(2)}) copy-start(bf16[3,384,128]{2,1,0:T(8,128)(2,1)} %factors_ref.3) | copy-start | bytes 884740
  1.6 0.8 %copy-start.2 = (f32[384,32]{0,1:T(8,128)S(1)}, f32[384,32]{0,1:T(8,128)}, u32[]{:S(2)}) copy-start(f32[384,32]{0,1:T(8,128)} %param.5) | copy-start | bytes 147460
  2.4 0.9 %copy-start.4 = (bf16[384,256]{1,0:T(8,128)(2,1)S(1)}, bf16[384,256]{1,0:T(8,128)(2,1)}, u32[]{:S(2)}) copy-start(bf16[384,256]{1,0:T(8,128)(2,1)} %embed_ref.1) | copy-start | bytes 589828
  3.5 6.7 %collective-permute-start.3 = (f32[64,128]{1,0:T(8,128)S(1)}, f32[64,128]{1,0:T(8,128)S(1)}, u32[]{:S(2)}, u32[]{:S(2)}) collective-permute-start(f32[64,128]{1,0:T(8,128)S(1)} %get-tuple-element.23), channel_id=1, source_target_pairs={{0,4},{4,0},{8,12},{12,8},{1,5},{5,1},{9,13},{13,9},{2,6},{6,2},{1... | collective-permute-start | bytes 98312 | tf_op jit(solution)/shard_map/ppermute | solution.py:414
  4.0 12.7 %collective-permute-start = (bf16[960,128]{1,0:T(8,128)(2,1)S(1)}, bf16[960,128]{1,0:T(8,128)(2,1)S(1)}, u32[]{:S(2)}, u32[]{:S(2)}) collective-permute-start(bf16[960,128]{1,0:T(8,128)(2,1)S(1)} %get-tuple-element.16.refs_0_), channel_id=1, source_target_pairs={{0,2},{4,5},{8,10},{12,13},{16,18},{20,21},{24,26},{28,29}} | collective-permute-start | bytes 737288 | tf_op jit(solution)/shard_map/ppermute | solution.py:411
  9.6 7.9 %collective-permute-start.1 = (bf16[960,128]{1,0:T(8,128)(2,1)S(1)}, bf16[960,128]{1,0:T(8,128)(2,1)S(1)}, u32[]{:S(2)}, u32[]{:S(2)}) collective-permute-start(bf16[960,128]{1,0:T(8,128)(2,1)S(1)} %get-tuple-element.16.refs_0_), channel_id=1, source_target_pairs={{1,2},{7,5},{9,10},{15,13},{17,18},{23,21},{25,26},{31,29}} | collective-permute-start | bytes 737288 | tf_op jit(solution)/shard_map/ppermute | solution.py:411
  10.3 3.8 %collective-permute-start.4 = (f32[32,128]{1,0:T(8,128)S(1)}, f32[32,128]{1,0:T(8,128)S(1)}, u32[]{:S(2)}, u32[]{:S(2)}) collective-permute-start(f32[32,128]{1,0:T(8,128)S(1)} %slice.13), channel_id=1, source_target_pairs={{0,8},{4,12},{8,0},{12,4},{1,9},{5,13},{9,1},{13,5},{2,10},{6,14},... | collective-permute-start | bytes 49160 | tf_op jit(solution)/shard_map/ppermute | solution.py:414
  11.8 5.6 %collective-permute-start.2 = (bf16[960,128]{1,0:T(8,128)(2,1)S(1)}, bf16[960,128]{1,0:T(8,128)(2,1)S(1)}, u32[]{:S(2)}, u32[]{:S(2)}) collective-permute-start(bf16[960,128]{1,0:T(8,128)(2,1)S(1)} %get-tuple-element.16.refs_0_), channel_id=1, source_target_pairs={{3,2},{6,5},{11,10},{14,13},{19,18},{22,21},{27,26},{30,29}} | collective-permute-start | bytes 737288 | tf_op jit(solution)/shard_map/ppermute | solution.py:411
  14.1 7.7 %collective-permute-start.5 = (bf16[1344,128]{1,0:T(8,128)(2,1)S(1)}, bf16[1344,128]{1,0:T(8,128)(2,1)S(1)}, u32[]{:S(2)}, u32[]{:S(2)}) collective-permute-start(bf16[1344,128]{1,0:T(8,128)(2,1)S(1)} %shard_map.53.refs_4_), channel_id=1, source_target_pairs={{0,2},{4,5},{8,10},{12,13},{16,18},{20,21},{24,26},{28,29}} | collective-permute-start | bytes 1032200 | tf_op jit(solution)/shard_map/ppermute | solution.py:411
  16.0 5.8 %collective-permute-start.6 = (bf16[1344,128]{1,0:T(8,128)(2,1)S(1)}, bf16[1344,128]{1,0:T(8,128)(2,1)S(1)}, u32[]{:S(2)}, u32[]{:S(2)}) collective-permute-start(bf16[1344,128]{1,0:T(8,128)(2,1)S(1)} %shard_map.53.refs_4_), channel_id=1, source_target_pairs={{1,2},{7,5},{9,10},{15,13},{17,18},{23,21},{25,26},{31,29}} | collective-permute-start | bytes 1032200 | tf_op jit(solution)/shard_map/ppermute | solution.py:411
  16.7 5.1 %collective-permute-start.7 = (bf16[1344,128]{1,0:T(8,128)(2,1)S(1)}, bf16[1344,128]{1,0:T(8,128)(2,1)S(1)}, u32[]{:S(2)}, u32[]{:S(2)}) collective-permute-start(bf16[1344,128]{1,0:T(8,128)(2,1)S(1)} %shard_map.53.refs_4_), channel_id=1, source_target_pairs={{3,2},{6,5},{11,10},{14,13},{19,18},{22,21},{27,26},{30,29}} | collective-permute-start | bytes 1032200 | tf_op jit(solution)/shard_map/ppermute | solution.py:411
  17.5 20.4 %copy-start.1 = (bf16[3,384,128]{2,1,0:T(8,128)(2,1)S(1)}, bf16[3,384,128]{2,1,0:T(8,128)(2,1)}, u32[]{:S(2)}) copy-start(bf16[3,384,128]{2,1,0:T(8,128)(2,1)} %factors_ref.3) | copy-start | bytes 884740
  17.5 20.4 %copy-start.3 = (f32[384,32]{0,1:T(8,128)S(1)}, f32[384,32]{0,1:T(8,128)}, u32[]{:S(2)}) copy-start(f32[384,32]{0,1:T(8,128)} %param.5) | copy-start | bytes 147460
  21.9 11.8 %collective-permute-start.10 = (bf16[512,128]{1,0:T(8,128)(2,1)S(1)}, bf16[512,128]{1,0:T(8,128)(2,1)S(1)}, u32[]{:S(2)}, u32[]{:S(2)}) collective-permute-start(bf16[512,128]{1,0:T(8,128)(2,1)S(1)} %get-tuple-element.27), channel_id=1, source_target_pairs={{2,0},{5,4},{10,8},{13,12},{18,16},{21,20},{26,24},{29,28}} | collective-permute-start | bytes 393224 | tf_op jit(solution)/shard_map/ppermute | solution.py:470
  23.2 10.5 %collective-permute-start.8 = (bf16[512,128]{1,0:T(8,128)(2,1)S(1)}, bf16[512,128]{1,0:T(8,128)(2,1)S(1)}, u32[]{:S(2)}, u32[]{:S(2)}) collective-permute-start(bf16[512,128]{1,0:T(8,128)(2,1)S(1)} %get-tuple-element.25), channel_id=1, source_target_pairs={{2,1},{5,7},{10,9},{13,15},{18,17},{21,23},{26,25},{29,31}} | collective-permute-start | bytes 393224 | tf_op jit(solution)/shard_map/ppermute | solution.py:470
  23.8 9.8 %collective-permute-start.9 = (bf16[512,128]{1,0:T(8,128)(2,1)S(1)}, bf16[512,128]{1,0:T(8,128)(2,1)S(1)}, u32[]{:S(2)}, u32[]{:S(2)}) collective-permute-start(bf16[512,128]{1,0:T(8,128)(2,1)S(1)} %get-tuple-element.26), channel_id=1, source_target_pairs={{2,3},{5,6},{10,11},{13,14},{18,19},{21,22},{26,27},{29,30}} | collective-permute-start | bytes 393224 | tf_op jit(solution)/shard_map/ppermute | solution.py:470
  33.7 3.7 %collective-permute-start.11 = (bf16[128,128]{1,0:T(8,128)(2,1)S(1)}, bf16[128,128]{1,0:T(8,128)(2,1)S(1)}, u32[]{:S(2)}, u32[]{:S(2)}) collective-permute-start(bf16[128,128]{1,0:T(8,128)(2,1)S(1)} %slice.14.refs_0_), channel_id=1, source_target_pairs={{0,12},{4,8},{8,4},{12,0},{1,13},{5,9},{9,5},{13,1},{2,14},{6,10},... | collective-permute-start | bytes 98312 | tf_op jit(solution)/shard_map/ppermute | solution.py:414
  33.8 4.0 %collective-permute-start.12 = (bf16[128,128]{1,0:T(8,128)(2,1)S(1)}, bf16[128,128]{1,0:T(8,128)(2,1)S(1)}, u32[]{:S(2)}, u32[]{:S(2)}) collective-permute-start(bf16[128,128]{1,0:T(8,128)(2,1)S(1)} %slice.14.refs_0_), channel_id=1, source_target_pairs={{0,8},{4,12},{8,0},{12,4},{1,9},{5,13},{9,1},{13,5},{2,10},{6,14},... | collective-permute-start | bytes 98312 | tf_op jit(solution)/shard_map/ppermute | solution.py:414
  35.4 2.5 %collective-permute-start.13 = (bf16[128,128]{1,0:T(8,128)(2,1)S(1)}, bf16[128,128]{1,0:T(8,128)(2,1)S(1)}, u32[]{:S(2)}, u32[]{:S(2)}) collective-permute-start(bf16[128,128]{1,0:T(8,128)(2,1)S(1)} %slice.14.refs_0_), channel_id=1, source_target_pairs={{0,4},{4,0},{8,12},{12,8},{1,5},{5,1},{9,13},{13,9},{2,6},{6,2},{1... | collective-permute-start | bytes 98312 | tf_op jit(solution)/shard_map/ppermute | solution.py:414

commit v7 on v6

--- a/solution.py
+++ b/solution.py
@@ -241,7 +241,7 @@
 
 
 def main_kernel(slots, shape, is_host_ref, full_ref, image_ref, *refs):
-    results = refs[2 * slots :]
+    *results, early_ref = refs[2 * slots :]
 
     @pl.when(is_host_ref[0] == 0)
     def _():
@@ -253,6 +253,10 @@
         rows, _, levels, rank, nrhs = shape
 
         def put(s, at, value):
+            if s == slots - 1 and at <= levels:
+                early_ref[at * nrhs : (at + 1) * nrhs] = value
+                return
+            at = at - levels - 1 if s == slots - 1 else at
             results[s][at * nrhs : (at + 1) * nrhs] = value
 
         def put_halves(s, at, value):
@@ -335,12 +339,12 @@
             pieces.append(piece[:nrhs] + piece[nrhs:])
         return jnp.concatenate(pieces, axis=1)
 
-    image = halves(levels + 1)
-    second = halves(levels + 1 + 2 * (rows // rank)) + 0.5 * image
+    image = halves(0)
+    second = halves(2 * (rows // rank)) + 0.5 * image
     lane = lax.broadcasted_iota(jnp.int32, (nrhs, rank), 1)
     packed = sums[0][levels * nrhs :].astype(F32)
     for m in range(1, leaves):
-        packed = packed + sums[m][levels * nrhs :].astype(F32)
+        packed = packed + sums[m][(levels - 1) * nrhs :].astype(F32)
 
     def scalar(k):
         inside = (lane >= 3 * k) & (lane < 3 * k + 3)
@@ -350,8 +354,9 @@
     wu = wu + 0.5 * ww
     for level in range(levels):
         nodes = {}
-        for m in range(leaves):
-            value = sums[m][level * nrhs : (level + 1) * nrhs].astype(F32)
+        for m in range(leaves if level else 1):
+            at = level if m == 0 else level - 1
+            value = sums[m][at * nrhs : (at + 1) * nrhs].astype(F32)
             node = m >> level
             nodes[node] = nodes[node] + value if node in nodes else value
         second = second + mm_nt(nodes[0].astype(BF16), factors_ref[level])
@@ -457,19 +462,29 @@
         flops=FAR_FLOPS,
     )
     height = (levels + 1 + 4 * (rows // rank)) * nrhs
-    results = call(
+    above = (levels + 1) * nrhs
+    heights = [height] * (inner - 1) + [height - above]
+    *results, early = call(
         functools.partial(main_kernel, inner, shape),
-        [((height, rank), BF16)] * inner,
+        [((size, rank), BF16) for size in heights + [above]],
         [is_host, full, image] + heads + tails,
         [SMEM] + [VMEM] * (2 + 2 * inner),
         flops=MAIN_FLOPS,
     )
-    result = results[0]
-    for slot in [*range(2, inner), 1][: inner - 1]:
-        route = [(b, a) for a, b in routes[slot - 1]]
-        result = result + lax.ppermute(results[slot], axes, route)
-    sums = result[: (levels + 1) * nrhs]
-    leaf_sums = [sums] + [over_leaf(sums, m) for m in range(leaves - 1, 0, -1)]
+
+    def from_host(value, slot):
+        return lax.ppermute(value, axes, [(b, a) for a, b in routes[slot - 1]])
+
+    back = [from_host(results[slot], slot) for slot in range(1, inner - 1)]
+    sums = results[0][:above]
+    for value in back:
+        sums = sums + value[:above]
+    sums = sums + from_host(early, inner - 1)
+    result = results[0][above:]
+    for value in back:
+        result = result + value[above:]
+    result = result + from_host(results[inner - 1], inner - 1)
+    leaf_sums = [sums] + [over_leaf(sums[nrhs:], m) for m in range(leaves - 1, 0, -1)]
     answer, residual = call(
         functools.partial(finish_kernel, leaves),
         [((nrhs, rows), F32)] * 2,

time: 39 us -> 38.9 us (level)
  waiting for transfers between devices: 17.2 us -> 16.4 us
  starting transfers between devices: 16.8 us -> 17.4 us
    ppermute x3 -> x4, waiting for transfers between devices: 9.15 us -> 8.47 us  [from_host(): return lax.ppermute(value, axes, [(b, a) for a, b in routes[slot - 1]])]
    ppermute x3 -> x4, starting transfers between devices: 2.63 us -> 3.29 us  [from_host(): return lax.ppermute(value, axes, [(b, a) for a, b in routes[slot - 1]])]
  transfers between devices with their start and end apart: 14 -> 15, of which waited for: 5 -> 5; matrix products, arithmetic and copies ran while one was open for 0% -> 0% of each run, Pallas kernels for 0% -> 0%
where the time goes in v7:
time: 38.9 us; the launch traced here: 38.5 us
  starting transfers between devices  17.4 us (45%)
  waiting for transfers between devices  16.4 us (42%)
  local copies, waits for them, and re-layouts  2.7 us (7%)
  Pallas kernels  1.1 us (3%)
  between operations  0.87 us (2%)
    ppermute x6, starting transfers between devices, to_host(): return [value] + [lax.ppermute(value, axes, route) for route in routes]  10.1 us
    ppermute x4, waiting for transfers between devices, from_host(): return lax.ppermute(value, axes, [(b, a) for a, b in routes[slot - 1]])  8.47 us
    ppermute x6, waiting for transfers between devices, to_host(): return [value] + [lax.ppermute(value, axes, route) for route in routes]  4.35 us
    ppermute x5, starting transfers between devices, over_leaf(): return lax.ppermute(value, 'leaf', [(i, i ^ m) for i in range(leaves)])  3.99 us
    ppermute x5, waiting for transfers between devices, over_leaf(): return lax.ppermute(value, 'leaf', [(i, i ^ m) for i in range(leaves)])  3.57 us
    ppermute x4, starting transfers between devices, from_host(): return lax.ppermute(value, axes, [(b, a) for a, b in routes[slot - 1]])  3.29 us
    unnamed x10, local copies, waits for them, and re-layouts  2.69 us
    pallas_call x6, Pallas kernels, call(): pl.pallas_call(kernel, out_shape=[jax.ShapeDtypeStruct(shape, dtype) for...  1.1 us
  transfers between devices with their start and end apart: 15, of which 5 were waited for; matrix products, arithmetic and copies ran while one was open for 0% of the time, Pallas kernels for 0%

profile of v7, /device:TPU:0, one launch (start us, length us, event | category | flops | bytes accessed | tf_op | source)
XLA Modules:
  0.0 38.5 jit_solution(14813686875282449904)
XLA Ops:
  0.6 0.0 copy-start
  0.6 1.0 %copy-done = bf16[3,384,128]{2,1,0:T(8,128)(2,1)S(1)} copy-done((bf16[3,384,128]{2,1,0:T(8,128)(2,1)S(1)}, bf16[3,384,128]{2,1,0:T(8,128)(2,1)}, u32[]{:S(2)}) %copy-start) | copy-done | bytes 294936
  1.6 0.8 %copy-done.2 = f32[384,32]{0,1:T(8,128)S(1)} copy-done((f32[384,32]{0,1:T(8,128)S(1)}, f32[384,32]{0,1:T(8,128)}, u32[]{:S(2)}) %copy-start.2) | copy-done | bytes 49176
  2.4 0.9 %copy-done.4 = bf16[384,256]{1,0:T(8,128)(2,1)S(1)} copy-done((bf16[384,256]{1,0:T(8,128)(2,1)S(1)}, bf16[384,256]{1,0:T(8,128)(2,1)}, u32[]{:S(2)}) %copy-start.4) | copy-done | bytes 196632
  3.3 0.2 shard_map.50
  3.5 0.5 %collective-permute-start.3 = (f32[64,128]{1,0:T(8,128)S(1)}, f32[64,128]{1,0:T(8,128)S(1)}, u32[]{:S(2)}, u32[]{:S(2)}) collective-permute-start(f32[64,128]{1,0:T(8,128)S(1)} %get-tuple-element.24), channel_id=1, source_target_pairs={{0,4},{4,0},{8,12},{12,8},{1,5},{5,1},{9,13},{13,9},{2,6},{6,2},{1... | collective-permute-start | bytes 98312 | tf_op jit(solution)/shard_map/ppermute | solution.py:419
  4.0 5.5 %collective-permute-start = (bf16[960,128]{1,0:T(8,128)(2,1)S(1)}, bf16[960,128]{1,0:T(8,128)(2,1)S(1)}, u32[]{:S(2)}, u32[]{:S(2)}) collective-permute-start(bf16[960,128]{1,0:T(8,128)(2,1)S(1)} %get-tuple-element.17.refs_0_), channel_id=1, source_target_pairs={{0,2},{4,5},{8,10},{12,13},{16,18},{20,21},{24,26},{28,29}} | collective-permute-start | bytes 737288 | tf_op jit(solution)/shard_map/ppermute | solution.py:416
  9.6 0.7 %collective-permute-start.1 = (bf16[960,128]{1,0:T(8,128)(2,1)S(1)}, bf16[960,128]{1,0:T(8,128)(2,1)S(1)}, u32[]{:S(2)}, u32[]{:S(2)}) collective-permute-start(bf16[960,128]{1,0:T(8,128)(2,1)S(1)} %get-tuple-element.17.refs_0_), channel_id=1, source_target_pairs={{1,2},{7,5},{9,10},{15,13},{17,18},{23,21},{25,26},{31,29}} | collective-permute-start | bytes 737288 | tf_op jit(solution)/shard_map/ppermute | solution.py:416
  10.2 0.0 collective-permute-done.3
  10.3 1.6 %collective-permute-start.4 = (f32[32,128]{1,0:T(8,128)S(1)}, f32[32,128]{1,0:T(8,128)S(1)}, u32[]{:S(2)}, u32[]{:S(2)}) collective-permute-start(f32[32,128]{1,0:T(8,128)S(1)} %slice.39), channel_id=1, source_target_pairs={{0,8},{4,12},{8,0},{12,4},{1,9},{5,13},{9,1},{13,5},{2,10},{6,14},... | collective-permute-start | bytes 49160 | tf_op jit(solution)/shard_map/ppermute | solution.py:419
  11.8 0.7 %collective-permute-start.2 = (bf16[960,128]{1,0:T(8,128)(2,1)S(1)}, bf16[960,128]{1,0:T(8,128)(2,1)S(1)}, u32[]{:S(2)}, u32[]{:S(2)}) collective-permute-start(bf16[960,128]{1,0:T(8,128)(2,1)S(1)} %get-tuple-element.17.refs_0_), channel_id=1, source_target_pairs={{3,2},{6,5},{11,10},{14,13},{19,18},{22,21},{27,26},{30,29}} | collective-permute-start | bytes 737288 | tf_op jit(solution)/shard_map/ppermute | solution.py:416
  12.5 1.6 %collective-permute-done.4 = f32[32,128]{1,0:T(8,128)S(1)} collective-permute-done((f32[32,128]{1,0:T(8,128)S(1)}, f32[32,128]{1,0:T(8,128)S(1)}, u32[]{:S(2)}, u32[]{:S(2)}) %collective-permute-start.4) | collective-permute-done | bytes 16416 | tf_op jit(solution)/shard_map/ppermute | solution.py:419
  14.1 1.9 %collective-permute-start.5 = (bf16[1344,128]{1,0:T(8,128)(2,1)S(1)}, bf16[1344,128]{1,0:T(8,128)(2,1)S(1)}, u32[]{:S(2)}, u32[]{:S(2)}) collective-permute-start(bf16[1344,128]{1,0:T(8,128)(2,1)S(1)} %shard_map.53.refs_4_), channel_id=1, source_target_pairs={{0,2},{4,5},{8,10},{12,13},{16,18},{20,21},{24,26},{28,29}} | collective-permute-start | bytes 1032200 | tf_op jit(solution)/shard_map/ppermute | solution.py:416
  16.0 0.7 %collective-permute-start.6 = (bf16[1344,128]{1,0:T(8,128)(2,1)S(1)}, bf16[1344,128]{1,0:T(8,128)(2,1)S(1)}, u32[]{:S(2)}, u32[]{:S(2)}) collective-permute-start(bf16[1344,128]{1,0:T(8,128)(2,1)S(1)} %shard_map.53.refs_4_), channel_id=1, source_target_pairs={{1,2},{7,5},{9,10},{15,13},{17,18},{23,21},{25,26},{31,29}} | collective-permute-start | bytes 1032200 | tf_op jit(solution)/shard_map/ppermute | solution.py:416
  16.7 0.0 collective-permute-done.refs_1_
  16.7 0.7 %collective-permute-start.7 = (bf16[1344,128]{1,0:T(8,128)(2,1)S(1)}, bf16[1344,128]{1,0:T(8,128)(2,1)S(1)}, u32[]{:S(2)}, u32[]{:S(2)}) collective-permute-start(bf16[1344,128]{1,0:T(8,128)(2,1)S(1)} %shard_map.53.refs_4_), channel_id=1, source_target_pairs={{3,2},{6,5},{11,10},{14,13},{19,18},{22,21},{27,26},{30,29}} | collective-permute-start | bytes 1032200 | tf_op jit(solution)/shard_map/ppermute | solution.py:416
  17.4 0.0 collective-permute-done.1.refs_2_
  17.4 0.0 collective-permute-done.2.refs_3_
  17.5 0.0 copy-start.1
  17.5 0.0 copy-start.3
  17.5 4.3 %collective-permute-done.5.refs_5_ = bf16[1344,128]{1,0:T(8,128)(2,1)S(1)} collective-permute-done((bf16[1344,128]{1,0:T(8,128)(2,1)S(1)}, bf16[1344,128]{1,0:T(8,128)(2,1)S(1)}, u32[]{:S(2)}, u32[]{:S(2)}) %collective-permute-start.5) | collective-permute-done | bytes 344096 | tf_op jit(solution)/shard_map/ppermute | solution.py:416
  21.9 1.3 %collective-permute-start.8 = (bf16[512,128]{1,0:T(8,128)(2,1)S(1)}, bf16[512,128]{1,0:T(8,128)(2,1)S(1)}, u32[]{:S(2)}, u32[]{:S(2)}) collective-permute-start(bf16[512,128]{1,0:T(8,128)(2,1)S(1)} %get-tuple-element.26), channel_id=1, source_target_pairs={{2,0},{5,4},{10,8},{13,12},{18,16},{21,20},{26,24},{29,28}} | collective-permute-start | bytes 393224 | tf_op jit(solution)/shard_map/ppermute | solution.py:476
  23.2 0.7 %collective-permute-start.9 = (bf16[512,128]{1,0:T(8,128)(2,1)S(1)}, bf16[512,128]{1,0:T(8,128)(2,1)S(1)}, u32[]{:S(2)}, u32[]{:S(2)}) collective-permute-start(bf16[512,128]{1,0:T(8,128)(2,1)S(1)} %get-tuple-element.27), channel_id=1, source_target_pairs={{2,1},{5,7},{10,9},{13,15},{18,17},{21,23},{26,25},{29,31}} | collective-permute-start | bytes 393224 | tf_op jit(solution)/shard_map/ppermute | solution.py:476
  23.8 0.7 %collective-permute-start.11 = (bf16[128,128]{1,0:T(8,128)(2,1)S(1)}, bf16[128,128]{1,0:T(8,128)(2,1)S(1)}, u32[]{:S(2)}, u32[]{:S(2)}) collective-permute-start(bf16[128,128]{1,0:T(8,128)(2,1)S(1)} %get-tuple-element.29), channel_id=1, source_target_pairs={{2,3},{5,6},{10,11},{13,14},{18,19},{21,22},{26,27},{29,30}} | collective-permute-start | bytes 98312 | tf_op jit(solution)/shard_map/ppermute | solution.py:476
  24.5 0.7 %collective-permute-start.10 = (bf16[384,128]{1,0:T(8,128)(2,1)S(1)}, bf16[384,128]{1,0:T(8,128)(2,1)S(1)}, u32[]{:S(2)}, u32[]{:S(2)}) collective-permute-start(bf16[384,128]{1,0:T(8,128)(2,1)S(1)} %get-tuple-element.28), channel_id=1, source_target_pairs={{2,3},{5,6},{10,11},{13,14},{18,19},{21,22},{26,27},{29,30}} | collective-permute-start | bytes 294920 | tf_op jit(solution)/shard_map/ppermute | solution.py:476
  25.2 8.5 %collective-permute-done.8 = bf16[512,128]{1,0:T(8,128)(2,1)S(1)} collective-permute-done((bf16[512,128]{1,0:T(8,128)(2,1)S(1)}, bf16[512,128]{1,0:T(8,128)(2,1)S(1)}, u32[]{:S(2)}, u32[]{:S(2)}) %collective-permute-start.8) | collective-permute-done | bytes 131104 | tf_op jit(solution)/shard_map/ppermute | solution.py:476
  33.7 0.1 collective-permute-start.12
  33.8 1.6 %collective-permute-start.13 = (bf16[96,128]{1,0:T(8,128)(2,1)S(1)}, bf16[96,128]{1,0:T(8,128)(2,1)S(1)}, u32[]{:S(2)}, u32[]{:S(2)}) collective-permute-start(bf16[96,128]{1,0:T(8,128)(2,1)S(1)} %slice.44), channel_id=1, source_target_pairs={{0,8},{4,12},{8,0},{12,4},{1,9},{5,13},{9,1},{13,5},{2,10},{6,14},... | collective-permute-start | bytes 73736 | tf_op jit(solution)/shard_map/ppermute | solution.py:419
  35.3 0.3 collective-permute-start.14
  35.7 1.6 %collective-permute-done.12.refs_1_ = bf16[96,128]{1,0:T(8,128)(2,1)S(1)} collective-permute-done((bf16[96,128]{1,0:T(8,128)(2,1)S(1)}, bf16[96,128]{1,0:T(8,128)(2,1)S(1)}, u32[]{:S(2)}, u32[]{:S(2)}) %collective-permute-start.12) | collective-permute-done | bytes 24608 | tf_op jit(solution)/shard_map/ppermute | solution.py:419
  37.2 0.4 %collective-permute-done.13.refs_2_ = bf16[96,128]{1,0:T(8,128)(2,1)S(1)} collective-permute-done((bf16[96,128]{1,0:T(8,128)(2,1)S(1)}, bf16[96,128]{1,0:T(8,128)(2,1)S(1)}, u32[]{:S(2)}, u32[]{:S(2)}) %collective-permute-start.13) | collective-permute-done | bytes 24608 | tf_op jit(solution)/shard_map/ppermute | solution.py:419
  37.7 0.9 %shard_map.55 = (f32[32,384]{1,0:T(8,128)}, f32[32,384]{1,0:T(8,128)}) custom-call(f32[32,384]{1,0:T(8,128)S(1)} %bitcast.5, bf16[3,384,128]{2,1,0:T(8,128)(2,1)S(1)} %copy-done.1, bf16[384,128]{1,0:T(8,128)(2,1)S(1)} %fusion.result_ref, bf16[128,128]{1,0:T(8,128)(2,1)S(1)} %fusion.1.refs_0_, bf16[96,128]{1,0:T(8,128)(2,1)S(1)} %collective-permute-done.12.refs_1_, ...), custom_call_target="tpu_custom_call" | custom-call | bytes 548864 | tf_op jit(solution)/shard_map/pallas_call | solution.py:378
  (20 shorter events, 0.1 us)
Async XLA Ops:
  0.6 1.0 %copy-start = (bf16[3,384,128]{2,1,0:T(8,128)(2,1)S(1)}, bf16[3,384,128]{2,1,0:T(8,128)(2,1)}, u32[]{:S(2)}) copy-start(bf16[3,384,128]{2,1,0:T(8,128)(2,1)} %factors_ref.3) | copy-start | bytes 884740
  1.6 0.8 %copy-start.2 = (f32[384,32]{0,1:T(8,128)S(1)}, f32[384,32]{0,1:T(8,128)}, u32[]{:S(2)}) copy-start(f32[384,32]{0,1:T(8,128)} %param.5) | copy-start | bytes 147460
  2.4 0.9 %copy-start.4 = (bf16[384,256]{1,0:T(8,128)(2,1)S(1)}, bf16[384,256]{1,0:T(8,128)(2,1)}, u32[]{:S(2)}) copy-start(bf16[384,256]{1,0:T(8,128)(2,1)} %embed_ref.1) | copy-start | bytes 589828
  3.5 6.7 %collective-permute-start.3 = (f32[64,128]{1,0:T(8,128)S(1)}, f32[64,128]{1,0:T(8,128)S(1)}, u32[]{:S(2)}, u32[]{:S(2)}) collective-permute-start(f32[64,128]{1,0:T(8,128)S(1)} %get-tuple-element.24), channel_id=1, source_target_pairs={{0,4},{4,0},{8,12},{12,8},{1,5},{5,1},{9,13},{13,9},{2,6},{6,2},{1... | collective-permute-start | bytes 98312 | tf_op jit(solution)/shard_map/ppermute | solution.py:419
  4.0 12.7 %collective-permute-start = (bf16[960,128]{1,0:T(8,128)(2,1)S(1)}, bf16[960,128]{1,0:T(8,128)(2,1)S(1)}, u32[]{:S(2)}, u32[]{:S(2)}) collective-permute-start(bf16[960,128]{1,0:T(8,128)(2,1)S(1)} %get-tuple-element.17.refs_0_), channel_id=1, source_target_pairs={{0,2},{4,5},{8,10},{12,13},{16,18},{20,21},{24,26},{28,29}} | collective-permute-start | bytes 737288 | tf_op jit(solution)/shard_map/ppermute | solution.py:416
  9.6 7.9 %collective-permute-start.1 = (bf16[960,128]{1,0:T(8,128)(2,1)S(1)}, bf16[960,128]{1,0:T(8,128)(2,1)S(1)}, u32[]{:S(2)}, u32[]{:S(2)}) collective-permute-start(bf16[960,128]{1,0:T(8,128)(2,1)S(1)} %get-tuple-element.17.refs_0_), channel_id=1, source_target_pairs={{1,2},{7,5},{9,10},{15,13},{17,18},{23,21},{25,26},{31,29}} | collective-permute-start | bytes 737288 | tf_op jit(solution)/shard_map/ppermute | solution.py:416
  10.3 3.8 %collective-permute-start.4 = (f32[32,128]{1,0:T(8,128)S(1)}, f32[32,128]{1,0:T(8,128)S(1)}, u32[]{:S(2)}, u32[]{:S(2)}) collective-permute-start(f32[32,128]{1,0:T(8,128)S(1)} %slice.39), channel_id=1, source_target_pairs={{0,8},{4,12},{8,0},{12,4},{1,9},{5,13},{9,1},{13,5},{2,10},{6,14},... | collective-permute-start | bytes 49160 | tf_op jit(solution)/shard_map/ppermute | solution.py:419
  11.8 5.6 %collective-permute-start.2 = (bf16[960,128]{1,0:T(8,128)(2,1)S(1)}, bf16[960,128]{1,0:T(8,128)(2,1)S(1)}, u32[]{:S(2)}, u32[]{:S(2)}) collective-permute-start(bf16[960,128]{1,0:T(8,128)(2,1)S(1)} %get-tuple-element.17.refs_0_), channel_id=1, source_target_pairs={{3,2},{6,5},{11,10},{14,13},{19,18},{22,21},{27,26},{30,29}} | collective-permute-start | bytes 737288 | tf_op jit(solution)/shard_map/ppermute | solution.py:416
  14.1 7.7 %collective-permute-start.5 = (bf16[1344,128]{1,0:T(8,128)(2,1)S(1)}, bf16[1344,128]{1,0:T(8,128)(2,1)S(1)}, u32[]{:S(2)}, u32[]{:S(2)}) collective-permute-start(bf16[1344,128]{1,0:T(8,128)(2,1)S(1)} %shard_map.53.refs_4_), channel_id=1, source_target_pairs={{0,2},{4,5},{8,10},{12,13},{16,18},{20,21},{24,26},{28,29}} | collective-permute-start | bytes 1032200 | tf_op jit(solution)/shard_map/ppermute | solution.py:416
  16.0 5.8 %collective-permute-start.6 = (bf16[1344,128]{1,0:T(8,128)(2,1)S(1)}, bf16[1344,128]{1,0:T(8,128)(2,1)S(1)}, u32[]{:S(2)}, u32[]{:S(2)}) collective-permute-start(bf16[1344,128]{1,0:T(8,128)(2,1)S(1)} %shard_map.53.refs_4_), channel_id=1, source_target_pairs={{1,2},{7,5},{9,10},{15,13},{17,18},{23,21},{25,26},{31,29}} | collective-permute-start | bytes 1032200 | tf_op jit(solution)/shard_map/ppermute | solution.py:416
  16.7 5.1 %collective-permute-start.7 = (bf16[1344,128]{1,0:T(8,128)(2,1)S(1)}, bf16[1344,128]{1,0:T(8,128)(2,1)S(1)}, u32[]{:S(2)}, u32[]{:S(2)}) collective-permute-start(bf16[1344,128]{1,0:T(8,128)(2,1)S(1)} %shard_map.53.refs_4_), channel_id=1, source_target_pairs={{3,2},{6,5},{11,10},{14,13},{19,18},{22,21},{27,26},{30,29}} | collective-permute-start | bytes 1032200 | tf_op jit(solution)/shard_map/ppermute | solution.py:416
  17.5 20.2 %copy-start.1 = (bf16[3,384,128]{2,1,0:T(8,128)(2,1)S(1)}, bf16[3,384,128]{2,1,0:T(8,128)(2,1)}, u32[]{:S(2)}) copy-start(bf16[3,384,128]{2,1,0:T(8,128)(2,1)} %factors_ref.3) | copy-start | bytes 884740
  17.5 20.2 %copy-start.3 = (f32[384,32]{0,1:T(8,128)S(1)}, f32[384,32]{0,1:T(8,128)}, u32[]{:S(2)}) copy-start(f32[384,32]{0,1:T(8,128)} %param.5) | copy-start | bytes 147460
  21.9 11.8 %collective-permute-start.8 = (bf16[512,128]{1,0:T(8,128)(2,1)S(1)}, bf16[512,128]{1,0:T(8,128)(2,1)S(1)}, u32[]{:S(2)}, u32[]{:S(2)}) collective-permute-start(bf16[512,128]{1,0:T(8,128)(2,1)S(1)} %get-tuple-element.26), channel_id=1, source_target_pairs={{2,0},{5,4},{10,8},{13,12},{18,16},{21,20},{26,24},{29,28}} | collective-permute-start | bytes 393224 | tf_op jit(solution)/shard_map/ppermute | solution.py:476
  23.2 10.5 %collective-permute-start.9 = (bf16[512,128]{1,0:T(8,128)(2,1)S(1)}, bf16[512,128]{1,0:T(8,128)(2,1)S(1)}, u32[]{:S(2)}, u32[]{:S(2)}) collective-permute-start(bf16[512,128]{1,0:T(8,128)(2,1)S(1)} %get-tuple-element.27), channel_id=1, source_target_pairs={{2,1},{5,7},{10,9},{13,15},{18,17},{21,23},{26,25},{29,31}} | collective-permute-start | bytes 393224 | tf_op jit(solution)/shard_map/ppermute | solution.py:476
  23.8 1.3 %collective-permute-start.11 = (bf16[128,128]{1,0:T(8,128)(2,1)S(1)}, bf16[128,128]{1,0:T(8,128)(2,1)S(1)}, u32[]{:S(2)}, u32[]{:S(2)}) collective-permute-start(bf16[128,128]{1,0:T(8,128)(2,1)S(1)} %get-tuple-element.29), channel_id=1, source_target_pairs={{2,3},{5,6},{10,11},{13,14},{18,19},{21,22},{26,27},{29,30}} | collective-permute-start | bytes 98312 | tf_op jit(solution)/shard_map/ppermute | solution.py:476
  24.5 11.1 %collective-permute-start.10 = (bf16[384,128]{1,0:T(8,128)(2,1)S(1)}, bf16[384,128]{1,0:T(8,128)(2,1)S(1)}, u32[]{:S(2)}, u32[]{:S(2)}) collective-permute-start(bf16[384,128]{1,0:T(8,128)(2,1)S(1)} %get-tuple-element.28), channel_id=1, source_target_pairs={{2,3},{5,6},{10,11},{13,14},{18,19},{21,22},{26,27},{29,30}} | collective-permute-start | bytes 294920 | tf_op jit(solution)/shard_map/ppermute | solution.py:476
  33.7 3.5 %collective-permute-start.12 = (bf16[96,128]{1,0:T(8,128)(2,1)S(1)}, bf16[96,128]{1,0:T(8,128)(2,1)S(1)}, u32[]{:S(2)}, u32[]{:S(2)}) collective-permute-start(bf16[96,128]{1,0:T(8,128)(2,1)S(1)} %slice.44), channel_id=1, source_target_pairs={{0,12},{4,8},{8,4},{12,0},{1,13},{5,9},{9,5},{13,1},{2,14},{6,10},... | collective-permute-start | bytes 73736 | tf_op jit(solution)/shard_map/ppermute | solution.py:419
  33.8 3.9 %collective-permute-start.13 = (bf16[96,128]{1,0:T(8,128)(2,1)S(1)}, bf16[96,128]{1,0:T(8,128)(2,1)S(1)}, u32[]{:S(2)}, u32[]{:S(2)}) collective-permute-start(bf16[96,128]{1,0:T(8,128)(2,1)S(1)} %slice.44), channel_id=1, source_target_pairs={{0,8},{4,12},{8,0},{12,4},{1,9},{5,13},{9,1},{13,5},{2,10},{6,14},... | collective-permute-start | bytes 73736 | tf_op jit(solution)/shard_map/ppermute | solution.py:419
  35.3 2.3 %collective-permute-start.14 = (bf16[96,128]{1,0:T(8,128)(2,1)S(1)}, bf16[96,128]{1,0:T(8,128)(2,1)S(1)}, u32[]{:S(2)}, u32[]{:S(2)}) collective-permute-start(bf16[96,128]{1,0:T(8,128)(2,1)S(1)} %slice.44), channel_id=1, source_target_pairs={{0,4},{4,0},{8,12},{12,8},{1,5},{5,1},{9,13},{13,9},{2,6},{6,2},{1... | collective-permute-start | bytes 73736 | tf_op jit(solution)/shard_map/ppermute | solution.py:419

commit v8 on v6

--- a/solution.py
+++ b/solution.py
@@ -340,7 +340,7 @@
     lane = lax.broadcasted_iota(jnp.int32, (nrhs, rank), 1)
     packed = sums[0][levels * nrhs :].astype(F32)
     for m in range(1, leaves):
-        packed = packed + sums[m][levels * nrhs :].astype(F32)
+        packed = packed + sums[m][(levels - 1) * nrhs :].astype(F32)
 
     def scalar(k):
         inside = (lane >= 3 * k) & (lane < 3 * k + 3)
@@ -350,8 +350,9 @@
     wu = wu + 0.5 * ww
     for level in range(levels):
         nodes = {}
-        for m in range(leaves):
-            value = sums[m][level * nrhs : (level + 1) * nrhs].astype(F32)
+        for m in range(leaves if level else 1):
+            at = level if m == 0 else level - 1
+            value = sums[m][at * nrhs : (at + 1) * nrhs].astype(F32)
             node = m >> level
             nodes[node] = nodes[node] + value if node in nodes else value
         second = second + mm_nt(nodes[0].astype(BF16), factors_ref[level])
@@ -469,7 +470,8 @@
         route = [(b, a) for a, b in routes[slot - 1]]
         result = result + lax.ppermute(results[slot], axes, route)
     sums = result[: (levels + 1) * nrhs]
-    leaf_sums = [sums] + [over_leaf(sums, m) for m in range(leaves - 1, 0, -1)]
+    above = sums[nrhs:]
+    leaf_sums = [sums] + [over_leaf(above, m) for m in range(leaves - 1, 0, -1)]
     answer, residual = call(
         functools.partial(finish_kernel, leaves),
         [((nrhs, rows), F32)] * 2,

time: 39 us -> 38.9 us (level)
  no operation moved by 1% of the time
where the time goes in v8:
time: 38.9 us; the launch traced here: 38.6 us
  waiting for transfers between devices  17.1 us (44%)
  starting transfers between devices  16.8 us (43%)
  local copies, waits for them, and re-layouts  2.7 us (7%)
  Pallas kernels  1.1 us (3%)
  between operations  0.85 us (2%)
    ppermute x6, starting transfers between devices, to_host(): return [value] + [lax.ppermute(value, axes, route) for route in routes]  10.1 us
    ppermute x3, waiting for transfers between devices, collected(): result = result + lax.ppermute(results[slot], axes, route)  9.15 us
    ppermute x6, waiting for transfers between devices, to_host(): return [value] + [lax.ppermute(value, axes, route) for route in routes]  4.35 us
    ppermute x5, starting transfers between devices, over_leaf(): return lax.ppermute(value, 'leaf', [(i, i ^ m) for i in range(leaves)])  3.99 us
    ppermute x5, waiting for transfers between devices, over_leaf(): return lax.ppermute(value, 'leaf', [(i, i ^ m) for i in range(leaves)])  3.6 us
    unnamed x10, local copies, waits for them, and re-layouts  2.69 us
    ppermute x3, starting transfers between devices, collected(): result = result + lax.ppermute(results[slot], axes, route)  2.63 us
    pallas_call x6, Pallas kernels, call(): pl.pallas_call(kernel, out_shape=[jax.ShapeDtypeStruct(shape, dtype) for...  1.1 us
  transfers between devices with their start and end apart: 14, of which 5 were waited for; matrix products, arithmetic and copies ran while one was open for 0% of the time, Pallas kernels for 0%

profile of v8, /device:TPU:0, one launch (start us, length us, event | category | flops | bytes accessed | tf_op | source)
XLA Modules:
  0.0 38.6 jit_solution(10229793110421805971)
XLA Ops:
  0.6 0.0 copy-start
  0.6 1.0 %copy-done = bf16[3,384,128]{2,1,0:T(8,128)(2,1)S(1)} copy-done((bf16[3,384,128]{2,1,0:T(8,128)(2,1)S(1)}, bf16[3,384,128]{2,1,0:T(8,128)(2,1)}, u32[]{:S(2)}) %copy-start) | copy-done | bytes 294936
  1.6 0.8 %copy-done.2 = f32[384,32]{0,1:T(8,128)S(1)} copy-done((f32[384,32]{0,1:T(8,128)S(1)}, f32[384,32]{0,1:T(8,128)}, u32[]{:S(2)}) %copy-start.2) | copy-done | bytes 49176
  2.4 0.9 %copy-done.4 = bf16[384,256]{1,0:T(8,128)(2,1)S(1)} copy-done((bf16[384,256]{1,0:T(8,128)(2,1)S(1)}, bf16[384,256]{1,0:T(8,128)(2,1)}, u32[]{:S(2)}) %copy-start.4) | copy-done | bytes 196632
  3.3 0.2 shard_map.50
  3.5 0.5 %collective-permute-start.3 = (f32[64,128]{1,0:T(8,128)S(1)}, f32[64,128]{1,0:T(8,128)S(1)}, u32[]{:S(2)}, u32[]{:S(2)}) collective-permute-start(f32[64,128]{1,0:T(8,128)S(1)} %get-tuple-element.23), channel_id=1, source_target_pairs={{0,4},{4,0},{8,12},{12,8},{1,5},{5,1},{9,13},{13,9},{2,6},{6,2},{1... | collective-permute-start | bytes 98312 | tf_op jit(solution)/shard_map/ppermute | solution.py:415
  4.0 5.5 %collective-permute-start = (bf16[960,128]{1,0:T(8,128)(2,1)S(1)}, bf16[960,128]{1,0:T(8,128)(2,1)S(1)}, u32[]{:S(2)}, u32[]{:S(2)}) collective-permute-start(bf16[960,128]{1,0:T(8,128)(2,1)S(1)} %get-tuple-element.16.refs_0_), channel_id=1, source_target_pairs={{0,2},{4,5},{8,10},{12,13},{16,18},{20,21},{24,26},{28,29}} | collective-permute-start | bytes 737288 | tf_op jit(solution)/shard_map/ppermute | solution.py:412
  9.6 0.7 %collective-permute-start.1 = (bf16[960,128]{1,0:T(8,128)(2,1)S(1)}, bf16[960,128]{1,0:T(8,128)(2,1)S(1)}, u32[]{:S(2)}, u32[]{:S(2)}) collective-permute-start(bf16[960,128]{1,0:T(8,128)(2,1)S(1)} %get-tuple-element.16.refs_0_), channel_id=1, source_target_pairs={{1,2},{7,5},{9,10},{15,13},{17,18},{23,21},{25,26},{31,29}} | collective-permute-start | bytes 737288 | tf_op jit(solution)/shard_map/ppermute | solution.py:412
  10.2 0.0 collective-permute-done.3
  10.3 1.6 %collective-permute-start.4 = (f32[32,128]{1,0:T(8,128)S(1)}, f32[32,128]{1,0:T(8,128)S(1)}, u32[]{:S(2)}, u32[]{:S(2)}) collective-permute-start(f32[32,128]{1,0:T(8,128)S(1)} %slice.18), channel_id=1, source_target_pairs={{0,8},{4,12},{8,0},{12,4},{1,9},{5,13},{9,1},{13,5},{2,10},{6,14},... | collective-permute-start | bytes 49160 | tf_op jit(solution)/shard_map/ppermute | solution.py:415
  11.8 0.7 %collective-permute-start.2 = (bf16[960,128]{1,0:T(8,128)(2,1)S(1)}, bf16[960,128]{1,0:T(8,128)(2,1)S(1)}, u32[]{:S(2)}, u32[]{:S(2)}) collective-permute-start(bf16[960,128]{1,0:T(8,128)(2,1)S(1)} %get-tuple-element.16.refs_0_), channel_id=1, source_target_pairs={{3,2},{6,5},{11,10},{14,13},{19,18},{22,21},{27,26},{30,29}} | collective-permute-start | bytes 737288 | tf_op jit(solution)/shard_map/ppermute | solution.py:412
  12.5 1.6 %collective-permute-done.4 = f32[32,128]{1,0:T(8,128)S(1)} collective-permute-done((f32[32,128]{1,0:T(8,128)S(1)}, f32[32,128]{1,0:T(8,128)S(1)}, u32[]{:S(2)}, u32[]{:S(2)}) %collective-permute-start.4) | collective-permute-done | bytes 16416 | tf_op jit(solution)/shard_map/ppermute | solution.py:415
  14.1 1.9 %collective-permute-start.5 = (bf16[1344,128]{1,0:T(8,128)(2,1)S(1)}, bf16[1344,128]{1,0:T(8,128)(2,1)S(1)}, u32[]{:S(2)}, u32[]{:S(2)}) collective-permute-start(bf16[1344,128]{1,0:T(8,128)(2,1)S(1)} %shard_map.53.refs_4_), channel_id=1, source_target_pairs={{0,2},{4,5},{8,10},{12,13},{16,18},{20,21},{24,26},{28,29}} | collective-permute-start | bytes 1032200 | tf_op jit(solution)/shard_map/ppermute | solution.py:412
  16.0 0.7 %collective-permute-start.6 = (bf16[1344,128]{1,0:T(8,128)(2,1)S(1)}, bf16[1344,128]{1,0:T(8,128)(2,1)S(1)}, u32[]{:S(2)}, u32[]{:S(2)}) collective-permute-start(bf16[1344,128]{1,0:T(8,128)(2,1)S(1)} %shard_map.53.refs_4_), channel_id=1, source_target_pairs={{1,2},{7,5},{9,10},{15,13},{17,18},{23,21},{25,26},{31,29}} | collective-permute-start | bytes 1032200 | tf_op jit(solution)/shard_map/ppermute | solution.py:412
  16.7 0.0 collective-permute-done.refs_1_
  16.7 0.7 %collective-permute-start.7 = (bf16[1344,128]{1,0:T(8,128)(2,1)S(1)}, bf16[1344,128]{1,0:T(8,128)(2,1)S(1)}, u32[]{:S(2)}, u32[]{:S(2)}) collective-permute-start(bf16[1344,128]{1,0:T(8,128)(2,1)S(1)} %shard_map.53.refs_4_), channel_id=1, source_target_pairs={{3,2},{6,5},{11,10},{14,13},{19,18},{22,21},{27,26},{30,29}} | collective-permute-start | bytes 1032200 | tf_op jit(solution)/shard_map/ppermute | solution.py:412
  17.4 0.0 collective-permute-done.1.refs_2_
  17.4 0.0 collective-permute-done.2.refs_3_
  17.5 0.0 copy-start.1
  17.5 0.0 copy-start.3
  17.5 4.3 %collective-permute-done.5.refs_5_ = bf16[1344,128]{1,0:T(8,128)(2,1)S(1)} collective-permute-done((bf16[1344,128]{1,0:T(8,128)(2,1)S(1)}, bf16[1344,128]{1,0:T(8,128)(2,1)S(1)}, u32[]{:S(2)}, u32[]{:S(2)}) %collective-permute-start.5) | collective-permute-done | bytes 344096 | tf_op jit(solution)/shard_map/ppermute | solution.py:412
  21.8 0.0 collective-permute-done.6.refs_6_
  21.9 1.3 %collective-permute-start.10 = (bf16[512,128]{1,0:T(8,128)(2,1)S(1)}, bf16[512,128]{1,0:T(8,128)(2,1)S(1)}, u32[]{:S(2)}, u32[]{:S(2)}) collective-permute-start(bf16[512,128]{1,0:T(8,128)(2,1)S(1)} %get-tuple-element.27), channel_id=1, source_target_pairs={{2,0},{5,4},{10,8},{13,12},{18,16},{21,20},{26,24},{29,28}} | collective-permute-start | bytes 393224 | tf_op jit(solution)/shard_map/ppermute | solution.py:471
  23.2 0.7 %collective-permute-start.8 = (bf16[512,128]{1,0:T(8,128)(2,1)S(1)}, bf16[512,128]{1,0:T(8,128)(2,1)S(1)}, u32[]{:S(2)}, u32[]{:S(2)}) collective-permute-start(bf16[512,128]{1,0:T(8,128)(2,1)S(1)} %get-tuple-element.25), channel_id=1, source_target_pairs={{2,1},{5,7},{10,9},{13,15},{18,17},{21,23},{26,25},{29,31}} | collective-permute-start | bytes 393224 | tf_op jit(solution)/shard_map/ppermute | solution.py:471
  23.8 0.7 %collective-permute-start.9 = (bf16[512,128]{1,0:T(8,128)(2,1)S(1)}, bf16[512,128]{1,0:T(8,128)(2,1)S(1)}, u32[]{:S(2)}, u32[]{:S(2)}) collective-permute-start(bf16[512,128]{1,0:T(8,128)(2,1)S(1)} %get-tuple-element.26), channel_id=1, source_target_pairs={{2,3},{5,6},{10,11},{13,14},{18,19},{21,22},{26,27},{29,30}} | collective-permute-start | bytes 393224 | tf_op jit(solution)/shard_map/ppermute | solution.py:471
  24.5 9.1 %collective-permute-done.10 = bf16[512,128]{1,0:T(8,128)(2,1)S(1)} collective-permute-done((bf16[512,128]{1,0:T(8,128)(2,1)S(1)}, bf16[512,128]{1,0:T(8,128)(2,1)S(1)}, u32[]{:S(2)}, u32[]{:S(2)}) %collective-permute-start.10) | collective-permute-done | bytes 131104 | tf_op jit(solution)/shard_map/ppermute | solution.py:471
  33.7 0.1 collective-permute-start.11
  33.8 1.6 %collective-permute-start.12 = (bf16[96,128]{1,0:T(8,128)(2,1)S(1)}, bf16[96,128]{1,0:T(8,128)(2,1)S(1)}, u32[]{:S(2)}, u32[]{:S(2)}) collective-permute-start(bf16[96,128]{1,0:T(8,128)(2,1)S(1)} %slice.20), channel_id=1, source_target_pairs={{0,8},{4,12},{8,0},{12,4},{1,9},{5,13},{9,1},{13,5},{2,10},{6,14},... | collective-permute-start | bytes 73736 | tf_op jit(solution)/shard_map/ppermute | solution.py:415
  35.4 0.3 collective-permute-start.13
  35.7 1.6 %collective-permute-done.11.refs_1_ = bf16[96,128]{1,0:T(8,128)(2,1)S(1)} collective-permute-done((bf16[96,128]{1,0:T(8,128)(2,1)S(1)}, bf16[96,128]{1,0:T(8,128)(2,1)S(1)}, u32[]{:S(2)}, u32[]{:S(2)}) %collective-permute-start.11) | collective-permute-done | bytes 24608 | tf_op jit(solution)/shard_map/ppermute | solution.py:415
  37.3 0.4 %collective-permute-done.12.refs_2_ = bf16[96,128]{1,0:T(8,128)(2,1)S(1)} collective-permute-done((bf16[96,128]{1,0:T(8,128)(2,1)S(1)}, bf16[96,128]{1,0:T(8,128)(2,1)S(1)}, u32[]{:S(2)}, u32[]{:S(2)}) %collective-permute-start.12) | collective-permute-done | bytes 24608 | tf_op jit(solution)/shard_map/ppermute | solution.py:415
  37.7 0.9 %shard_map.55 = (f32[32,384]{1,0:T(8,128)}, f32[32,384]{1,0:T(8,128)}) custom-call(f32[32,384]{1,0:T(8,128)S(1)} %bitcast.5, bf16[3,384,128]{2,1,0:T(8,128)(2,1)S(1)} %copy-done.1, bf16[512,128]{1,0:T(8,128)(2,1)S(1)} %add_add_fusion.result_ref, bf16[128,128]{1,0:T(8,128)(2,1)S(1)} %slice.19.refs_0_, bf16[96,128]{1,0:T(8,128)(2,1)S(1)} %collective-permute-done.11.refs_1_, ...), custom_call_target="tpu_custom_call" | custom-call | bytes 581632 | tf_op jit(solution)/shard_map/pallas_call | solution.py:374
  (18 shorter events, 0.1 us)
Async XLA Ops:
  0.6 1.0 %copy-start = (bf16[3,384,128]{2,1,0:T(8,128)(2,1)S(1)}, bf16[3,384,128]{2,1,0:T(8,128)(2,1)}, u32[]{:S(2)}) copy-start(bf16[3,384,128]{2,1,0:T(8,128)(2,1)} %factors_ref.3) | copy-start | bytes 884740
  1.6 0.8 %copy-start.2 = (f32[384,32]{0,1:T(8,128)S(1)}, f32[384,32]{0,1:T(8,128)}, u32[]{:S(2)}) copy-start(f32[384,32]{0,1:T(8,128)} %param.5) | copy-start | bytes 147460
  2.4 0.9 %copy-start.4 = (bf16[384,256]{1,0:T(8,128)(2,1)S(1)}, bf16[384,256]{1,0:T(8,128)(2,1)}, u32[]{:S(2)}) copy-start(bf16[384,256]{1,0:T(8,128)(2,1)} %embed_ref.1) | copy-start | bytes 589828
  3.5 6.7 %collective-permute-start.3 = (f32[64,128]{1,0:T(8,128)S(1)}, f32[64,128]{1,0:T(8,128)S(1)}, u32[]{:S(2)}, u32[]{:S(2)}) collective-permute-start(f32[64,128]{1,0:T(8,128)S(1)} %get-tuple-element.23), channel_id=1, source_target_pairs={{0,4},{4,0},{8,12},{12,8},{1,5},{5,1},{9,13},{13,9},{2,6},{6,2},{1... | collective-permute-start | bytes 98312 | tf_op jit(solution)/shard_map/ppermute | solution.py:415
  4.0 12.7 %collective-permute-start = (bf16[960,128]{1,0:T(8,128)(2,1)S(1)}, bf16[960,128]{1,0:T(8,128)(2,1)S(1)}, u32[]{:S(2)}, u32[]{:S(2)}) collective-permute-start(bf16[960,128]{1,0:T(8,128)(2,1)S(1)} %get-tuple-element.16.refs_0_), channel_id=1, source_target_pairs={{0,2},{4,5},{8,10},{12,13},{16,18},{20,21},{24,26},{28,29}} | collective-permute-start | bytes 737288 | tf_op jit(solution)/shard_map/ppermute | solution.py:412
  9.6 7.9 %collective-permute-start.1 = (bf16[960,128]{1,0:T(8,128)(2,1)S(1)}, bf16[960,128]{1,0:T(8,128)(2,1)S(1)}, u32[]{:S(2)}, u32[]{:S(2)}) collective-permute-start(bf16[960,128]{1,0:T(8,128)(2,1)S(1)} %get-tuple-element.16.refs_0_), channel_id=1, source_target_pairs={{1,2},{7,5},{9,10},{15,13},{17,18},{23,21},{25,26},{31,29}} | collective-permute-start | bytes 737288 | tf_op jit(solution)/shard_map/ppermute | solution.py:412
  10.3 3.8 %collective-permute-start.4 = (f32[32,128]{1,0:T(8,128)S(1)}, f32[32,128]{1,0:T(8,128)S(1)}, u32[]{:S(2)}, u32[]{:S(2)}) collective-permute-start(f32[32,128]{1,0:T(8,128)S(1)} %slice.18), channel_id=1, source_target_pairs={{0,8},{4,12},{8,0},{12,4},{1,9},{5,13},{9,1},{13,5},{2,10},{6,14},... | collective-permute-start | bytes 49160 | tf_op jit(solution)/shard_map/ppermute | solution.py:415
  11.8 5.6 %collective-permute-start.2 = (bf16[960,128]{1,0:T(8,128)(2,1)S(1)}, bf16[960,128]{1,0:T(8,128)(2,1)S(1)}, u32[]{:S(2)}, u32[]{:S(2)}) collective-permute-start(bf16[960,128]{1,0:T(8,128)(2,1)S(1)} %get-tuple-element.16.refs_0_), channel_id=1, source_target_pairs={{3,2},{6,5},{11,10},{14,13},{19,18},{22,21},{27,26},{30,29}} | collective-permute-start | bytes 737288 | tf_op jit(solution)/shard_map/ppermute | solution.py:412
  14.1 7.7 %collective-permute-start.5 = (bf16[1344,128]{1,0:T(8,128)(2,1)S(1)}, bf16[1344,128]{1,0:T(8,128)(2,1)S(1)}, u32[]{:S(2)}, u32[]{:S(2)}) collective-permute-start(bf16[1344,128]{1,0:T(8,128)(2,1)S(1)} %shard_map.53.refs_4_), channel_id=1, source_target_pairs={{0,2},{4,5},{8,10},{12,13},{16,18},{20,21},{24,26},{28,29}} | collective-permute-start | bytes 1032200 | tf_op jit(solution)/shard_map/ppermute | solution.py:412
  16.0 5.8 %collective-permute-start.6 = (bf16[1344,128]{1,0:T(8,128)(2,1)S(1)}, bf16[1344,128]{1,0:T(8,128)(2,1)S(1)}, u32[]{:S(2)}, u32[]{:S(2)}) collective-permute-start(bf16[1344,128]{1,0:T(8,128)(2,1)S(1)} %shard_map.53.refs_4_), channel_id=1, source_target_pairs={{1,2},{7,5},{9,10},{15,13},{17,18},{23,21},{25,26},{31,29}} | collective-permute-start | bytes 1032200 | tf_op jit(solution)/shard_map/ppermute | solution.py:412
  16.7 5.1 %collective-permute-start.7 = (bf16[1344,128]{1,0:T(8,128)(2,1)S(1)}, bf16[1344,128]{1,0:T(8,128)(2,1)S(1)}, u32[]{:S(2)}, u32[]{:S(2)}) collective-permute-start(bf16[1344,128]{1,0:T(8,128)(2,1)S(1)} %shard_map.53.refs_4_), channel_id=1, source_target_pairs={{3,2},{6,5},{11,10},{14,13},{19,18},{22,21},{27,26},{30,29}} | collective-permute-start | bytes 1032200 | tf_op jit(solution)/shard_map/ppermute | solution.py:412
  17.5 20.2 %copy-start.1 = (bf16[3,384,128]{2,1,0:T(8,128)(2,1)S(1)}, bf16[3,384,128]{2,1,0:T(8,128)(2,1)}, u32[]{:S(2)}) copy-start(bf16[3,384,128]{2,1,0:T(8,128)(2,1)} %factors_ref.3) | copy-start | bytes 884740
  17.5 20.2 %copy-start.3 = (f32[384,32]{0,1:T(8,128)S(1)}, f32[384,32]{0,1:T(8,128)}, u32[]{:S(2)}) copy-start(f32[384,32]{0,1:T(8,128)} %param.5) | copy-start | bytes 147460
  21.9 11.8 %collective-permute-start.10 = (bf16[512,128]{1,0:T(8,128)(2,1)S(1)}, bf16[512,128]{1,0:T(8,128)(2,1)S(1)}, u32[]{:S(2)}, u32[]{:S(2)}) collective-permute-start(bf16[512,128]{1,0:T(8,128)(2,1)S(1)} %get-tuple-element.27), channel_id=1, source_target_pairs={{2,0},{5,4},{10,8},{13,12},{18,16},{21,20},{26,24},{29,28}} | collective-permute-start | bytes 393224 | tf_op jit(solution)/shard_map/ppermute | solution.py:471
  23.2 10.5 %collective-permute-start.8 = (bf16[512,128]{1,0:T(8,128)(2,1)S(1)}, bf16[512,128]{1,0:T(8,128)(2,1)S(1)}, u32[]{:S(2)}, u32[]{:S(2)}) collective-permute-start(bf16[512,128]{1,0:T(8,128)(2,1)S(1)} %get-tuple-element.25), channel_id=1, source_target_pairs={{2,1},{5,7},{10,9},{13,15},{18,17},{21,23},{26,25},{29,31}} | collective-permute-start | bytes 393224 | tf_op jit(solution)/shard_map/ppermute | solution.py:471
  23.8 9.8 %collective-permute-start.9 = (bf16[512,128]{1,0:T(8,128)(2,1)S(1)}, bf16[512,128]{1,0:T(8,128)(2,1)S(1)}, u32[]{:S(2)}, u32[]{:S(2)}) collective-permute-start(bf16[512,128]{1,0:T(8,128)(2,1)S(1)} %get-tuple-element.26), channel_id=1, source_target_pairs={{2,3},{5,6},{10,11},{13,14},{18,19},{21,22},{26,27},{29,30}} | collective-permute-start | bytes 393224 | tf_op jit(solution)/shard_map/ppermute | solution.py:471
  33.7 3.5 %collective-permute-start.11 = (bf16[96,128]{1,0:T(8,128)(2,1)S(1)}, bf16[96,128]{1,0:T(8,128)(2,1)S(1)}, u32[]{:S(2)}, u32[]{:S(2)}) collective-permute-start(bf16[96,128]{1,0:T(8,128)(2,1)S(1)} %slice.20), channel_id=1, source_target_pairs={{0,12},{4,8},{8,4},{12,0},{1,13},{5,9},{9,5},{13,1},{2,14},{6,10},... | collective-permute-start | bytes 73736 | tf_op jit(solution)/shard_map/ppermute | solution.py:415
  33.8 3.9 %collective-permute-start.12 = (bf16[96,128]{1,0:T(8,128)(2,1)S(1)}, bf16[96,128]{1,0:T(8,128)(2,1)S(1)}, u32[]{:S(2)}, u32[]{:S(2)}) collective-permute-start(bf16[96,128]{1,0:T(8,128)(2,1)S(1)} %slice.20), channel_id=1, source_target_pairs={{0,8},{4,12},{8,0},{12,4},{1,9},{5,13},{9,1},{13,5},{2,10},{6,14},... | collective-permute-start | bytes 73736 | tf_op jit(solution)/shard_map/ppermute | solution.py:415
  35.4 2.3 %collective-permute-start.13 = (bf16[96,128]{1,0:T(8,128)(2,1)S(1)}, bf16[96,128]{1,0:T(8,128)(2,1)S(1)}, u32[]{:S(2)}, u32[]{:S(2)}) collective-permute-start(bf16[96,128]{1,0:T(8,128)(2,1)S(1)} %slice.20), channel_id=1, source_target_pairs={{0,4},{4,0},{8,12},{12,8},{1,5},{5,1},{9,13},{13,9},{2,6},{6,2},{1... | collective-permute-start | bytes 73736 | tf_op jit(solution)/shard_map/ppermute | solution.py:415
